TPU v7x, 256 devices: a whole 4x4x8 slice. The times are simulated.
256 devices in a mesh: dp: 8 (over z), expert: 32 (over x, y, core).
Axes of the slice: x: 4, y: 4, z: 8, core: 2. Of those that a mesh axis runs over, the one named last changes fastest.
Arguments:
- tokens: bfloat16 [4, 256, 2048], P(None, ('dp', 'expert')), may hold values from -6 to 6
- route_ids: int32 [4, 256, 10], P(None, ('dp', 'expert')), may hold values from 0 to 31, all different within a row
- route_weights: bfloat16 [4, 256, 10], P(None, ('dp', 'expert')), may hold values from 0.019897461 to 0.29882812
- active_mask: int32 [4, 256], P(None, 'dp'), may hold values 0 or 1
- migration: int32 [256], replicated, may hold values from 0 to 255, as said below
- state_in: float32 [256, 32, 128, 128], P('dp', 'expert'), may hold values from -6 to 6
- in_gain: float32 [2048], replicated, may hold values from 0.5 to 1.5
- query_key: bfloat16 [2048, 4096], P(None, 'expert'), may hold values from -0.125 to 0.125
- value_gate: bfloat16 [2048, 8192], P(None, 'expert'), may hold values from -0.125 to 0.125
- gates_proj: bfloat16 [2048, 64], P(None, 'expert'), may hold values from -0.125 to 0.125
- log_rate: float32 [32], P('expert'), may hold values from -3 to 1.5
- step_bias: float32 [32], P('expert'), may hold values from -3 to 1
- head_gain: float32 [128], replicated, may hold values from 0.5 to 1.5
- out_proj: bfloat16 [4096, 2048], P('expert'), may hold values from -0.09375 to 0.09375
- post_gain: float32 [2048], replicated, may hold values from 0.5 to 1.5
- expert_up: bfloat16 [32, 2048, 512], P('expert'), may hold values from -0.125 to 0.125
- expert_down: bfloat16 [32, 256, 2048], P('expert'), may hold values from -0.375 to 0.375
Outputs:
- layer_out: bfloat16 [4, 256, 2048], P(None, ('dp', 'expert'))
- state_out: float32 [256, 32, 128, 128], P('dp', 'expert')
Inputs may be any that keep to these rules, and one draw needn't show every extreme that they name: `migration`: a permutation; the rows are in groups of 32; a row either keeps its place or moves to another group, every group sends the same number of rows to the group o places further on (cyclically), at most 2 rows go from one group to another, and exactly 2 for some o. `route_ids`: each row names 10 different experts.
All inputs are finite; a program needn't handle non-finite values. No bound on the sum of `active_mask` on one device may be relied on, other than what follows from the above.
Results may differ from a plain program's by a relative error of at most 0.02.
Values may be sent and summed in bfloat16 or wider, within the bound.
No kernel may reach another device: no remote copies, remote signals or barrier semaphores. Data moves between devices by JAX's collectives and lax.ppermute only.
A program may use at most 64 MiB of HBM per device.

v0:
```python
import jax
import jax.numpy as jnp
from jax import lax
from jax.sharding import PartitionSpec as P

STEPS = 4
CAP = 2


def swapped(value, axis, bit):
    return lax.ppermute(value, axis, [(i, i ^ 1 << bit) for i in range(lax.axis_size(axis))])


def root_norm(values_in, gain_vec):
    values_f = values_in.astype(jnp.float32)
    scale = lax.rsqrt(jnp.mean(values_f * values_f, axis=-1, keepdims=True) + 1e-06)
    return values_f * scale * gain_vec


def unit_norm(vectors):
    return vectors * lax.rsqrt(jnp.sum(vectors * vectors, axis=-1, keepdims=True) + 1e-06)


def migrate_states(state_in, migration, group_index, groups):
    local_rows = state_in.shape[0]
    layout_plan = migration.reshape(groups, local_rows)
    anchor = layout_plan // local_rows
    offset = layout_plan % local_rows
    target_grid = jnp.arange(groups, dtype=jnp.int32)[:, None]
    outgoing = (anchor == group_index) & (target_grid != group_index)
    order_rank = jnp.cumsum(outgoing.astype(jnp.int32), axis=1) - 1
    slot_ids = jnp.arange(CAP, dtype=jnp.int32)
    picked = outgoing[:, None, :] & (order_rank[:, None, :] == slot_ids[None, :, None])
    source_row = jnp.sum(jnp.where(picked, offset[:, None, :], 0), axis=2)
    filled = jnp.any(picked, axis=2)
    parcel = jnp.where(filled[:, :, None, None, None], state_in[source_row], 0.0)
    received = lax.all_to_all(
        parcel.astype(jnp.bfloat16), "dp", split_axis=0, concat_axis=0, tiled=True
    ).astype(parcel.dtype)
    mine_plan = lax.dynamic_index_in_dim(layout_plan, group_index, 0, keepdims=False)
    mine_anchor = mine_plan // local_rows
    mine_offset = mine_plan % local_rows
    same_anchor = mine_anchor[:, None] == mine_anchor[None, :]
    slot_range = jnp.arange(local_rows, dtype=jnp.int32)
    earlier = slot_range[None, :] < slot_range[:, None]
    rank_slot = jnp.sum((same_anchor & earlier).astype(jnp.int32), axis=1)
    flat_recv = received.reshape((groups * CAP,) + state_in.shape[1:])
    remote_index = mine_anchor * CAP + jnp.minimum(rank_slot, CAP - 1)
    keep_here = (mine_anchor == group_index)[:, None, None, None]
    return jnp.where(keep_here, state_in[mine_offset], flat_recv[remote_index])


def pair_keys(qk_part, member):
    partner = swapped(qk_part, "expert", 0)
    is_even = member % 2 == 0
    first_half = jnp.where(is_even, qk_part, partner)
    second_half = jnp.where(is_even, partner, qk_part)
    return (first_half[:, None, :], second_half[:, None, :])


def run_experts(rows_in, comb_local, expert_up, expert_down):
    hidden_units = expert_down.shape[1]
    up_proj = jnp.dot(rows_in, expert_up[0], preferred_element_type=jnp.float32)
    activated = (jax.nn.silu(up_proj[:, :hidden_units]) * up_proj[:, hidden_units:]).astype(
        jnp.bfloat16
    )
    result = jnp.dot(activated, expert_down[0], preferred_element_type=jnp.float32)
    summed = comb_local[:, 0].astype(jnp.float32)[:, None] * result
    return summed.astype(jnp.bfloat16)


def body(
    tokens,
    route_ids,
    route_weights,
    active_mask,
    migration,
    state_in,
    in_gain,
    query_key,
    value_gate,
    gates_proj,
    log_rate,
    step_bias,
    head_gain,
    out_proj,
    post_gain,
    expert_up,
    expert_down,
):
    groups = lax.axis_size("dp")
    members = lax.axis_size("expert")
    group_index = lax.axis_index("dp")
    member = lax.axis_index("expert")
    local_rows = state_in.shape[0]
    heads_here = state_in.shape[1]
    head_dim = state_in.shape[2]
    own_rows = tokens.shape[1]
    experts_here = expert_up.shape[0]
    experts_total = experts_here * members
    states = migrate_states(state_in, migration, group_index, groups)
    qk_width = query_key.shape[1]
    vz_width = value_gate.shape[1]
    proj_cat = jnp.concatenate([query_key, value_gate, gates_proj], axis=1)
    rates = jnp.exp(log_rate)
    outputs = []
    for step_index in range(STEPS):
        own_tokens = tokens[step_index]
        normed = root_norm(own_tokens, in_gain).astype(jnp.bfloat16)
        projected = jnp.dot(
            lax.all_gather(normed, "expert", axis=0, tiled=True),
            proj_cat,
            preferred_element_type=jnp.float32,
        )
        qk_part = projected[:, :qk_width].astype(jnp.bfloat16)
        vz_part = projected[:, qk_width : qk_width + vz_width].astype(jnp.bfloat16)
        ab_part = projected[:, qk_width + vz_width :].reshape(local_rows, heads_here, 2)
        query_raw, key_raw = pair_keys(qk_part, member)
        repeat_by = heads_here // query_raw.shape[1]
        queries = unit_norm(
            jnp.repeat(query_raw.astype(jnp.float32), repeat_by, axis=1)
        ) * head_dim ** (-0.5)
        key_vecs = unit_norm(jnp.repeat(key_raw.astype(jnp.float32), repeat_by, axis=1))
        vz_heads = vz_part.reshape(local_rows, heads_here, 2, head_dim).astype(jnp.float32)
        values = vz_heads[:, :, 0]
        gate_z = vz_heads[:, :, 1]
        beta_gate = jax.nn.sigmoid(ab_part[:, :, 1])
        decays = jnp.exp(-rates * jax.nn.softplus(ab_part[:, :, 0] + step_bias))
        decayed = states * decays[:, :, None, None]
        recall = jnp.einsum("rhk,rhkv->rhv", key_vecs, decayed)
        updated = (
            decayed
            + beta_gate[:, :, None, None]
            * key_vecs[:, :, :, None]
            * (values - recall)[:, :, None, :]
        )
        live_rows = (active_mask[step_index] == 1)[:, None, None, None]
        states = jnp.where(live_rows, updated, states)
        readout = jnp.einsum("rhk,rhkv->rhv", queries, updated)
        heads = (
            (root_norm(readout, head_gain) * jax.nn.silu(gate_z))
            .astype(jnp.bfloat16)
            .reshape(local_rows, heads_here * head_dim)
        )
        attention = lax.psum_scatter(
            jnp.dot(heads, out_proj, preferred_element_type=jnp.float32).astype(jnp.bfloat16),
            "expert",
            scatter_dimension=0,
            tiled=True,
        ).astype(jnp.float32)
        mixed = (own_tokens.astype(jnp.float32) + attention).astype(jnp.bfloat16)
        moe_in = root_norm(mixed, post_gain).astype(jnp.bfloat16)
        choose = (
            route_ids[step_index][:, :, None]
            == jnp.arange(experts_total, dtype=jnp.int32)[None, None, :]
        )
        combine = jnp.sum(
            jnp.where(choose, route_weights[step_index].astype(jnp.float32)[:, :, None], 0.0),
            axis=1,
        ).astype(jnp.bfloat16)
        per_device = combine.reshape(own_rows, members, experts_here).transpose(1, 0, 2)
        routed = jnp.any(per_device != 0, axis=2)
        outgoing_rows = jnp.where(
            routed[:, :, None], moe_in[None, :, :], jnp.zeros((), jnp.bfloat16)
        )
        rows_got = lax.all_to_all(outgoing_rows, "expert", split_axis=0, concat_axis=0, tiled=True)
        comb_got = lax.all_to_all(per_device, "expert", split_axis=0, concat_axis=0, tiled=True)
        senders = rows_got.shape[0]
        items = rows_got.shape[1]
        flat_rows = rows_got.reshape(senders * items, rows_got.shape[2])
        flat_comb = comb_got.reshape(senders * items, comb_got.shape[2])
        served = run_experts(flat_rows, flat_comb, expert_up, expert_down)
        served = served.reshape(senders, items, served.shape[1])
        returned = lax.all_to_all(served, "expert", split_axis=0, concat_axis=0, tiled=True)
        expert_sum = jnp.sum(returned.astype(jnp.float32), axis=0)
        outputs.append((mixed.astype(jnp.float32) + expert_sum).astype(jnp.bfloat16))
    return (jnp.stack(outputs), states)


def solution(mesh):
    in_specs = (
        P(None, ("dp", "expert"), None),
        P(None, ("dp", "expert"), None),
        P(None, ("dp", "expert"), None),
        P(None, "dp"),
        P(),
        P("dp", "expert", None, None),
        P(),
        P(None, "expert"),
        P(None, "expert"),
        P(None, "expert"),
        P("expert"),
        P("expert"),
        P(),
        P("expert", None),
        P(),
        P("expert", None, None),
        P("expert", None, None),
    )
    out_specs = (P(None, ("dp", "expert"), None), P("dp", "expert", None, None))
    return jax.shard_map(body, mesh=mesh, in_specs=in_specs, out_specs=out_specs, check_vma=False)
```

profile of v0, /device:TPU:32, one launch (start us, length us, event | category | flops | bytes accessed | tf_op | source)
XLA Modules:
  0.0 447.1 jit_solution(9456516324792589047)
XLA Ops:
  9.7 7.3 %all-to-all-start.7 = ((bf16[32,1,1]{2,1,0:T(2,128)(2,1)}), bf16[32,1,1]{2,1,0:T(2,128)(2,1)S(1)}, u32[]{:S(2)}, u32[]{:S(2)}) async-start(bf16[32,1,1]{2,1,0:T(2,128)(2,1)} %copy.87), calls=%async_computation.7 | async-start | bytes 32768 | tf_op jit(solution)/shard_map/all_to_all | solution.py:167
  23.0 24.9 %all-gather.3 = bf16[65536]{0:T(1024)(128)(2,1)S(1)} all-gather(bf16[2048]{0:T(1024)(128)(2,1)S(1)} %get-tuple-element.68), channel_id=5, replica_groups=mesh['dp'=8,'expert'=32] {'expert'}, dimensions={0}, use_global_device_ids=true | all-gather | bytes 135168 | tf_op jit(solution)/shard_map/all_gather | solution.py:111
  52.8 23.9 %all-gather.1 = bf16[65536]{0:T(1024)(128)(2,1)S(1)} all-gather(bf16[2048]{0:T(1024)(128)(2,1)S(1)} %get-tuple-element.66), channel_id=3, replica_groups=mesh['dp'=8,'expert'=32] {'expert'}, dimensions={0}, use_global_device_ids=true | all-gather | bytes 135168 | tf_op jit(solution)/shard_map/all_gather | solution.py:111
  79.3 22.4 %all-gather = bf16[65536]{0:T(1024)(128)(2,1)S(1)} all-gather(bf16[2048]{0:T(1024)(128)(2,1)S(1)} %get-tuple-element.67), channel_id=2, replica_groups=mesh['dp'=8,'expert'=32] {'expert'}, dimensions={0}, use_global_device_ids=true | all-gather | bytes 135168 | tf_op jit(solution)/shard_map/all_gather | solution.py:111
  104.2 23.9 %all-gather.2 = bf16[65536]{0:T(1024)(128)(2,1)S(1)} all-gather(bf16[2048]{0:T(1024)(128)(2,1)S(1)} %get-tuple-element.65), channel_id=4, replica_groups=mesh['dp'=8,'expert'=32] {'expert'}, dimensions={0}, use_global_device_ids=true | all-gather | bytes 135168 | tf_op jit(solution)/shard_map/all_gather | solution.py:111
  142.1 4.3 all-to-all-start.10
  147.2 6.5 %all-to-all-done.10 = bf16[32,1,1]{2,1,0:T(2,128)(2,1)S(1)} async-done(((bf16[32,1,1]{2,1,0:T(2,128)(2,1)}), bf16[32,1,1]{2,1,0:T(2,128)(2,1)S(1)}, u32[]{:S(2)}, u32[]{:S(2)}) %all-to-all-start.10) | async-done | bytes 96 | tf_op jit(solution)/shard_map/all_to_all | solution.py:167
  158.5 6.4 %all-to-all-done.1 = bf16[32,1,1]{2,1,0:T(2,128)(2,1)S(1)} async-done(((bf16[32,1,1]{2,1,0:T(2,128)(2,1)}), bf16[32,1,1]{2,1,0:T(2,128)(2,1)S(1)}, u32[]{:S(2)}, u32[]{:S(2)}) %all-to-all-start.1) | async-done | bytes 96 | tf_op jit(solution)/shard_map/all_to_all | solution.py:167
  169.6 6.5 %all-to-all-done.4 = bf16[32,1,1]{2,1,0:T(2,128)(2,1)S(1)} async-done(((bf16[32,1,1]{2,1,0:T(2,128)(2,1)}), bf16[32,1,1]{2,1,0:T(2,128)(2,1)S(1)}, u32[]{:S(2)}, u32[]{:S(2)}) %all-to-all-start.4) | async-done | bytes 96 | tf_op jit(solution)/shard_map/all_to_all | solution.py:167
  176.0 8.8 %all-to-all-start = ((bf16[8,2,1,128,128]{4,3,1,2,0:T(8,128)(2,1)}), bf16[8,2,1,128,128]{4,3,1,2,0:T(8,128)(2,1)}, u32[]{:S(2)}, u32[]{:S(2)}) async-start(bf16[8,2,1,128,128]{4,3,1,2,0:T(8,128)(2,1)} %select_convert_fusion), calls=%async_computation | async-start | bytes 1048576 | tf_op jit(solution)/shard_map/all_to_all | solution.py:37
  186.4 14.6 %all-to-all-done = bf16[8,2,1,128,128]{4,3,1,2,0:T(8,128)(2,1)} async-done(((bf16[8,2,1,128,128]{4,3,1,2,0:T(8,128)(2,1)}), bf16[8,2,1,128,128]{4,3,1,2,0:T(8,128)(2,1)}, u32[]{:S(2)}, u32[]{:S(2)}) %all-to-all-start) | async-done | bytes 524320 | tf_op jit(solution)/shard_map/all_to_all | solution.py:37
  221.3 7.5 %add_select_fusion = f32[32,1,128,128]{3,2,1,0:T(8,128)} fusion(f32[32,128,128]{2,1,0:T(8,128)} %gather_fusion.2, f32[32,128,128]{2,1,0:T(8,128)} %gather_fusion, f32[32,128]{1,0:T(8,128)S(1)} %sub.44, f32[32,128]{1,0:T(8,128)S(1)} %get-tuple-element.30, f32[32]{0:T(128)S(1)} %fusion.150, f32[32,128]{1,0:T(8,128)S(1)} %sub.43, ...), kind=kLoop, calls=%fused_computation.29 | loop fusion | flops 8912896 | bytes 6423200 | tf_op jit(solution)/shard_map/jit(_where)/select_n | solution.py:138
  228.8 100.1 %all-reduce.7.cloned.1.call-done = (bf16[32,2048]{1,0:T(8,128)(2,1)}, bf16[32,2048]{1,0:T(8,128)(2,1)}, bf16[32,2048]{1,0:T(8,128)(2,1)}, bf16[32,2048]{1,0:T(8,128)(2,1)}) async-done(((bf16[32,2048]{1,0:T(8,128)(2,1)}, bf16[32,2048]{1,0:T(8,128)(2,1)}, bf16[32,2048]{1,0:T(8,128)(2,1)}, bf16[32,2048]{1,0:T(8,128)(2,1)}), (bf16[32,2048]{1,0:T(8,128)(2,1)}, bf16[32,2048]{1,0:T(8,128)(2,1)}, ...) | async-done | bytes 524304
  336.6 5.2 %all-to-all-start.2 = ((bf16[32,2,1024]{2,1,0:T(2,128)(2,1)}), bf16[32,2,1024]{2,1,0:T(2,128)(2,1)S(1)}, u32[]{:S(2)}, u32[]{:S(2)}) async-start(bf16[32,2,1024]{2,1,0:T(2,128)(2,1)} %reshape.2064), calls=%async_computation.2 | async-start | bytes 262144 | tf_op jit(solution)/shard_map/all_to_all | solution.py:166
  351.9 7.5 %all-to-all-start.11 = ((bf16[32,2,1024]{2,1,0:T(2,128)(2,1)}), bf16[32,2,1024]{2,1,0:T(2,128)(2,1)}, u32[]{:S(2)}, u32[]{:S(2)}) async-start(bf16[32,2,1024]{2,1,0:T(2,128)(2,1)} %reshape.2052), calls=%async_computation.11 | async-start | bytes 262144 | tf_op jit(solution)/shard_map/all_to_all | solution.py:166
  363.1 4.2 all-to-all-done.11
  367.3 4.1 all-to-all-start.8
  379.2 4.6 %all-to-all-start.5 = ((bf16[32,2,1024]{2,1,0:T(2,128)(2,1)}), bf16[32,2,1024]{2,1,0:T(2,128)(2,1)}, u32[]{:S(2)}, u32[]{:S(2)}) async-start(bf16[32,2,1024]{2,1,0:T(2,128)(2,1)} %reshape.2060), calls=%async_computation.5 | async-start | bytes 262144 | tf_op jit(solution)/shard_map/all_to_all | solution.py:166
  387.6 4.1 all-to-all-done.5
  391.7 3.9 all-to-all-start.3
  403.4 4.5 %all-to-all-start.12 = ((bf16[32,2,1024]{2,1,0:T(2,128)(2,1)}), bf16[32,2,1024]{2,1,0:T(2,128)(2,1)S(1)}, u32[]{:S(2)}, u32[]{:S(2)}) async-start(bf16[32,2,1024]{2,1,0:T(2,128)(2,1)} %reshape.2054), calls=%async_computation.12 | async-start | bytes 262144 | tf_op jit(solution)/shard_map/all_to_all | solution.py:174
  409.0 6.8 %all-to-all-done.12 = bf16[32,2,1024]{2,1,0:T(2,128)(2,1)S(1)} async-done(((bf16[32,2,1024]{2,1,0:T(2,128)(2,1)}), bf16[32,2,1024]{2,1,0:T(2,128)(2,1)S(1)}, u32[]{:S(2)}, u32[]{:S(2)}) %all-to-all-start.12) | async-done | bytes 131104 | tf_op jit(solution)/shard_map/all_to_all | solution.py:174
  420.0 7.5 %all-to-all-done.9 = bf16[32,2,1024]{2,1,0:T(2,128)(2,1)S(1)} async-done(((bf16[32,2,1024]{2,1,0:T(2,128)(2,1)}), bf16[32,2,1024]{2,1,0:T(2,128)(2,1)S(1)}, u32[]{:S(2)}, u32[]{:S(2)}) %all-to-all-start.9) | async-done | bytes 131104 | tf_op jit(solution)/shard_map/all_to_all | solution.py:174
  431.7 7.5 %all-to-all-done.6 = bf16[32,2,1024]{2,1,0:T(2,128)(2,1)S(1)} async-done(((bf16[32,2,1024]{2,1,0:T(2,128)(2,1)}), bf16[32,2,1024]{2,1,0:T(2,128)(2,1)S(1)}, u32[]{:S(2)}, u32[]{:S(2)}) %all-to-all-start.6) | async-done | bytes 131104 | tf_op jit(solution)/shard_map/all_to_all | solution.py:174
  (231 shorter events, 108.6 us)
Async XLA Ops:
  7.2 130.7 %copy-start = (f32[32,1,128,128]{3,2,1,0:T(8,128)S(1)}, f32[32,1,128,128]{3,2,1,0:T(8,128)}, u32[]{:S(2)}) copy-start(f32[32,1,128,128]{3,2,1,0:T(8,128)} %param.22) | copy-start | bytes 6291460
  9.7 132.4 %all-to-all-start.7 = ((bf16[32,1,1]{2,1,0:T(2,128)(2,1)}), bf16[32,1,1]{2,1,0:T(2,128)(2,1)S(1)}, u32[]{:S(2)}, u32[]{:S(2)}) async-start(bf16[32,1,1]{2,1,0:T(2,128)(2,1)} %copy.87), calls=%async_computation.7 | async-start | bytes 32768 | tf_op jit(solution)/shard_map/all_to_all | solution.py:167
  52.4 133.5 %collective-permute-start.3 = (bf16[32,128]{1,0:T(8,128)(2,1)S(1)}, bf16[32,128]{1,0:T(8,128)(2,1)S(1)}, u32[]{:S(2)}, u32[]{:S(2)}) collective-permute-start(bf16[32,128]{1,0:T(8,128)(2,1)S(1)} %slice.243), channel_id=1, source_target_pairs={{0,1},{1,0},{2,3},{3,2},{4,5},{5,4},{6,7},{7,6},{8,9},{9,8},{10,11... | collective-permute-start | bytes 24584 | tf_op jit(solution)/shard_map/ppermute | solution.py:11
  78.8 106.8 %collective-permute-start.1 = (bf16[32,128]{1,0:T(8,128)(2,1)S(1)}, bf16[32,128]{1,0:T(8,128)(2,1)S(1)}, u32[]{:S(2)}, u32[]{:S(2)}) collective-permute-start(bf16[32,128]{1,0:T(8,128)(2,1)S(1)} %slice.229), channel_id=1, source_target_pairs={{0,1},{1,0},{2,3},{3,2},{4,5},{5,4},{6,7},{7,6},{8,9},{9,8},{10,11... | collective-permute-start | bytes 24584 | tf_op jit(solution)/shard_map/ppermute | solution.py:11
  103.8 81.9 %collective-permute-start = (bf16[32,128]{1,0:T(8,128)(2,1)S(1)}, bf16[32,128]{1,0:T(8,128)(2,1)S(1)}, u32[]{:S(2)}, u32[]{:S(2)}) collective-permute-start(bf16[32,128]{1,0:T(8,128)(2,1)S(1)} %slice.222), channel_id=1, source_target_pairs={{0,1},{1,0},{2,3},{3,2},{4,5},{5,4},{6,7},{7,6},{8,9},{9,8},{10,11... | collective-permute-start | bytes 24584 | tf_op jit(solution)/shard_map/ppermute | solution.py:11
  130.2 55.6 %collective-permute-start.2 = (bf16[32,128]{1,0:T(8,128)(2,1)S(1)}, bf16[32,128]{1,0:T(8,128)(2,1)S(1)}, u32[]{:S(2)}, u32[]{:S(2)}) collective-permute-start(bf16[32,128]{1,0:T(8,128)(2,1)S(1)} %slice.236), channel_id=1, source_target_pairs={{0,1},{1,0},{2,3},{3,2},{4,5},{5,4},{6,7},{7,6},{8,9},{9,8},{10,11... | collective-permute-start | bytes 24584 | tf_op jit(solution)/shard_map/ppermute | solution.py:11
  142.1 11.6 %all-to-all-start.10 = ((bf16[32,1,1]{2,1,0:T(2,128)(2,1)}), bf16[32,1,1]{2,1,0:T(2,128)(2,1)S(1)}, u32[]{:S(2)}, u32[]{:S(2)}) async-start(bf16[32,1,1]{2,1,0:T(2,128)(2,1)} %copy.91), calls=%async_computation.10 | async-start | bytes 32768 | tf_op jit(solution)/shard_map/all_to_all | solution.py:167
  153.7 11.2 %all-to-all-start.1 = ((bf16[32,1,1]{2,1,0:T(2,128)(2,1)}), bf16[32,1,1]{2,1,0:T(2,128)(2,1)S(1)}, u32[]{:S(2)}, u32[]{:S(2)}) async-start(bf16[32,1,1]{2,1,0:T(2,128)(2,1)} %copy.79), calls=%async_computation.1 | async-start | bytes 32768 | tf_op jit(solution)/shard_map/all_to_all | solution.py:167
  164.9 11.1 %all-to-all-start.4 = ((bf16[32,1,1]{2,1,0:T(2,128)(2,1)}), bf16[32,1,1]{2,1,0:T(2,128)(2,1)S(1)}, u32[]{:S(2)}, u32[]{:S(2)}) async-start(bf16[32,1,1]{2,1,0:T(2,128)(2,1)} %copy.83), calls=%async_computation.4 | async-start | bytes 32768 | tf_op jit(solution)/shard_map/all_to_all | solution.py:167
  176.0 24.9 %all-to-all-start = ((bf16[8,2,1,128,128]{4,3,1,2,0:T(8,128)(2,1)}), bf16[8,2,1,128,128]{4,3,1,2,0:T(8,128)(2,1)}, u32[]{:S(2)}, u32[]{:S(2)}) async-start(bf16[8,2,1,128,128]{4,3,1,2,0:T(8,128)(2,1)} %select_convert_fusion), calls=%async_computation | async-start | bytes 1048576 | tf_op jit(solution)/shard_map/all_to_all | solution.py:37
  184.8 144.1 %all-reduce.7.cloned.1.call-start = ((), (), s32[]{:S(2)}) async-start(), calls=%async_computation.13 | async-start | bytes 1048576
  221.2 107.7 %copy-start.4 = (bf16[4,1,2048]{2,0,1:T(4,128)(2,1)S(1)}, bf16[4,1,2048]{2,0,1:T(4,128)(2,1)}, u32[]{:S(2)}) copy-start(bf16[4,1,2048]{2,0,1:T(4,128)(2,1)} %param.17) | copy-start | bytes 49156
  221.2 112.5 %copy-start.8 = (f32[2048]{0:T(1024)S(1)}, f32[2048]{0:T(1024)}, u32[]{:S(2)}) copy-start(f32[2048]{0:T(1024)} %param.31) | copy-start | bytes 24580
  221.2 120.6 %copy-start.17 = (pred[32]{0:T(512)(128)(4,1)S(1)}, pred[32]{0:T(512)(128)(4,1)}, u32[]{:S(2)}) copy-start(pred[32]{0:T(512)(128)(4,1)} %convert_compare_fusion) | copy-start | bytes 100
  221.2 120.9 %copy-start.16 = (pred[32]{0:T(512)(128)(4,1)S(1)}, pred[32]{0:T(512)(128)(4,1)}, u32[]{:S(2)}) copy-start(pred[32]{0:T(512)(128)(4,1)} %convert_compare_fusion.1) | copy-start | bytes 100
  221.2 121.1 %copy-start.18 = (pred[32]{0:T(512)(128)(4,1)S(1)}, pred[32]{0:T(512)(128)(4,1)}, u32[]{:S(2)}) copy-start(pred[32]{0:T(512)(128)(4,1)} %convert_compare_fusion.2) | copy-start | bytes 100
  336.6 15.3 %all-to-all-start.2 = ((bf16[32,2,1024]{2,1,0:T(2,128)(2,1)}), bf16[32,2,1024]{2,1,0:T(2,128)(2,1)S(1)}, u32[]{:S(2)}, u32[]{:S(2)}) async-start(bf16[32,2,1024]{2,1,0:T(2,128)(2,1)} %reshape.2064), calls=%async_computation.2 | async-start | bytes 262144 | tf_op jit(solution)/shard_map/all_to_all | solution.py:166
  351.9 15.4 %all-to-all-start.11 = ((bf16[32,2,1024]{2,1,0:T(2,128)(2,1)}), bf16[32,2,1024]{2,1,0:T(2,128)(2,1)}, u32[]{:S(2)}, u32[]{:S(2)}) async-start(bf16[32,2,1024]{2,1,0:T(2,128)(2,1)} %reshape.2052), calls=%async_computation.11 | async-start | bytes 262144 | tf_op jit(solution)/shard_map/all_to_all | solution.py:166
  367.3 11.9 %all-to-all-start.8 = ((bf16[32,2,1024]{2,1,0:T(2,128)(2,1)}), bf16[32,2,1024]{2,1,0:T(2,128)(2,1)S(1)}, u32[]{:S(2)}, u32[]{:S(2)}) async-start(bf16[32,2,1024]{2,1,0:T(2,128)(2,1)} %reshape.2056), calls=%async_computation.8 | async-start | bytes 262144 | tf_op jit(solution)/shard_map/all_to_all | solution.py:166
  379.2 12.5 %all-to-all-start.5 = ((bf16[32,2,1024]{2,1,0:T(2,128)(2,1)}), bf16[32,2,1024]{2,1,0:T(2,128)(2,1)}, u32[]{:S(2)}, u32[]{:S(2)}) async-start(bf16[32,2,1024]{2,1,0:T(2,128)(2,1)} %reshape.2060), calls=%async_computation.5 | async-start | bytes 262144 | tf_op jit(solution)/shard_map/all_to_all | solution.py:166
  391.7 11.7 %all-to-all-start.3 = ((bf16[32,2,1024]{2,1,0:T(2,128)(2,1)}), bf16[32,2,1024]{2,1,0:T(2,128)(2,1)S(1)}, u32[]{:S(2)}, u32[]{:S(2)}) async-start(bf16[32,2,1024]{2,1,0:T(2,128)(2,1)} %reshape.2066), calls=%async_computation.3 | async-start | bytes 262144 | tf_op jit(solution)/shard_map/all_to_all | solution.py:174
  403.4 12.4 %all-to-all-start.12 = ((bf16[32,2,1024]{2,1,0:T(2,128)(2,1)}), bf16[32,2,1024]{2,1,0:T(2,128)(2,1)S(1)}, u32[]{:S(2)}, u32[]{:S(2)}) async-start(bf16[32,2,1024]{2,1,0:T(2,128)(2,1)} %reshape.2054), calls=%async_computation.12 | async-start | bytes 262144 | tf_op jit(solution)/shard_map/all_to_all | solution.py:174
  415.8 11.7 %all-to-all-start.9 = ((bf16[32,2,1024]{2,1,0:T(2,128)(2,1)}), bf16[32,2,1024]{2,1,0:T(2,128)(2,1)S(1)}, u32[]{:S(2)}, u32[]{:S(2)}) async-start(bf16[32,2,1024]{2,1,0:T(2,128)(2,1)} %reshape.2058), calls=%async_computation.9 | async-start | bytes 262144 | tf_op jit(solution)/shard_map/all_to_all | solution.py:174
  427.5 11.7 %all-to-all-start.6 = ((bf16[32,2,1024]{2,1,0:T(2,128)(2,1)}), bf16[32,2,1024]{2,1,0:T(2,128)(2,1)S(1)}, u32[]{:S(2)}, u32[]{:S(2)}) async-start(bf16[32,2,1024]{2,1,0:T(2,128)(2,1)} %reshape.2062), calls=%async_computation.6 | async-start | bytes 262144 | tf_op jit(solution)/shard_map/all_to_all | solution.py:174
  (14 other events, 119.9 us)
Sparse Core Ops, SparseCore 0:
  221.3 107.5 all-reduce.6
where the time goes:
time: 451 us; the launch traced here: 447 us
  waiting for transfers between devices  170 us (38%)
  blocking collectives  95 us (21%)
  starting transfers between devices  67.2 us (15%)
  other arithmetic  42.3 us (9%)
  matrix products  27.9 us (6%)
  local copies, waits for them, and re-layouts  23.1 us (5%)
  between operations  21.6 us (5%)
    unnamed x2, waiting for transfers between devices  100 us
    all_gather x4, blocking collectives, body(): lax.all_gather(normed, 'expert', axis=0, tiled=True)  95 us
    all_to_all x4, waiting for transfers between devices, body(): lax.all_to_all(served, 'expert', split_axis=0, concat_axis=0, tiled=True)  24.6 us
    all_to_all x4, starting transfers between devices, body(): lax.all_to_all(outgoing_rows, 'expert', split_axis=0, concat_axis=0, tile...  21.4 us
    all_to_all x4, waiting for transfers between devices, body(): lax.all_to_all(per_device, 'expert', split_axis=0, concat_axis=0, tiled=T...  19.4 us
    all_to_all x4, starting transfers between devices, body(): lax.all_to_all(per_device, 'expert', split_axis=0, concat_axis=0, tiled=T...  19.2 us
    all_to_all x4, starting transfers between devices, body(): lax.all_to_all(served, 'expert', split_axis=0, concat_axis=0, tiled=True)  16.1 us
    all_to_all x1, waiting for transfers between devices, migrate_states(): lax.all_to_all(parcel.astype(jnp.bfloat16), 'dp', split_axis=0, concat_ax...  14.6 us
  transfers between devices with their start and end apart: 18, of which 12 were waited for; matrix products, arithmetic and copies ran while one was open for 14% of the time, Pallas kernels for 0%

commit v1 on v0

v1 whole, which is shorter than its diff:
```python
import functools

import jax
import jax.numpy as jnp
from jax import lax
from jax.experimental import pallas as pl
from jax.experimental.pallas import tpu as pltpu
from jax.sharding import PartitionSpec as P

F32 = jnp.float32
BF16 = jnp.bfloat16
STEPS = 4
CAP = 2
EPS = 1e-06
EXTRA = 128
VMEM = pl.BlockSpec(memory_space=pltpu.VMEM)
SMEM = pl.BlockSpec(memory_space=pltpu.SMEM)


def core_swap(value):
    n = lax.axis_size("expert")
    return lax.ppermute(value, "expert", [(i, i ^ 1) for i in range(n)])


def exchange(chunks):
    n = lax.axis_size("expert")
    groups = [list(range(0, n, 2)), list(range(1, n, 2))]
    return lax.all_to_all(
        chunks, "expert", split_axis=0, concat_axis=0, tiled=True, axis_index_groups=groups
    )


def call(kernel, out_shape, in_specs, out_specs, scratch=(), limit=24, flops=0, moved=0):
    return pl.pallas_call(
        kernel,
        out_shape=out_shape,
        in_specs=in_specs,
        out_specs=out_specs,
        scratch_shapes=list(scratch),
        compiler_params=pltpu.CompilerParams(vmem_limit_bytes=limit * 1024 * 1024),
        cost_estimate=pl.CostEstimate(flops=flops, bytes_accessed=moved, transcendentals=0),
    )


def prep_kernel(place, tok, gain, ids, wts, mask, out):
    me = place[1]
    x = tok[...].astype(F32)
    scale = lax.rsqrt(jnp.mean(x * x, axis=-1, keepdims=True) + EPS)
    normed = (x * scale * gain[...]).astype(BF16)
    lane = lax.broadcasted_iota(jnp.int32, (STEPS, EXTRA), 1)
    ids_v = ids[...]
    wts_v = wts[...].astype(F32)
    comb = jnp.zeros((STEPS, EXTRA), F32)
    for k in range(ids_v.shape[1]):
        comb = comb + jnp.where(lane == ids_v[:, k : k + 1], wts_v[:, k : k + 1], 0.0)
    mask_v = mask[...].astype(F32)
    col = lax.broadcasted_iota(jnp.int32, mask_v.shape, 1)
    own_mask = jnp.sum(jnp.where(col == me, mask_v, 0.0), axis=-1, keepdims=True)
    comb = jnp.where(lane == EXTRA - 1, own_mask, comb).astype(BF16)
    width = x.shape[1]
    for j in range(out.shape[0]):
        out[j, :, :width] = normed
        out[j, :, width:] = comb


def parcel_kernel(place, mig, states, out):
    group = place[0]
    rows = states.shape[0]
    out[...] = jnp.zeros(out.shape, out.dtype)
    for g in range(out.shape[0]):

        def visit(i, count, g=g):
            old = mig[g * rows + i]
            take = (old // rows == group) & (group != g)

            @pl.when(take)
            def _():
                out[g, jnp.minimum(count, CAP - 1)] = states[old % rows].astype(BF16)

            return count + take.astype(jnp.int32)

        lax.fori_loop(0, rows, visit, jnp.int32(0), unroll=8)


def plan_rows(place, mig, slot_of, counts, rows, groups):
    group = place[0]
    for g in range(groups):
        counts[g] = 0
    for r in range(rows):
        src = mig[group * rows + r] // rows
        slot_of[r] = jnp.minimum(counts[src], CAP - 1)
        counts[src] = counts[src] + 1


def start_state(place, mig, slot_of, states, recv, s, rows):
    group = place[0]
    core = place[1] % 2
    half = rows // 2
    r = 2 * (s % half) + (s // half + core) % 2
    old = mig[group * rows + r]
    src = old // rows
    here = states[old % rows]
    sent = recv[src, slot_of[r]].astype(F32)
    return r, jnp.where(src == group, here, sent)


def heads_kernel(
    place, mig, rates, own_in, other_in, w_own, w_other, w_vz, w_ab, head_gain, w_out, states, recv,
    part_own, part_other, k_out, w_rows, decay_out,
    kq, ks, qs, q_all, v_all, z_all, d_all, b_all, m_all, h_all, slot_of, counts,
):
    rows = states.shape[0]
    dim = states.shape[1]
    total = rows * STEPS
    width = w_own.shape[0]
    plan_rows(place, mig, slot_of, counts, rows, recv.shape[0])
    x = jnp.concatenate([own_in[:, :width], other_in[:, :width]], axis=0)
    extra = jnp.concatenate([own_in[:, width:], other_in[:, width:]], axis=0).astype(F32)
    live = extra[:, EXTRA - 1 :]
    first = jnp.dot(x, w_own[...], preferred_element_type=F32)
    second = jnp.dot(x, w_other[...], preferred_element_type=F32)
    vz = jnp.dot(x, w_vz[...], preferred_element_type=F32)
    ab = jnp.dot(x, w_ab[...], preferred_element_type=F32)
    even = place[1] % 2 == 0
    q = jnp.where(even, first, second)
    k = jnp.where(even, second, first)
    q = q * (lax.rsqrt(jnp.sum(q * q, axis=-1, keepdims=True) + EPS) * dim**-0.5)
    k = k * lax.rsqrt(jnp.sum(k * k, axis=-1, keepdims=True) + EPS)
    beta = jax.nn.sigmoid(ab[:, 1:2])
    rate = jnp.exp(jnp.full((total, 1), rates[0], F32))
    drive = ab[:, 0:1] + rates[1]
    soft = jnp.maximum(drive, 0.0) + jnp.log1p(jnp.exp(-jnp.abs(drive)))
    decay = jnp.exp(-rate * soft)
    wide = (total, dim)
    q_all[...] = q
    k_out[...] = k
    v_all[...] = vz[:, :dim]
    z_all[...] = vz[:, dim:]
    d_all[...] = jnp.broadcast_to(decay, wide)
    b_all[...] = jnp.broadcast_to(beta, wide)
    m_all[...] = jnp.broadcast_to(live, wide)
    for s in range(rows):
        kq[8 * s : 8 * s + 4] = k[4 * s : 4 * s + 4]
        kq[8 * s + 4 : 8 * s + 8] = q[4 * s : 4 * s + 4]
    for s in range(rows):
        _, begin = start_state(place, mig, slot_of, states, recv, s, rows)
        both = jnp.dot(
            kq[8 * s : 8 * s + 8].astype(BF16), begin.astype(BF16), preferred_element_type=F32
        )
        ks[4 * s : 4 * s + 4] = both[:4]
        qs[4 * s : 4 * s + 4] = both[4:]

    def at(ref, t):
        return ref[pl.ds(t, rows, stride=STEPS), :]

    kept = jnp.ones((rows, dim), F32)
    past = []
    gain = head_gain[...]
    for t in range(STEPS):
        k_t, q_t, d_t, m_t = at(k_out, t), at(q_all, t), at(d_all, t), at(m_all, t)
        k_state = kept * at(ks, t)
        q_state = kept * at(qs, t)
        for k_s, w_s in past:
            k_state = k_state + jnp.sum(k_t * k_s, axis=-1, keepdims=True) * w_s
            q_state = q_state + jnp.sum(q_t * k_s, axis=-1, keepdims=True) * w_s
        write = at(b_all, t) * (at(v_all, t) - d_t * k_state)
        o = d_t * q_state + jnp.sum(q_t * k_t, axis=-1, keepdims=True) * write
        scale = lax.rsqrt(jnp.mean(o * o, axis=-1, keepdims=True) + EPS)
        z_t = at(z_all, t)
        h_all[pl.ds(t, rows, stride=STEPS), :] = o * scale * gain * (z_t * jax.nn.sigmoid(z_t))
        alive = m_t > 0.5
        a_t = jnp.where(alive, d_t, 1.0)
        kept = kept * a_t
        past = [(k_s, w_s * a_t) for k_s, w_s in past] + [(k_t, jnp.where(alive, write, 0.0))]
    for t in range(STEPS):
        w_rows[pl.ds(t, rows, stride=STEPS), :] = past[t][1]
    decay_out[...] = kept
    part = jnp.dot(h_all[...].astype(BF16), w_out[...], preferred_element_type=F32)
    half = total // 2
    part_own[...] = part[:half].astype(BF16)
    part_other[...] = part[half:].astype(BF16)


def state_kernel(place, mig, k_in, w_rows, decay, states, recv, out, slot_of, counts):
    rows = states.shape[0]
    plan_rows(place, mig, slot_of, counts, rows, recv.shape[0])
    for s in range(rows):
        r, begin = start_state(place, mig, slot_of, states, recv, s, rows)
        k_s = k_in[4 * s : 4 * s + 4, :]
        w_s = w_rows[4 * s : 4 * s + 4, :]
        outer = lax.dot_general(k_s, w_s, (((0,), (0,)), ((), ())), preferred_element_type=F32)
        out[r] = decay[s : s + 1, :] * begin + outer


def mixed_kernel(got, tok, gain, out, mixed_out):
    attention = jnp.sum(got[...].astype(F32), axis=0)
    mixed = (tok[...].astype(F32) + attention).astype(BF16)
    mixed_out[...] = mixed
    m = mixed.astype(F32)
    scale = lax.rsqrt(jnp.mean(m * m, axis=-1, keepdims=True) + EPS)
    normed = (m * scale * gain[...]).astype(BF16)
    for j in range(out.shape[0]):
        out[j] = normed


def expert_kernel(place, rows_in, extra, up_own, up_other, down_own, down_other, out):
    me = place[1]
    partner = me + 1 - 2 * (me % 2)
    x = rows_in[...]
    comb = extra[...].astype(F32)
    lane = lax.broadcasted_iota(jnp.int32, comb.shape, 1)
    total = None
    for index, up, down in ((me, up_own, down_own), (partner, up_other, down_other)):
        hidden = down.shape[0]
        proj = jnp.dot(x, up[...], preferred_element_type=F32)
        g, u = proj[:, :hidden], proj[:, hidden:]
        act = (g * jax.nn.sigmoid(g) * u).astype(BF16)
        weight = jnp.sum(jnp.where(lane == index, comb, 0.0), axis=-1, keepdims=True)
        result = weight * jnp.dot(act, down[...], preferred_element_type=F32)
        total = result if total is None else total + result
    out[...] = total.astype(BF16)


def sum_kernel(got, mixed, out):
    out[...] = (mixed[...].astype(F32) + jnp.sum(got[...].astype(F32), axis=0)).astype(BF16)


def body(
    tokens, route_ids, route_weights, active_mask, migration, state_in, in_gain, query_key,
    value_gate, gates_proj, log_rate, step_bias, head_gain, out_proj, post_gain, expert_up,
    expert_down,
):
    groups = lax.axis_size("dp")
    members = lax.axis_size("expert")
    rows = state_in.shape[0]
    dim = state_in.shape[2]
    width = tokens.shape[2]
    peers = members // 2
    half = rows * STEPS // 2
    place = jnp.stack([lax.axis_index("dp"), lax.axis_index("expert")]).astype(jnp.int32)
    sds = jax.ShapeDtypeStruct
    tok = tokens.reshape(STEPS, width)
    states = state_in.reshape(rows, dim, dim)

    w_other = core_swap(query_key)
    payload = call(
        prep_kernel, sds((peers, STEPS, width + EXTRA), BF16), [SMEM] + [VMEM] * 5, VMEM
    )(
        place, tok, in_gain.reshape(1, width), route_ids.reshape(STEPS, -1),
        route_weights.reshape(STEPS, -1), active_mask,
    )
    parcel = call(
        parcel_kernel, sds((groups, CAP, dim, dim), BF16), [SMEM, SMEM, VMEM], VMEM
    )(place, migration, states)
    recv = lax.all_to_all(parcel, "dp", split_axis=0, concat_axis=0, tiled=True)
    own_in = exchange(payload).reshape(half, width + EXTRA)
    other_in = core_swap(own_in)

    total = rows * STEPS
    rates = jnp.concatenate([log_rate, step_bias])
    tall = pltpu.VMEM((total, dim), F32)
    part_own, part_other, k_rows, w_rows, decay = call(
        heads_kernel,
        (
            sds((half, width), BF16), sds((half, width), BF16), sds((total, dim), F32),
            sds((total, dim), F32), sds((rows, dim), F32),
        ),
        [SMEM] * 3 + [VMEM] * 10,
        (VMEM,) * 5,
        scratch=[pltpu.VMEM((2 * total, dim), F32)] + [tall] * 9
        + [pltpu.SMEM((rows,), jnp.int32), pltpu.SMEM((groups,), jnp.int32)],
        flops=2 * total * width * 700,
        moved=6 << 20,
    )(
        place, migration, rates, own_in, other_in, query_key, w_other, value_gate, gates_proj,
        head_gain.reshape(1, dim), out_proj, states, recv,
    )
    swapped = core_swap(part_other)
    up_own = expert_up.reshape(width, -1)
    down_own = expert_down.reshape(-1, width)
    part = (part_own.astype(F32) + swapped.astype(F32)).astype(BF16)
    part, up_out, down_out = lax.optimization_barrier((part, up_own, down_own))
    up_other = core_swap(up_out)
    down_other = core_swap(down_out)
    got = exchange(part.reshape(peers, STEPS, width))

    state_out = call(
        state_kernel,
        sds((rows, dim, dim), F32),
        [SMEM] * 2 + [VMEM] * 5,
        VMEM,
        scratch=[pltpu.SMEM((rows,), jnp.int32), pltpu.SMEM((groups,), jnp.int32)],
        flops=2 * total * dim * dim,
        moved=5 << 20,
    )(place, migration, k_rows, w_rows, decay, states, recv)

    moe, mixed = call(
        mixed_kernel,
        (sds((peers, STEPS, width), BF16), sds((STEPS, width), BF16)),
        [VMEM] * 3,
        (VMEM, VMEM),
    )(got, tok, post_gain.reshape(1, width))
    moe_rows = exchange(moe).reshape(half, width)
    served = call(
        expert_kernel, sds((half, width), BF16), [SMEM] + [VMEM] * 6, VMEM, flops=1 << 29, moved=7 << 20
    )(place, moe_rows, own_in[:, width:], up_own, up_other, down_own, down_other)
    back = exchange(served.reshape(peers, STEPS, width))
    out = call(sum_kernel, sds((STEPS, width), BF16), [VMEM] * 2, VMEM)(back, mixed)
    return (out.reshape(STEPS, 1, width), state_out.reshape(state_in.shape))


def solution(mesh):
    in_specs = (
        P(None, ("dp", "expert"), None),
        P(None, ("dp", "expert"), None),
        P(None, ("dp", "expert"), None),
        P(None, "dp"),
        P(),
        P("dp", "expert", None, None),
        P(),
        P(None, "expert"),
        P(None, "expert"),
        P(None, "expert"),
        P("expert"),
        P("expert"),
        P(),
        P("expert", None),
        P(),
        P("expert", None, None),
        P("expert", None, None),
    )
    out_specs = (P(None, ("dp", "expert"), None), P("dp", "expert", None, None))
    return jax.shard_map(body, mesh=mesh, in_specs=in_specs, out_specs=out_specs, check_vma=False)
```

time: 451 us -> 106 us (0.24)
  waiting for transfers between devices: 170 us -> 28 us
  blocking collectives: 95 us -> 15.5 us
  starting transfers between devices: 67.2 us -> 24.2 us
  other arithmetic: 42.3 us -> 0.74 us
  matrix products: 27.9 us -> 0 us
  between operations: 21.6 us -> 2.12 us
  Pallas kernels: 0 us -> 18.4 us
  local copies, waits for them, and re-layouts: 23.1 us -> 15.3 us
    unnamed x2 -> x0, waiting for transfers between devices: 100 us -> none
    all_gather x4 -> x0, blocking collectives: 95 us -> none  [body(): lax.all_gather(normed, 'expert', axis=0, tiled=True)]
    all_to_all x13 -> x4, waiting for transfers between devices: 69.8 us -> 26.5 us  [the longest x3 14.3 us: exchange(): lax.all_to_all(chunks, 'expert', split_axis=0, concat_axis=0, tiled=True,...]
    all_to_all x13 -> x4, starting transfers between devices: 65.5 us -> 22.9 us  [the longest x3 14.3 us: exchange(): lax.all_to_all(chunks, 'expert', split_axis=0, concat_axis=0, tiled=True,...]
    dot_general x24 -> x0, matrix products: 27.9 us -> none  [the longest x4 7.94 us: run_experts(): up_proj = jnp.dot(rows_in, expert_up[0], preferred_element_type=jnp.float32)]
    select_n x14 -> x0, other arithmetic: 20.1 us -> none  [the longest x2 9.13 us: body(): states = jnp.where(live_rows, updated, states)]
    pallas_call x0 -> x7, Pallas kernels: none -> 18.4 us  [the longest x1 5.75 us: body(): call(parcel_kernel, sds((groups, CAP, dim, dim), BF16), [SMEM, SMEM, VMEM...]
    all_to_all x0 -> x1, blocking collectives: none -> 15.5 us  [exchange(): lax.all_to_all(chunks, 'expert', split_axis=0, concat_axis=0, tiled=True,...]
  transfers between devices with their start and end apart: 18 -> 9, of which waited for: 12 -> 5; matrix products, arithmetic and copies ran while one was open for 14% -> 2% of each run, Pallas kernels for 0% -> 9%
where the time goes in v1:
time: 106 us; the launch traced here: 104 us
  waiting for transfers between devices  28 us (26%)
  starting transfers between devices  24.2 us (23%)
  Pallas kernels  18.4 us (17%)
  blocking collectives  15.5 us (15%)
  local copies, waits for them, and re-layouts  15.3 us (14%)
  between operations  2.12 us (2%)
    all_to_all x1, blocking collectives, exchange(): lax.all_to_all(chunks, 'expert', split_axis=0, concat_axis=0, tiled=True,...  15.5 us
    all_to_all x3, starting transfers between devices, exchange(): lax.all_to_all(chunks, 'expert', split_axis=0, concat_axis=0, tiled=True,...  14.3 us
    all_to_all x3, waiting for transfers between devices, exchange(): lax.all_to_all(chunks, 'expert', split_axis=0, concat_axis=0, tiled=True,...  14.3 us
    unnamed x53, local copies, waits for them, and re-layouts  13.7 us
    all_to_all x1, waiting for transfers between devices, body(): recv = lax.all_to_all(parcel, 'dp', split_axis=0, concat_axis=0, tiled=True)  12.2 us
    all_to_all x1, starting transfers between devices, body(): recv = lax.all_to_all(parcel, 'dp', split_axis=0, concat_axis=0, tiled=True)  8.57 us
    pallas_call x1, Pallas kernels, body(): call(parcel_kernel, sds((groups, CAP, dim, dim), BF16), [SMEM, SMEM, VMEM...  5.75 us
    pallas_call x1, Pallas kernels, body(): call(expert_kernel, sds((half, width), BF16), [SMEM] + [VMEM] * 6, VMEM,...  4.17 us
  transfers between devices with their start and end apart: 9, of which 5 were waited for; matrix products, arithmetic and copies ran while one was open for 2% of the time, Pallas kernels for 9%

profile of v1, /device:TPU:32, one launch (start us, length us, event | category | flops | bytes accessed | tf_op | source)
XLA Modules:
  0.0 104.3 jit_solution(6173865606203119554)
XLA Ops:
  0.7 0.7 copy-done.5
  1.4 0.7 copy-done.18
  4.2 1.4 %shard_map.176 = bf16[16,4,2176]{2,1,0:T(4,128)(2,1)} custom-call(s32[2]{0:T(128)S(1)} %pad_add_fusion.place, bf16[4,2048]{1,0:T(4,128)(2,1)S(1)} %bitcast.18, f32[1,2048]{1,0:T(1,128)S(1)} %bitcast.20, s32[4,10]{1,0:T(4,128)S(1)} %bitcast.22, bf16[4,10]{1,0:T(4,128)(2,1)S(1)} %bitcast.23, s32[4,32]{1,0:T(4,128)S(1)} %copy-done.21), custom_call_target="tpu_custom_call" | custom-call | tf_op jit(solution)/shard_map/pallas_call | solution.py:246
  5.6 7.0 %all-to-all-start = ((bf16[16,4,2176]{2,1,0:T(4,128)(2,1)}), bf16[16,4,2176]{2,1,0:T(4,128)(2,1)S(1)}, u32[]{:S(2)}, u32[]{:S(2)}) async-start(bf16[16,4,2176]{2,1,0:T(4,128)(2,1)} %shard_map.176), calls=%async_computation | async-start | bytes 557056 | tf_op jit(solution)/shard_map/all_to_all | solution.py:28
  12.6 1.6 %copy-done = f32[32,1,128,128]{3,2,1,0:T(8,128)S(1)} copy-done((f32[32,1,128,128]{3,2,1,0:T(8,128)S(1)}, f32[32,1,128,128]{3,2,1,0:T(8,128)}, u32[]{:S(2)}) %copy-start) | copy-done | bytes 2097176
  14.9 5.7 %shard_map.177 = bf16[8,2,128,128]{3,2,1,0:T(8,128)(2,1)} custom-call(s32[2]{0:T(128)S(1)} %pad_add_fusion.place, s32[256]{0:T(256)S(1)} %copy-done.15, f32[32,128,128]{2,1,0:T(8,128)S(1)} %bitcast.15), custom_call_target="tpu_custom_call" | custom-call | tf_op jit(solution)/shard_map/pallas_call | solution.py:252
  21.3 8.6 %all-to-all-start.1 = ((bf16[8,2,128,128]{3,2,1,0:T(8,128)(2,1)}), bf16[8,2,128,128]{3,2,1,0:T(8,128)(2,1)S(1)}, u32[]{:S(2)}, u32[]{:S(2)}) async-start(bf16[8,2,128,128]{3,2,1,0:T(8,128)(2,1)} %shard_map.177), calls=%async_computation.1 | async-start | bytes 1048576 | tf_op jit(solution)/shard_map/all_to_all | solution.py:255
  32.7 12.2 %all-to-all-done.1.recv = bf16[8,2,128,128]{3,2,1,0:T(8,128)(2,1)S(1)} async-done(((bf16[8,2,128,128]{3,2,1,0:T(8,128)(2,1)}), bf16[8,2,128,128]{3,2,1,0:T(8,128)(2,1)S(1)}, u32[]{:S(2)}, u32[]{:S(2)}) %all-to-all-start.1) | async-done | bytes 524320 | tf_op jit(solution)/shard_map/all_to_all | solution.py:255
  45.0 1.2 %copy-done.2 = bf16[2048,256]{1,0:T(8,128)(2,1)S(1)} copy-done((bf16[2048,256]{1,0:T(8,128)(2,1)S(1)}, bf16[2048,256]{1,0:T(8,128)(2,1)}, u32[]{:S(2)}) %copy-start.2) | copy-done | bytes 1048600
  46.2 1.0 copy-done.3
  49.8 2.8 %shard_map.178 = (bf16[64,2048]{1,0:T(8,128)(2,1)S(1)}, bf16[64,2048]{1,0:T(8,128)(2,1)S(1)}, f32[128,128]{1,0:T(8,128)S(1)}, f32[128,128]{1,0:T(8,128)S(1)}, f32[32,128]{1,0:T(8,128)S(1)}) custom-call(s32[2]{0:T(128)S(1)} %copy-done.12, s32[256]{0:T(256)S(1)} %copy-done.16, f32[2]{0:T(128)S(1)} %copy-done.24, bf16[64,2176]{1,0:T(8,128)(2,1)S(1)} %reshape.53.own_in, ...), custom_call_target="tpu_custom_call" | custom-call | flops 367001600 | bytes 6291456 | tf_op jit(solution)/shard_map/pallas_call | solution.py:262
  52.7 1.5 %collective-permute-done.2 = bf16[64,2048]{1,0:T(8,128)(2,1)S(1)} collective-permute-done((bf16[64,2048]{1,0:T(8,128)(2,1)S(1)}, bf16[64,2048]{1,0:T(8,128)(2,1)S(1)}, u32[]{:S(2)}, u32[]{:S(2)}) %collective-permute-start.2) | collective-permute-done | bytes 262176 | tf_op jit(solution)/shard_map/ppermute | solution.py:22
  55.0 15.5 %all_to_all.25.got = bf16[16,4,2048]{2,1,0:T(4,128)(2,1)S(1)} all-to-all(bf16[16,4,2048]{2,1,0:T(4,128)(2,1)S(1)} %reshape.58), channel_id=1, replica_groups={{0,2,4,6,8,10,12,14,16,18,20,22,24,26,28,30},{1,3,5,7,9,11,13,15,17,19,..., dimensions={0} | all-to-all | bytes 524288 | tf_op jit(solution)/shard_map/all_to_all | solution.py:28
  70.6 0.7 copy-done.6
  72.0 1.0 shard_map.179
  72.9 3.6 %all-to-all-start.3 = ((bf16[16,4,2048]{2,1,0:T(4,128)(2,1)}), bf16[16,4,2048]{2,1,0:T(4,128)(2,1)S(1)}, u32[]{:S(2)}, u32[]{:S(2)}) async-start(bf16[16,4,2048]{2,1,0:T(4,128)(2,1)} %get-tuple-element.15), calls=%async_computation.3 | async-start | bytes 524288 | tf_op jit(solution)/shard_map/all_to_all | solution.py:28
  77.2 7.9 %all-to-all-done.3 = bf16[16,4,2048]{2,1,0:T(4,128)(2,1)S(1)} async-done(((bf16[16,4,2048]{2,1,0:T(4,128)(2,1)}), bf16[16,4,2048]{2,1,0:T(4,128)(2,1)S(1)}, u32[]{:S(2)}, u32[]{:S(2)}) %all-to-all-start.3) | async-done | bytes 262176 | tf_op jit(solution)/shard_map/all_to_all | solution.py:28
  85.2 0.7 copy-done.4
  86.5 4.2 %shard_map.180 = bf16[64,2048]{1,0:T(8,128)(2,1)S(1)} custom-call(s32[2]{0:T(128)S(1)} %copy-done.13, bf16[64,2048]{1,0:T(8,128)(2,1)S(1)} %reshape.60.rows_in, bf16[64,128]{1,0:T(8,128)(2,1)S(1)} %copy-done.4, bf16[2048,512]{1,0:T(8,128)(2,1)} %bitcast.8.up_own, bf16[2048,512]{1,0:T(8,128)(2,1)} %collective-permute-done.3.up_other, ...), custom_call_target="tpu_custom_call" | custom-call | flops 536870912 | bytes 7340032 | tf_op jit(solution)/shard_map/pallas_call | solution.py:304
  90.6 0.8 reshape.61
  91.5 3.7 %all-to-all-start.4 = ((bf16[16,4,2048]{2,1,0:T(4,128)(2,1)}), bf16[16,4,2048]{2,1,0:T(4,128)(2,1)S(1)}, u32[]{:S(2)}, u32[]{:S(2)}) async-start(bf16[16,4,2048]{2,1,0:T(4,128)(2,1)} %reshape.61), calls=%async_computation.4 | async-start | bytes 524288 | tf_op jit(solution)/shard_map/all_to_all | solution.py:28
  95.2 2.6 %shard_map.182 = f32[32,128,128]{2,1,0:T(8,128)} custom-call(s32[2]{0:T(128)S(1)} %copy-done.14, s32[256]{0:T(256)S(1)} %copy-done.17, f32[128,128]{1,0:T(8,128)S(1)} %get-tuple-element.19.k_in, f32[128,128]{1,0:T(8,128)S(1)} %get-tuple-element.20.w_rows, f32[32,128]{1,0:T(8,128)S(1)} %copy-done.8, f32[32,128,128]{2,1,0:T(8,128)S(1)} %bitcast.17, ...), custom_call_target="tpu_custom_call" | custom-call | flops 4194304 | bytes 5242880 | tf_op jit(solution)/shard_map/pallas_call | solution.py:287
  97.8 5.8 %all-to-all-done.4.got = bf16[16,4,2048]{2,1,0:T(4,128)(2,1)S(1)} async-done(((bf16[16,4,2048]{2,1,0:T(4,128)(2,1)}), bf16[16,4,2048]{2,1,0:T(4,128)(2,1)S(1)}, u32[]{:S(2)}, u32[]{:S(2)}) %all-to-all-start.4) | async-done | bytes 262176 | tf_op jit(solution)/shard_map/all_to_all | solution.py:28
  103.6 0.7 shard_map.181
  (63 shorter events, 10.5 us)
Async XLA Ops:
  0.7 20.6 %copy-start.11 = (s32[2]{0:T(128)}, s32[2]{0:T(128)S(1)}, u32[]{:S(2)}) copy-start(s32[2]{0:T(128)S(1)} %pad_add_fusion.place) | copy-start | bytes 28
  0.7 0.7 copy-start.5
  5.6 15.7 %all-to-all-start = ((bf16[16,4,2176]{2,1,0:T(4,128)(2,1)}), bf16[16,4,2176]{2,1,0:T(4,128)(2,1)S(1)}, u32[]{:S(2)}, u32[]{:S(2)}) async-start(bf16[16,4,2176]{2,1,0:T(4,128)(2,1)} %shard_map.176), calls=%async_computation | async-start | bytes 557056 | tf_op jit(solution)/shard_map/all_to_all | solution.py:28
  12.6 1.6 %copy-start = (f32[32,1,128,128]{3,2,1,0:T(8,128)S(1)}, f32[32,1,128,128]{3,2,1,0:T(8,128)}, u32[]{:S(2)}) copy-start(f32[32,1,128,128]{3,2,1,0:T(8,128)} %param.22) | copy-start | bytes 6291460
  14.9 16.9 %copy-start.25 = (bf16[2048,2]{0,1:T(2,128)(2,1)S(1)}, bf16[2048,2]{0,1:T(2,128)(2,1)}, u32[]{:S(2)}) copy-start(bf16[2048,2]{0,1:T(2,128)(2,1)} %param.26) | copy-start | bytes 24580
  14.9 30.1 %copy-start.1 = (f32[32,1,128,128]{3,2,1,0:T(8,128)S(1)}, f32[32,1,128,128]{3,2,1,0:T(8,128)}, u32[]{:S(2)}) copy-start(f32[32,1,128,128]{3,2,1,0:T(8,128)} %param.22) | copy-start | bytes 6291460
  21.3 23.7 %all-to-all-start.1 = ((bf16[8,2,128,128]{3,2,1,0:T(8,128)(2,1)}), bf16[8,2,128,128]{3,2,1,0:T(8,128)(2,1)S(1)}, u32[]{:S(2)}, u32[]{:S(2)}) async-start(bf16[8,2,128,128]{3,2,1,0:T(8,128)(2,1)} %shard_map.177), calls=%async_computation.1 | async-start | bytes 1048576 | tf_op jit(solution)/shard_map/all_to_all | solution.py:255
  29.8 2.9 %collective-permute-start.1 = (bf16[2048,128]{1,0:T(8,128)(2,1)}, bf16[2048,128]{1,0:T(8,128)(2,1)}, u32[]{:S(2)}, u32[]{:S(2)}) collective-permute-start(bf16[2048,128]{1,0:T(8,128)(2,1)} %w_own.1), channel_id=1, source_target_pairs={{0,1},{1,0},{2,3},{3,2},{4,5},{5,4},{6,7},{7,6},{8,9},{9,8},{10,11... | collective-permute-start | bytes 1572872 | tf_op jit(solution)/shard_map/ppermute | solution.py:22
  29.9 2.8 %collective-permute-start = (bf16[64,2176]{1,0:T(8,128)(2,1)S(1)}, bf16[64,2176]{1,0:T(8,128)(2,1)}, u32[]{:S(2)}, u32[]{:S(2)}) collective-permute-start(bf16[64,2176]{1,0:T(8,128)(2,1)S(1)} %reshape.53.own_in), channel_id=1, source_target_pairs={{0,1},{1,0},{2,3},{3,2},{4,5},{5,4},{6,7},{7,6},{8,9},{9,8},{10,11... | collective-permute-start | bytes 835592 | tf_op jit(solution)/shard_map/ppermute | solution.py:22
  45.0 1.2 %copy-start.2 = (bf16[2048,256]{1,0:T(8,128)(2,1)S(1)}, bf16[2048,256]{1,0:T(8,128)(2,1)}, u32[]{:S(2)}) copy-start(bf16[2048,256]{1,0:T(8,128)(2,1)} %w_vz.1) | copy-start | bytes 3145732
  46.2 1.0 copy-start.3
  52.6 1.7 %copy-start.7 = (f32[32,128]{1,0:T(8,128)}, f32[32,128]{1,0:T(8,128)S(1)}, u32[]{:S(2)}) copy-start(f32[32,128]{1,0:T(8,128)S(1)} %get-tuple-element.21.decay) | copy-start | bytes 49156
  52.6 1.6 %collective-permute-start.2 = (bf16[64,2048]{1,0:T(8,128)(2,1)S(1)}, bf16[64,2048]{1,0:T(8,128)(2,1)S(1)}, u32[]{:S(2)}, u32[]{:S(2)}) collective-permute-start(bf16[64,2048]{1,0:T(8,128)(2,1)S(1)} %get-tuple-element.13), channel_id=1, source_target_pairs={{0,1},{1,0},{2,3},{3,2},{4,5},{5,4},{6,7},{7,6},{8,9},{9,8},{10,11... | collective-permute-start | bytes 786440 | tf_op jit(solution)/shard_map/ppermute | solution.py:22
  54.3 30.8 %collective-permute-start.3 = (bf16[2048,512]{1,0:T(8,128)(2,1)}, bf16[2048,512]{1,0:T(8,128)(2,1)}, u32[]{:S(2)}, u32[]{:S(2)}) collective-permute-start(bf16[2048,512]{1,0:T(8,128)(2,1)} %bitcast.8.up_own), channel_id=1, source_target_pairs={{0,1},{1,0},{2,3},{3,2},{4,5},{5,4},{6,7},{7,6},{8,9},{9,8},{10,11... | collective-permute-start | bytes 6291464 | tf_op jit(solution)/shard_map/ppermute | solution.py:22
  54.5 30.6 %collective-permute-start.4 = (bf16[256,2048]{1,0:T(8,128)(2,1)}, bf16[256,2048]{1,0:T(8,128)(2,1)}, u32[]{:S(2)}, u32[]{:S(2)}) collective-permute-start(bf16[256,2048]{1,0:T(8,128)(2,1)} %bitcast.9.down_own), channel_id=1, source_target_pairs={{0,1},{1,0},{2,3},{3,2},{4,5},{5,4},{6,7},{7,6},{8,9},{9,8},{10,11... | collective-permute-start | bytes 3145736 | tf_op jit(solution)/shard_map/ppermute | solution.py:22
  70.6 0.7 copy-start.6
  72.9 4.2 %copy-start.9 = (bf16[4,2048]{1,0:T(4,128)(2,1)}, bf16[4,2048]{1,0:T(4,128)(2,1)S(1)}, u32[]{:S(2)}) copy-start(bf16[4,2048]{1,0:T(4,128)(2,1)S(1)} %get-tuple-element.18.mixed) | copy-start | bytes 49156
  72.9 12.1 %all-to-all-start.3 = ((bf16[16,4,2048]{2,1,0:T(4,128)(2,1)}), bf16[16,4,2048]{2,1,0:T(4,128)(2,1)S(1)}, u32[]{:S(2)}, u32[]{:S(2)}) async-start(bf16[16,4,2048]{2,1,0:T(4,128)(2,1)} %get-tuple-element.15), calls=%async_computation.3 | async-start | bytes 524288 | tf_op jit(solution)/shard_map/all_to_all | solution.py:28
  85.0 10.1 %copy-start.8 = (f32[32,128]{1,0:T(8,128)S(1)}, f32[32,128]{1,0:T(8,128)}, u32[]{:S(2)}) copy-start(f32[32,128]{1,0:T(8,128)} %copy-done.7) | copy-start | bytes 49156
  85.0 10.1 %copy-start.14 = (s32[2]{0:T(128)S(1)}, s32[2]{0:T(128)}, u32[]{:S(2)}) copy-start(s32[2]{0:T(128)} %copy-done.11) | copy-start | bytes 28
  85.0 10.1 %copy-start.17 = (s32[256]{0:T(256)S(1)}, s32[256]{0:T(256)}, u32[]{:S(2)}) copy-start(s32[256]{0:T(256)} %mig.5) | copy-start | bytes 3076
  85.1 0.7 copy-start.4
  91.5 12.1 %all-to-all-start.4 = ((bf16[16,4,2048]{2,1,0:T(4,128)(2,1)}), bf16[16,4,2048]{2,1,0:T(4,128)(2,1)S(1)}, u32[]{:S(2)}, u32[]{:S(2)}) async-start(bf16[16,4,2048]{2,1,0:T(4,128)(2,1)} %reshape.61), calls=%async_computation.4 | async-start | bytes 524288 | tf_op jit(solution)/shard_map/all_to_all | solution.py:28
  95.2 8.4 %copy-start.10 = (bf16[4,2048]{1,0:T(4,128)(2,1)S(1)}, bf16[4,2048]{1,0:T(4,128)(2,1)}, u32[]{:S(2)}) copy-start(bf16[4,2048]{1,0:T(4,128)(2,1)} %copy-done.9) | copy-start | bytes 49156
  (11 other events, 7.3 us)

commit v2 on v1

v2 whole, which is shorter than its diff:
```python
import functools

import jax
import jax.numpy as jnp
from jax import lax
from jax.experimental import pallas as pl
from jax.experimental.pallas import tpu as pltpu
from jax.sharding import PartitionSpec as P

F32 = jnp.float32
BF16 = jnp.bfloat16
STEPS = 4
CAP = 2
EPS = 1e-06
EXTRA = 128
VMEM = pl.BlockSpec(memory_space=pltpu.VMEM)
HBM = pl.BlockSpec(memory_space=pltpu.HBM)
ANY = pl.BlockSpec(memory_space=pl.ANY)


def core_swap(value):
    n = lax.axis_size("expert")
    return lax.ppermute(value, "expert", [(i, i ^ 1) for i in range(n)])


def hop(value, mask):
    n = lax.axis_size("expert")
    return lax.ppermute(value, "expert", [(i, i ^ mask) for i in range(n)])


def exchange(chunks):
    n = lax.axis_size("expert")
    groups = [list(range(0, n, 2)), list(range(1, n, 2))]
    return lax.all_to_all(
        chunks, "expert", split_axis=0, concat_axis=0, tiled=True, axis_index_groups=groups
    )


def call(kernel, out_shape, in_specs, out_specs, scratch=(), limit=24, flops=0, moved=0):
    return pl.pallas_call(
        kernel,
        out_shape=out_shape,
        in_specs=in_specs,
        out_specs=out_specs,
        scratch_shapes=list(scratch),
        compiler_params=pltpu.CompilerParams(vmem_limit_bytes=limit * 1024 * 1024),
        cost_estimate=pl.CostEstimate(flops=flops, bytes_accessed=moved, transcendentals=0),
    )


def fetch(sems, *pairs):
    copies = [pltpu.make_async_copy(src, dst, sems.at[i]) for i, (src, dst) in enumerate(pairs)]
    for copy in copies:
        copy.start()
    return copies


def start_kernel(
    tok, gain, ids, wts, mask, mig, states, out, parcel,
    tok_v, gain_v, ids_v, wts_v, mask_v, mig_s, picked, loaded, sems, row_sems,
):
    groups = parcel.shape[0]
    rows = states.shape[0]
    bits = rows.bit_length() - 1
    group = lax.axis_index("dp")
    me = lax.axis_index("expert")
    copies = fetch(
        sems, (mig, mig_s), (tok, tok_v), (gain, gain_v), (ids, ids_v), (wts, wts_v), (mask, mask_v)
    )
    copies[0].wait()
    row_copies = []
    for o in range(1, groups):
        base = ((group + o) % groups) * rows
        spot = (CAP + 1) * o
        for slot in range(CAP):
            picked[spot + slot] = 0
        count = jnp.int32(0)
        for i in range(rows):
            old = mig_s[base + i]
            picked[spot + jnp.minimum(count, CAP)] = old & (rows - 1)
            count = count + ((old >> bits) == group).astype(jnp.int32)
        for slot in range(CAP):
            k = (o - 1) * CAP + slot
            copy = pltpu.make_async_copy(
                states.at[picked[spot + slot]], loaded.at[k], row_sems.at[k]
            )
            copy.start()
            row_copies.append(copy)
    for copy in copies[1:]:
        copy.wait()
    x = tok_v[...].astype(F32)
    scale = lax.rsqrt(jnp.mean(x * x, axis=-1, keepdims=True) + EPS)
    normed = (x * scale * gain_v[...]).astype(BF16)
    lane = lax.broadcasted_iota(jnp.int32, (STEPS, EXTRA), 1)
    chosen = ids_v[...]
    weights = wts_v[...].astype(F32)
    comb = jnp.zeros((STEPS, EXTRA), F32)
    for k in range(chosen.shape[1]):
        comb = comb + jnp.where(lane == chosen[:, k : k + 1], weights[:, k : k + 1], 0.0)
    masks = mask_v[...].astype(F32)
    col = lax.broadcasted_iota(jnp.int32, masks.shape, 1)
    own_mask = jnp.sum(jnp.where(col == me, masks, 0.0), axis=-1, keepdims=True)
    comb = jnp.where(lane == EXTRA - 1, own_mask, comb).astype(BF16)
    width = x.shape[1]
    out[:, :width] = normed
    out[:, width:] = comb
    parcel[group] = jnp.zeros(parcel.shape[1:], BF16)
    for k, copy in enumerate(row_copies):
        copy.wait()
        parcel[(group + k // CAP + 1) % groups, k % CAP] = loaded[k].astype(BF16)


def place_moved(mig_s, filled, dest, begin, moved):
    rows = begin.shape[0]
    groups = moved.shape[0]
    group = lax.axis_index("dp")
    for g in range(groups):
        filled[g] = 0
    for r in range(rows):
        g = mig_s[group * rows + r] >> (rows.bit_length() - 1)
        slot = filled[g]
        dest[CAP * g + jnp.minimum(slot, CAP - 1)] = r
        filled[g] = slot + 1
    for g in range(groups):
        for slot in range(CAP):

            @pl.when((filled[g] > slot) & (group != g))
            def _(g=g, slot=slot):
                begin[dest[CAP * g + slot]] = moved[g, slot].astype(F32)


def heads_kernel(
    own_v, other_v, w_other_v, moved, log_rate, bias, w_own, w_vz, w_ab, head_gain, w_out, mig,
    states, tok, post_gain, *refs
):
    part_own, part_other, k_out, w_rows, decay_out, comb_out = refs[:6]
    (
        w_own_v, w_vz_v, w_ab_v, lr_v, bias_v, gain_v, w_out_v, mig_s, begin, tok_v, post_v,
        kq, ks, qs, q_all, v_all, z_all, d_all, b_all, m_all, h_all, dest, filled, sems,
    ) = refs[6:]
    rows = states.shape[0]
    dim = states.shape[1]
    total = rows * STEPS
    width = w_own.shape[0]
    copies = fetch(
        sems, (w_own, w_own_v), (w_vz, w_vz_v),
        (w_ab, w_ab_v), (log_rate, lr_v), (bias, bias_v), (mig, mig_s), (states, begin),
        (head_gain, gain_v), (w_out, w_out_v), (tok, tok_v), (post_gain, post_v),
    )
    for copy in copies[:5]:
        copy.wait()
    x = jnp.concatenate([own_v[:, :width], other_v[:, :width]], axis=0)
    extra = jnp.concatenate([own_v[:, width:], other_v[:, width:]], axis=0).astype(F32)
    live = extra[:, EXTRA - 1 :]
    first = jnp.dot(x, w_own_v[...], preferred_element_type=F32)
    second = jnp.dot(x, w_other_v[...], preferred_element_type=F32)
    vz = jnp.dot(x, w_vz_v[...], preferred_element_type=F32)
    ab = lax.dot_general(
        x, w_ab_v[...], (((1,), (1,)), ((), ())), preferred_element_type=F32
    )
    me = lax.axis_index("expert")
    even = me % 2 == 0
    q = jnp.where(even, first, second)
    k = jnp.where(even, second, first)
    q = q * (lax.rsqrt(jnp.sum(q * q, axis=-1, keepdims=True) + EPS) * dim**-0.5)
    k = k * lax.rsqrt(jnp.sum(k * k, axis=-1, keepdims=True) + EPS)
    beta = jax.nn.sigmoid(ab[:, 1:2])
    rate = jnp.exp(jnp.full((total, 1), lr_v[0], F32))
    drive = ab[:, 0:1] + bias_v[0]
    soft = jnp.maximum(drive, 0.0) + jnp.log1p(jnp.exp(-jnp.abs(drive)))
    decay = jnp.exp(-rate * soft)
    wide = (total, dim)
    q_all[...] = q
    k_out[...] = k
    v_all[...] = vz[:, :dim]
    z_all[...] = vz[:, dim:]
    d_all[...] = jnp.broadcast_to(decay, wide)
    b_all[...] = jnp.broadcast_to(beta, wide)
    m_all[...] = jnp.broadcast_to(live, wide)
    for s in range(rows):
        kq[8 * s : 8 * s + 4] = k[4 * s : 4 * s + 4]
        kq[8 * s + 4 : 8 * s + 8] = q[4 * s : 4 * s + 4]
    for copy in copies[5:]:
        copy.wait()
    place_moved(mig_s, filled, dest, begin, moved)
    for s in range(rows):
        r = me ^ (2 * (s % (rows // 2)) + s // (rows // 2))
        both = jnp.dot(
            kq[8 * s : 8 * s + 8].astype(BF16), begin[r].astype(BF16), preferred_element_type=F32
        )
        ks[4 * s : 4 * s + 4] = both[:4]
        qs[4 * s : 4 * s + 4] = both[4:]

    def at(ref, t):
        return ref[pl.ds(t, rows, stride=STEPS), :]

    kept = jnp.ones((rows, dim), F32)
    past = []
    gain = gain_v[...]
    for t in range(STEPS):
        k_t, q_t, d_t, m_t = at(k_out, t), at(q_all, t), at(d_all, t), at(m_all, t)
        k_state = kept * at(ks, t)
        q_state = kept * at(qs, t)
        for k_s, w_s in past:
            k_state = k_state + jnp.sum(k_t * k_s, axis=-1, keepdims=True) * w_s
            q_state = q_state + jnp.sum(q_t * k_s, axis=-1, keepdims=True) * w_s
        write = at(b_all, t) * (at(v_all, t) - d_t * k_state)
        o = d_t * q_state + jnp.sum(q_t * k_t, axis=-1, keepdims=True) * write
        scale = lax.rsqrt(jnp.mean(o * o, axis=-1, keepdims=True) + EPS)
        z_t = at(z_all, t)
        h_all[pl.ds(t, rows, stride=STEPS), :] = o * scale * gain * (z_t * jax.nn.sigmoid(z_t))
        alive = m_t > 0.5
        a_t = jnp.where(alive, d_t, 1.0)
        kept = kept * a_t
        past = [(k_s, w_s * a_t) for k_s, w_s in past] + [(k_t, jnp.where(alive, write, 0.0))]
    for t in range(STEPS):
        w_rows[pl.ds(t, rows, stride=STEPS), :] = past[t][1]
    decay_out[...] = kept
    part = jnp.dot(h_all[...].astype(BF16), w_out_v[...], preferred_element_type=F32)
    for u in range(rows // 2):
        chip = (me // 2) ^ u
        own = part[STEPS * u : STEPS * (u + 1)]
        if u == 0:
            own = own + tok_v[...].astype(F32)
        part_own[chip] = own.astype(BF16)
        part_other[chip] = part[STEPS * (rows // 2 + u) : STEPS * (rows // 2 + u + 1)].astype(BF16)
        comb_out[chip, :STEPS] = extra[STEPS * u : STEPS * (u + 1)]
        comb_out[u, STEPS : STEPS + 1] = post_v[:, EXTRA * u : EXTRA * (u + 1)]


def state_kernel(k_in, w_rows, decay, mig, states, *refs):
    moved, out, mig_s, dest, filled, sems = refs
    rows = states.shape[0]
    copies = fetch(
        sems, (mig, mig_s), (states, out)
    )
    for copy in copies:
        copy.wait()
    place_moved(mig_s, filled, dest, out, moved)
    me = lax.axis_index("expert")
    for s in range(rows):
        r = me ^ (2 * (s % (rows // 2)) + s // (rows // 2))
        k_s = k_in[4 * s : 4 * s + 4, :]
        w_s = w_rows[4 * s : 4 * s + 4, :]
        outer = lax.dot_general(k_s, w_s, (((0,), (0,)), ((), ())), preferred_element_type=F32)
        out[r] = decay[s : s + 1, :] * out[r] + outer


def mixed_kernel(got, out, mixed_out):
    mixed = jnp.sum(got[...].astype(F32), axis=0).astype(BF16)
    mixed_out[...] = mixed
    m = mixed.astype(F32)
    scale = lax.rsqrt(jnp.mean(m * m, axis=-1, keepdims=True) + EPS)
    normed = (m * scale).astype(BF16)
    for j in range(out.shape[0]):
        out[j] = normed


def expert_kernel(
    rows_in, packed, up_own, up_other, down_own, down_other, out,
    extra_v, up_own_v, up_other_v, down_own_v, down_other_v, sems,
):
    half = rows_in.shape[0] * STEPS
    copies = fetch(
        sems, (up_own, up_own_v), (down_own, down_own_v), (up_other, up_other_v),
        (down_other, down_other_v), (packed, extra_v),
    )
    me = lax.axis_index("expert")
    partner = me + 1 - 2 * (me % 2)
    copies[4].wait()
    extra = extra_v[...]
    gain = jnp.concatenate([extra[j, STEPS : STEPS + 1] for j in range(extra.shape[0])], axis=1)
    x = (rows_in[...].astype(F32).reshape(half, -1) * gain).astype(BF16)
    comb = extra[:, :STEPS].reshape(half, EXTRA)
    lane = lax.broadcasted_iota(jnp.int32, comb.shape, 1)
    total = None
    for index, up, down, up_copy, down_copy in (
        (me, up_own_v, down_own_v, copies[0], copies[1]),
        (partner, up_other_v, down_other_v, copies[2], copies[3]),
    ):
        hidden = down.shape[0]
        up_copy.wait()
        proj = jnp.dot(x, up[...], preferred_element_type=F32)
        g, u = proj[:, :hidden], proj[:, hidden:]
        act = (g * jax.nn.sigmoid(g) * u).astype(BF16)
        weight = jnp.sum(jnp.where(lane == index, comb, 0.0), axis=-1, keepdims=True)
        down_copy.wait()
        result = weight * jnp.dot(act, down[...], preferred_element_type=F32)
        total = result if total is None else total + result
    total = total.astype(BF16)
    for j in range(out.shape[0]):
        out[j] = total[STEPS * j : STEPS * (j + 1)]


def sum_kernel(got, mixed, out):
    out[...] = (mixed[...].astype(F32) + jnp.sum(got[...].astype(F32), axis=0)).astype(BF16)


def body(
    tokens, route_ids, route_weights, active_mask, migration, state_in, in_gain, query_key,
    value_gate, gates_proj, log_rate, step_bias, head_gain, out_proj, post_gain, expert_up,
    expert_down,
):
    groups = lax.axis_size("dp")
    members = lax.axis_size("expert")
    rows = state_in.shape[0]
    dim = state_in.shape[2]
    width = tokens.shape[2]
    peers = members // 2
    half = rows * STEPS // 2
    total = rows * STEPS
    sds = jax.ShapeDtypeStruct
    vm = pltpu.VMEM
    dma = pltpu.SemaphoreType.DMA
    tok = tokens.reshape(STEPS, width)
    states = state_in.reshape(rows, dim, dim)
    top = route_ids.shape[2]

    w_other = core_swap(query_key)
    payload, parcel = call(
        start_kernel,
        (sds((STEPS, width + EXTRA), BF16), sds((groups, CAP, dim, dim), BF16)),
        [HBM] * 7,
        (VMEM, VMEM),
        scratch=[
            vm((STEPS, width), BF16), vm((1, width), F32), vm((STEPS, top), jnp.int32),
            vm((STEPS, top), BF16), vm((STEPS, rows), jnp.int32),
            pltpu.SMEM((groups * rows,), jnp.int32), pltpu.SMEM((groups * (CAP + 1),), jnp.int32),
            vm(((groups - 1) * CAP, dim, dim), F32), dma((6,)), dma(((groups - 1) * CAP,)),
        ],
        limit=60,
    )(
        tok, in_gain.reshape(1, width), route_ids.reshape(STEPS, top),
        route_weights.reshape(STEPS, top), active_mask, migration, states,
    )
    recv = lax.all_to_all(parcel, "dp", split_axis=0, concat_axis=0, tiled=True)
    line = jnp.concatenate([payload] + [hop(payload, m) for m in (2, 4, 6)])
    own_in = jnp.concatenate([line] + [hop(line, m) for m in (8, 16, 24)])
    other_in = core_swap(own_in)

    tall = vm((total, dim), F32)
    plan = [pltpu.SMEM((groups * CAP,), jnp.int32), pltpu.SMEM((groups,), jnp.int32)]
    part_own, part_other, k_rows, w_rows, decay, comb = call(
        heads_kernel,
        (
            sds((peers, STEPS, width), BF16), sds((peers, STEPS, width), BF16),
            sds((total, dim), F32), sds((total, dim), F32), sds((rows, dim), F32),
            sds((peers, 2 * STEPS, EXTRA), F32),
        ),
        [VMEM] * 4 + [HBM] * 11,
        (VMEM,) * 6,
        scratch=[
            vm((width, dim), BF16), vm((width, 2 * dim), BF16), vm((2, width), BF16),
            pltpu.SMEM((1,), F32), pltpu.SMEM((1,), F32),
            vm((1, dim), F32), vm((dim, width), BF16), pltpu.SMEM((groups * rows,), jnp.int32),
            vm((rows, dim, dim), F32), vm((STEPS, width), BF16), vm((1, width), F32),
            vm((2 * total, dim), F32),
        ] + [tall] * 9 + plan + [dma((11,))],
        flops=2 * total * width * 700,
        moved=6 << 20,
        limit=52,
    )(
        own_in, other_in, w_other, recv, log_rate, step_bias, query_key, value_gate, gates_proj.T,
        head_gain.reshape(1, dim), out_proj, migration, states, tok, post_gain.reshape(1, width),
    )
    swapped = core_swap(part_other)
    up_own = expert_up.reshape(width, -1)
    down_own = expert_down.reshape(-1, width)
    hidden = down_own.shape[0]
    part = (part_own.astype(F32) + swapped.astype(F32)).astype(BF16)
    part, up_out, down_out = lax.optimization_barrier((part, up_own, down_own))
    up_other = core_swap(up_out)
    down_other = core_swap(down_out)
    got = exchange(part)

    state_out = call(
        state_kernel,
        sds((rows, dim, dim), F32),
        [VMEM] * 3 + [HBM] * 2 + [VMEM],
        VMEM,
        scratch=[pltpu.SMEM((groups * rows,), jnp.int32)] + plan + [dma((2,))],
        flops=2 * total * dim * dim,
        moved=5 << 20,
    )(k_rows, w_rows, decay, migration, states, recv)

    moe, mixed = call(
        mixed_kernel,
        (sds((peers, STEPS, width), BF16), sds((STEPS, width), BF16)),
        [VMEM],
        (VMEM, VMEM),
    )(got)
    moe_rows = exchange(moe)
    served = call(
        expert_kernel,
        sds((peers, STEPS, width), BF16),
        [VMEM, ANY] + [HBM] * 4,
        VMEM,
        scratch=[
            vm((peers, 2 * STEPS, EXTRA), F32), vm((width, 2 * hidden), BF16), vm((width, 2 * hidden), BF16),
            vm((hidden, width), BF16), vm((hidden, width), BF16), dma((5,)),
        ],
        flops=1 << 29,
        moved=7 << 20,
    )(moe_rows, comb, up_own, up_other, down_own, down_other)
    back = exchange(served)
    out = call(sum_kernel, sds((STEPS, width), BF16), [VMEM] * 2, VMEM)(back, mixed)
    return (out.reshape(STEPS, 1, width), state_out.reshape(state_in.shape))


def solution(mesh):
    in_specs = (
        P(None, ("dp", "expert"), None),
        P(None, ("dp", "expert"), None),
        P(None, ("dp", "expert"), None),
        P(None, "dp"),
        P(),
        P("dp", "expert", None, None),
        P(),
        P(None, "expert"),
        P(None, "expert"),
        P(None, "expert"),
        P("expert"),
        P("expert"),
        P(),
        P("expert", None),
        P(),
        P("expert", None, None),
        P("expert", None, None),
    )
    out_specs = (P(None, ("dp", "expert"), None), P("dp", "expert", None, None))
    return jax.shard_map(body, mesh=mesh, in_specs=in_specs, out_specs=out_specs, check_vma=False)
```

time: 106 us -> 83.9 us (0.79); the launches traced: 104 us -> 83.3 us
  local copies, waits for them, and re-layouts: 15.3 us -> 1.69 us
  waiting for transfers between devices: 28 us -> 17 us
  blocking collectives: 15.5 us -> 23.8 us
  Pallas kernels: 18.4 us -> 15.1 us
  starting transfers between devices: 24.2 us -> 22.8 us
    unnamed x53 -> x22, local copies, waits for them, and re-layouts: 13.7 us -> 0.84 us
    all_to_all x1, waiting for transfers between devices: 12.2 us -> 0.01 us  [body(): recv = lax.all_to_all(parcel, 'dp', split_axis=0, concat_axis=0, tiled=True)]
    all_to_all x3 -> x1, starting transfers between devices: 14.3 us -> 3.64 us  [exchange(): lax.all_to_all(chunks, 'expert', split_axis=0, concat_axis=0, tiled=True,...]
    ppermute x0 -> x6, waiting for transfers between devices: none -> 9.98 us  [hop(): return lax.ppermute(value, 'expert', [(i, i ^ mask) for i in range(n)])]
    ppermute x0 -> x6, starting transfers between devices: none -> 9.48 us  [hop(): return lax.ppermute(value, 'expert', [(i, i ^ mask) for i in range(n)])]
    all_to_all x3 -> x1, waiting for transfers between devices: 14.3 us -> 5.49 us  [exchange(): lax.all_to_all(chunks, 'expert', split_axis=0, concat_axis=0, tiled=True,...]
    all_to_all x1 -> x2, blocking collectives: 15.5 us -> 23.8 us  [exchange(): lax.all_to_all(chunks, 'expert', split_axis=0, concat_axis=0, tiled=True,...]
    pallas_call x5 -> x4, Pallas kernels: 16.7 us -> 14.2 us  [the longest x1 4.64 us: body(): call(heads_kernel, (sds((peers, STEPS, width), BF16), sds((peers, STEPS,...]
  transfers between devices with their start and end apart: 9 -> 13, of which waited for: 5 -> 7; matrix products, arithmetic and copies ran while one was open for 2% -> 2% of each run, Pallas kernels for 9% -> 4%
where the time goes in v2:
time: 83.9 us; the launch traced here: 83.3 us
  blocking collectives  23.8 us (28%)
  starting transfers between devices  22.8 us (27%)
  waiting for transfers between devices  17 us (20%)
  Pallas kernels  15.1 us (18%)
  between operations  2.12 us (3%)
  local copies, waits for them, and re-layouts  1.69 us (2%)
  other arithmetic  0.92 us (1%)
    all_to_all x2, blocking collectives, exchange(): lax.all_to_all(chunks, 'expert', split_axis=0, concat_axis=0, tiled=True,...  23.8 us
    ppermute x6, waiting for transfers between devices, hop(): return lax.ppermute(value, 'expert', [(i, i ^ mask) for i in range(n)])  9.98 us
    ppermute x6, starting transfers between devices, hop(): return lax.ppermute(value, 'expert', [(i, i ^ mask) for i in range(n)])  9.48 us
    all_to_all x1, starting transfers between devices, body(): recv = lax.all_to_all(parcel, 'dp', split_axis=0, concat_axis=0, tiled=True)  8.58 us
    all_to_all x1, waiting for transfers between devices, exchange(): lax.all_to_all(chunks, 'expert', split_axis=0, concat_axis=0, tiled=True,...  5.49 us
    pallas_call x1, Pallas kernels, body(): call(heads_kernel, (sds((peers, STEPS, width), BF16), sds((peers, STEPS,...  4.64 us
    all_to_all x1, starting transfers between devices, exchange(): lax.all_to_all(chunks, 'expert', split_axis=0, concat_axis=0, tiled=True,...  3.64 us
    pallas_call x1, Pallas kernels, body(): call(start_kernel, (sds((STEPS, width + EXTRA), BF16), sds((groups, CAP,...  3.6 us
  transfers between devices with their start and end apart: 13, of which 7 were waited for; matrix products, arithmetic and copies ran while one was open for 2% of the time, Pallas kernels for 4%

profile of v2, /device:TPU:32, one launch (start us, length us, event | category | flops | bytes accessed | tf_op | source)
XLA Modules:
  0.0 83.3 jit_solution(15782656399981178937)
XLA Ops:
  0.7 3.6 %shard_map.176 = (bf16[4,2176]{1,0:T(4,128)(2,1)}, bf16[8,2,128,128]{3,2,1,0:T(8,128)(2,1)}) custom-call(bf16[4,2048]{1,0:T(4,128)(2,1)} %bitcast.21, f32[1,2048]{1,0:T(1,128)} %bitcast.28, s32[4,10]{1,0:T(4,128)} %bitcast.29, bf16[4,10]{1,0:T(4,128)(2,1)} %bitcast.30, s32[4,32]{1,0:T(4,128)} %mask.1, s32[256]{0:T(256)} %mig.5, f32[32,128,128]{2,1,0:T(8,128)} %bitcast.14), custom_call_target="tpu_custom_call" | custom-call | tf_op jit(solution)/shard_map/pallas_call | solution.py:320
  4.3 8.6 %all-to-all-start = ((bf16[8,2,128,128]{3,2,1,0:T(8,128)(2,1)}), bf16[8,2,128,128]{3,2,1,0:T(8,128)(2,1)S(1)}, u32[]{:S(2)}, u32[]{:S(2)}) async-start(bf16[8,2,128,128]{3,2,1,0:T(8,128)(2,1)} %get-tuple-element.16), calls=%async_computation | async-start | bytes 1048576 | tf_op jit(solution)/shard_map/all_to_all | solution.py:336
  12.9 1.6 %collective-permute-start = (bf16[4,2176]{1,0:T(4,128)(2,1)}, bf16[4,2176]{1,0:T(4,128)(2,1)S(1)}, u32[]{:S(2)}, u32[]{:S(2)}) collective-permute-start(bf16[4,2176]{1,0:T(4,128)(2,1)} %get-tuple-element.15), channel_id=1, source_target_pairs={{0,2},{1,3},{2,0},{3,1},{4,6},{5,7},{6,4},{7,5},{8,10},{9,11},{10,... | collective-permute-start | bytes 52232 | tf_op jit(solution)/shard_map/ppermute | solution.py:28
  14.5 2.9 %collective-permute-start.1 = (bf16[4,2176]{1,0:T(4,128)(2,1)}, bf16[4,2176]{1,0:T(4,128)(2,1)S(1)}, u32[]{:S(2)}, u32[]{:S(2)}) collective-permute-start(bf16[4,2176]{1,0:T(4,128)(2,1)} %get-tuple-element.15), channel_id=1, source_target_pairs={{0,4},{1,5},{2,6},{3,7},{4,0},{5,1},{6,2},{7,3},{8,12},{9,13},{10,... | collective-permute-start | bytes 52232 | tf_op jit(solution)/shard_map/ppermute | solution.py:28
  17.6 2.3 %collective-permute-done.1 = bf16[4,2176]{1,0:T(4,128)(2,1)S(1)} collective-permute-done((bf16[4,2176]{1,0:T(4,128)(2,1)}, bf16[4,2176]{1,0:T(4,128)(2,1)S(1)}, u32[]{:S(2)}, u32[]{:S(2)}) %collective-permute-start.1) | collective-permute-done | bytes 17440 | tf_op jit(solution)/shard_map/ppermute | solution.py:28
  19.9 2.6 %collective-permute-done.2 = bf16[4,2176]{1,0:T(4,128)(2,1)S(1)} collective-permute-done((bf16[4,2176]{1,0:T(4,128)(2,1)}, bf16[4,2176]{1,0:T(4,128)(2,1)S(1)}, u32[]{:S(2)}, u32[]{:S(2)}) %collective-permute-start.2) | collective-permute-done | bytes 17440 | tf_op jit(solution)/shard_map/ppermute | solution.py:28
  22.5 0.8 pad_maximum_fusion
  23.3 1.6 %collective-permute-start.3 = (bf16[16,2176]{1,0:T(8,128)(2,1)S(1)}, bf16[16,2176]{1,0:T(8,128)(2,1)S(1)}, u32[]{:S(2)}, u32[]{:S(2)}) collective-permute-start(bf16[16,2176]{1,0:T(8,128)(2,1)S(1)} %pad_maximum_fusion), channel_id=1, source_target_pairs={{0,8},{1,9},{2,10},{3,11},{4,12},{5,13},{6,14},{7,15},{8,0},{9,1},... | collective-permute-start | bytes 208904 | tf_op jit(solution)/shard_map/ppermute | solution.py:28
  24.9 2.7 %collective-permute-start.4 = (bf16[16,2176]{1,0:T(8,128)(2,1)S(1)}, bf16[16,2176]{1,0:T(8,128)(2,1)S(1)}, u32[]{:S(2)}, u32[]{:S(2)}) collective-permute-start(bf16[16,2176]{1,0:T(8,128)(2,1)S(1)} %pad_maximum_fusion), channel_id=1, source_target_pairs={{0,16},{1,17},{2,18},{3,19},{4,20},{5,21},{6,22},{7,23},{8,24},{9,... | collective-permute-start | bytes 208904 | tf_op jit(solution)/shard_map/ppermute | solution.py:28
  27.6 0.5 collective-permute-start.5
  28.1 2.6 %collective-permute-done.4 = bf16[16,2176]{1,0:T(8,128)(2,1)S(1)} collective-permute-done((bf16[16,2176]{1,0:T(8,128)(2,1)S(1)}, bf16[16,2176]{1,0:T(8,128)(2,1)S(1)}, u32[]{:S(2)}, u32[]{:S(2)}) %collective-permute-start.4) | collective-permute-done | bytes 69664 | tf_op jit(solution)/shard_map/ppermute | solution.py:28
  30.7 2.4 %collective-permute-done.5 = bf16[16,2176]{1,0:T(8,128)(2,1)S(1)} collective-permute-done((bf16[16,2176]{1,0:T(8,128)(2,1)S(1)}, bf16[16,2176]{1,0:T(8,128)(2,1)S(1)}, u32[]{:S(2)}, u32[]{:S(2)}) %collective-permute-start.5) | collective-permute-done | bytes 69664 | tf_op jit(solution)/shard_map/ppermute | solution.py:28
  33.1 0.8 %concatenate.8.own_v = bf16[64,2176]{1,0:T(8,128)(2,1)S(1)} concatenate(bf16[4,2176]{1,0:T(4,128)(2,1)} %get-tuple-element.15, bf16[4,2176]{1,0:T(4,128)(2,1)S(1)} %collective-permute-done, bf16[4,2176]{1,0:T(4,128)(2,1)S(1)} %collective-permute-done.1, bf16[4,2176]{1,0:T(4,128)(2,1)S(1)} %collective-permute-done.2, bf16[16,2176]{1,0:T(8,128)(2,1)S(1)} %collective-permute-done.3, ...), dimensions={0} | concatenate | bytes 557056 | tf_op jit(solution)/shard_map/concatenate | solution.py:338
  35.6 0.8 copy-done.1
  36.5 4.6 %shard_map.177 = (bf16[16,4,2048]{2,1,0:T(4,128)(2,1)S(1)}, bf16[16,4,2048]{2,1,0:T(4,128)(2,1)S(1)}, f32[128,128]{1,0:T(8,128)S(1)}, f32[128,128]{1,0:T(8,128)S...) custom-call(bf16[64,2176]{1,0:T(8,128)(2,1)S(1)} %concatenate.8.own_v, ...), custom_call_target="tpu_custom_call" | custom-call | flops 367001600 | bytes 6291456 | tf_op jit(solution)/shard_map/pallas_call | solution.py:343
  41.1 0.4 collective-permute-start.8
  41.5 1.3 %collective-permute-done.8 = bf16[16,4,2048]{2,1,0:T(4,128)(2,1)S(1)} collective-permute-done((bf16[16,4,2048]{2,1,0:T(4,128)(2,1)S(1)}, bf16[16,4,2048]{2,1,0:T(4,128)(2,1)S(1)}, u32[]{:S(2)}, u32[]{:S(2)}) %collective-permute-start.8) | collective-permute-done | bytes 262176 | tf_op jit(solution)/shard_map/ppermute | solution.py:23
  43.5 11.8 %all_to_all.20.got = bf16[16,4,2048]{2,1,0:T(4,128)(2,1)S(1)} all-to-all(bf16[16,4,2048]{2,1,0:T(4,128)(2,1)S(1)} %add_convert_fusion), channel_id=1, replica_groups={{0,2,4,6,8,10,12,14,16,18,20,22,24,26,28,30},{1,3,5,7,9,11,13,15,17,19,..., dimensions={0} | all-to-all | bytes 524288 | tf_op jit(solution)/shard_map/all_to_all | solution.py:34
  55.5 12.0 %all_to_all.21.rows_in = bf16[16,4,2048]{2,1,0:T(4,128)(2,1)S(1)} all-to-all(bf16[16,4,2048]{2,1,0:T(4,128)(2,1)S(1)} %get-tuple-element.20), channel_id=1, replica_groups={{0,2,4,6,8,10,12,14,16,18,20,22,24,26,28,30},{1,3,5,7,9,11,13,15,17,19,..., dimensions={0} | all-to-all | bytes 524288 | tf_op jit(solution)/shard_map/all_to_all | solution.py:34
  67.5 3.0 %shard_map.179 = bf16[16,4,2048]{2,1,0:T(4,128)(2,1)} custom-call(bf16[16,4,2048]{2,1,0:T(4,128)(2,1)S(1)} %all_to_all.21.rows_in, f32[16,8,128]{2,1,0:T(8,128)S(1)} %get-tuple-element.21.packed, bf16[2048,512]{1,0:T(8,128)(2,1)S(1)} %bitcast.18, bf16[2048,512]{1,0:T(8,128)(2,1)S(1)} %collective-permute-done.9.up_other, bf16[256,2048]{1,0:T(8,128)(2,1)S(1)} %bitcast.20, ...), custom_call_target="tpu_custom_call" | custom-call | flops 536870912 | bytes 7340032 | tf_op jit(solution)/shard_map/pallas_call | solution.py:393
  70.5 3.6 %all-to-all-start.3 = ((bf16[16,4,2048]{2,1,0:T(4,128)(2,1)}), bf16[16,4,2048]{2,1,0:T(4,128)(2,1)S(1)}, u32[]{:S(2)}, u32[]{:S(2)}) async-start(bf16[16,4,2048]{2,1,0:T(4,128)(2,1)} %shard_map.179), calls=%async_computation.3 | async-start | bytes 524288 | tf_op jit(solution)/shard_map/all_to_all | solution.py:34
  74.2 3.0 %shard_map.181 = f32[32,128,128]{2,1,0:T(8,128)} custom-call(f32[128,128]{1,0:T(8,128)S(1)} %get-tuple-element.25.k_in, f32[128,128]{1,0:T(8,128)S(1)} %get-tuple-element.26.w_rows, f32[32,128]{1,0:T(8,128)S(1)} %get-tuple-element.27.decay, s32[256]{0:T(256)S(1)} %copy-done.6, f32[32,128,128]{2,1,0:T(8,128)S(1)} %bitcast.16, ...), custom_call_target="tpu_custom_call" | custom-call | flops 4194304 | bytes 5242880 | tf_op jit(solution)/shard_map/pallas_call | solution.py:376
  77.1 5.5 %all-to-all-done.3.got = bf16[16,4,2048]{2,1,0:T(4,128)(2,1)S(1)} async-done(((bf16[16,4,2048]{2,1,0:T(4,128)(2,1)}), bf16[16,4,2048]{2,1,0:T(4,128)(2,1)S(1)}, u32[]{:S(2)}, u32[]{:S(2)}) %all-to-all-start.3) | async-done | bytes 262176 | tf_op jit(solution)/shard_map/all_to_all | solution.py:34
  82.6 0.7 shard_map.180
  (35 shorter events, 1.6 us)
Async XLA Ops:
  0.6 35.8 %copy-start.5 = (bf16[4,1,2048]{2,0,1:T(4,128)(2,1)S(1)}, bf16[4,1,2048]{2,0,1:T(4,128)(2,1)}, u32[]{:S(2)}) copy-start(bf16[4,1,2048]{2,0,1:T(4,128)(2,1)} %param.17) | copy-start | bytes 49156
  0.6 35.8 %copy-start.6 = (s32[256]{0:T(256)S(1)}, s32[256]{0:T(256)}, u32[]{:S(2)}) copy-start(s32[256]{0:T(256)} %mig.5) | copy-start | bytes 3076
  0.7 16.9 %copy-start.10 = (bf16[2048,128]{1,0:T(8,128)(2,1)S(1)}, bf16[2048,128]{1,0:T(8,128)(2,1)}, u32[]{:S(2)}) copy-start(bf16[2048,128]{1,0:T(8,128)(2,1)} %w_own.1) | copy-start | bytes 1572868
  0.7 35.8 %copy-start.7 = (bf16[2048,2]{0,1:T(2,128)(2,1)S(1)}, bf16[2048,2]{0,1:T(2,128)(2,1)}, u32[]{:S(2)}) copy-start(bf16[2048,2]{0,1:T(2,128)(2,1)} %param.26) | copy-start | bytes 24580
  0.7 35.8 %copy-start.9 = (f32[128]{0:T(128)S(1)}, f32[128]{0:T(128)}, u32[]{:S(2)}) copy-start(f32[128]{0:T(128)} %param.29) | copy-start | bytes 1540
  0.7 35.7 %copy-start.8 = (f32[2048]{0:T(1024)S(1)}, f32[2048]{0:T(1024)}, u32[]{:S(2)}) copy-start(f32[2048]{0:T(1024)} %param.31) | copy-start | bytes 24580
  4.3 31.3 %all-to-all-start = ((bf16[8,2,128,128]{3,2,1,0:T(8,128)(2,1)}), bf16[8,2,128,128]{3,2,1,0:T(8,128)(2,1)S(1)}, u32[]{:S(2)}, u32[]{:S(2)}) async-start(bf16[8,2,128,128]{3,2,1,0:T(8,128)(2,1)} %get-tuple-element.16), calls=%async_computation | async-start | bytes 1048576 | tf_op jit(solution)/shard_map/all_to_all | solution.py:336
  12.9 4.7 %collective-permute-start = (bf16[4,2176]{1,0:T(4,128)(2,1)}, bf16[4,2176]{1,0:T(4,128)(2,1)S(1)}, u32[]{:S(2)}, u32[]{:S(2)}) collective-permute-start(bf16[4,2176]{1,0:T(4,128)(2,1)} %get-tuple-element.15), channel_id=1, source_target_pairs={{0,2},{1,3},{2,0},{3,1},{4,6},{5,7},{6,4},{7,5},{8,10},{9,11},{10,... | collective-permute-start | bytes 52232 | tf_op jit(solution)/shard_map/ppermute | solution.py:28
  14.5 5.5 %collective-permute-start.1 = (bf16[4,2176]{1,0:T(4,128)(2,1)}, bf16[4,2176]{1,0:T(4,128)(2,1)S(1)}, u32[]{:S(2)}, u32[]{:S(2)}) collective-permute-start(bf16[4,2176]{1,0:T(4,128)(2,1)} %get-tuple-element.15), channel_id=1, source_target_pairs={{0,4},{1,5},{2,6},{3,7},{4,0},{5,1},{6,2},{7,3},{8,12},{9,13},{10,... | collective-permute-start | bytes 52232 | tf_op jit(solution)/shard_map/ppermute | solution.py:28
  17.4 5.2 %collective-permute-start.2 = (bf16[4,2176]{1,0:T(4,128)(2,1)}, bf16[4,2176]{1,0:T(4,128)(2,1)S(1)}, u32[]{:S(2)}, u32[]{:S(2)}) collective-permute-start(bf16[4,2176]{1,0:T(4,128)(2,1)} %get-tuple-element.15), channel_id=1, source_target_pairs={{0,6},{1,7},{2,4},{3,5},{4,2},{5,3},{6,0},{7,1},{8,14},{9,15},{10,... | collective-permute-start | bytes 52232 | tf_op jit(solution)/shard_map/ppermute | solution.py:28
  17.6 18.0 %collective-permute-start.7 = (bf16[2048,128]{1,0:T(8,128)(2,1)S(1)}, bf16[2048,128]{1,0:T(8,128)(2,1)S(1)}, u32[]{:S(2)}, u32[]{:S(2)}) collective-permute-start(bf16[2048,128]{1,0:T(8,128)(2,1)S(1)} %copy-done.10), channel_id=1, source_target_pairs={{0,1},{1,0},{2,3},{3,2},{4,5},{5,4},{6,7},{7,6},{8,9},{9,8},{10,11... | collective-permute-start | bytes 1572872 | tf_op jit(solution)/shard_map/ppermute | solution.py:23
  23.3 4.8 %collective-permute-start.3 = (bf16[16,2176]{1,0:T(8,128)(2,1)S(1)}, bf16[16,2176]{1,0:T(8,128)(2,1)S(1)}, u32[]{:S(2)}, u32[]{:S(2)}) collective-permute-start(bf16[16,2176]{1,0:T(8,128)(2,1)S(1)} %pad_maximum_fusion), channel_id=1, source_target_pairs={{0,8},{1,9},{2,10},{3,11},{4,12},{5,13},{6,14},{7,15},{8,0},{9,1},... | collective-permute-start | bytes 208904 | tf_op jit(solution)/shard_map/ppermute | solution.py:28
  24.9 5.8 %collective-permute-start.4 = (bf16[16,2176]{1,0:T(8,128)(2,1)S(1)}, bf16[16,2176]{1,0:T(8,128)(2,1)S(1)}, u32[]{:S(2)}, u32[]{:S(2)}) collective-permute-start(bf16[16,2176]{1,0:T(8,128)(2,1)S(1)} %pad_maximum_fusion), channel_id=1, source_target_pairs={{0,16},{1,17},{2,18},{3,19},{4,20},{5,21},{6,22},{7,23},{8,24},{9,... | collective-permute-start | bytes 208904 | tf_op jit(solution)/shard_map/ppermute | solution.py:28
  27.6 5.5 %collective-permute-start.5 = (bf16[16,2176]{1,0:T(8,128)(2,1)S(1)}, bf16[16,2176]{1,0:T(8,128)(2,1)S(1)}, u32[]{:S(2)}, u32[]{:S(2)}) collective-permute-start(bf16[16,2176]{1,0:T(8,128)(2,1)S(1)} %pad_maximum_fusion), channel_id=1, source_target_pairs={{0,24},{1,25},{2,26},{3,27},{4,28},{5,29},{6,30},{7,31},{8,16},{9,... | collective-permute-start | bytes 208904 | tf_op jit(solution)/shard_map/ppermute | solution.py:28
  34.0 1.6 %collective-permute-start.6 = (bf16[64,2176]{1,0:T(8,128)(2,1)S(1)}, bf16[64,2176]{1,0:T(8,128)(2,1)S(1)}, u32[]{:S(2)}, u32[]{:S(2)}) collective-permute-start(bf16[64,2176]{1,0:T(8,128)(2,1)S(1)} %concatenate.8.own_v), channel_id=1, source_target_pairs={{0,1},{1,0},{2,3},{3,2},{4,5},{5,4},{6,7},{7,6},{8,9},{9,8},{10,11... | collective-permute-start | bytes 835592 | tf_op jit(solution)/shard_map/ppermute | solution.py:23
  35.6 0.8 copy-start.1
  36.4 6.5 %copy-start.3 = (bf16[1,2048,512]{2,1,0:T(8,128)(2,1)S(1)}, bf16[1,2048,512]{2,1,0:T(8,128)(2,1)}, u32[]{:S(2)}) copy-start(bf16[1,2048,512]{2,1,0:T(8,128)(2,1)} %param.32) | copy-start | bytes 6291460
  36.5 6.8 %copy-start.4 = (bf16[1,256,2048]{2,1,0:T(8,128)(2,1)S(1)}, bf16[1,256,2048]{2,1,0:T(8,128)(2,1)}, u32[]{:S(2)}) copy-start(bf16[1,256,2048]{2,1,0:T(8,128)(2,1)} %param.33) | copy-start | bytes 3145732
  41.1 1.6 %collective-permute-start.8 = (bf16[16,4,2048]{2,1,0:T(4,128)(2,1)S(1)}, bf16[16,4,2048]{2,1,0:T(4,128)(2,1)S(1)}, u32[]{:S(2)}, u32[]{:S(2)}) collective-permute-start(bf16[16,4,2048]{2,1,0:T(4,128)(2,1)S(1)} %get-tuple-element.18), channel_id=1, source_target_pairs={{0,1},{1,0},{2,3},{3,2},{4,5},{5,4},{6,7},{7,6},{8,9},{9,8},{10,11... | collective-permute-start | bytes 786440 | tf_op jit(solution)/shard_map/ppermute | solution.py:23
  42.9 24.6 %collective-permute-start.9 = (bf16[2048,512]{1,0:T(8,128)(2,1)S(1)}, bf16[2048,512]{1,0:T(8,128)(2,1)S(1)}, u32[]{:S(2)}, u32[]{:S(2)}) collective-permute-start(bf16[2048,512]{1,0:T(8,128)(2,1)S(1)} %bitcast.17), channel_id=1, source_target_pairs={{0,1},{1,0},{2,3},{3,2},{4,5},{5,4},{6,7},{7,6},{8,9},{9,8},{10,11... | collective-permute-start | bytes 6291464 | tf_op jit(solution)/shard_map/ppermute | solution.py:23
  43.3 24.2 %collective-permute-start.10 = (bf16[256,2048]{1,0:T(8,128)(2,1)S(1)}, bf16[256,2048]{1,0:T(8,128)(2,1)S(1)}, u32[]{:S(2)}, u32[]{:S(2)}) collective-permute-start(bf16[256,2048]{1,0:T(8,128)(2,1)S(1)} %bitcast.19), channel_id=1, source_target_pairs={{0,1},{1,0},{2,3},{3,2},{4,5},{5,4},{6,7},{7,6},{8,9},{9,8},{10,11... | collective-permute-start | bytes 3145736 | tf_op jit(solution)/shard_map/ppermute | solution.py:23
  67.5 6.6 %copy-start = (f32[32,1,128,128]{3,2,1,0:T(8,128)S(1)}, f32[32,1,128,128]{3,2,1,0:T(8,128)}, u32[]{:S(2)}) copy-start(f32[32,1,128,128]{3,2,1,0:T(8,128)} %param.22) | copy-start | bytes 6291460
  67.5 6.6 %copy-start.2 = (bf16[8,2,128,128]{3,2,1,0:T(8,128)(2,1)S(1)}, bf16[8,2,128,128]{3,2,1,0:T(8,128)(2,1)}, u32[]{:S(2)}) copy-start(bf16[8,2,128,128]{3,2,1,0:T(8,128)(2,1)} %copy-done.1) | copy-start | bytes 1572868
  70.5 12.1 %all-to-all-start.3 = ((bf16[16,4,2048]{2,1,0:T(4,128)(2,1)}), bf16[16,4,2048]{2,1,0:T(4,128)(2,1)S(1)}, u32[]{:S(2)}, u32[]{:S(2)}) async-start(bf16[16,4,2048]{2,1,0:T(4,128)(2,1)} %shard_map.179), calls=%async_computation.3 | async-start | bytes 524288 | tf_op jit(solution)/shard_map/all_to_all | solution.py:34

commit v3 on v2

--- a/solution.py
+++ b/solution.py
@@ -57,7 +57,7 @@
 
 def start_kernel(
     tok, gain, ids, wts, mask, mig, states, out, parcel,
-    tok_v, gain_v, ids_v, wts_v, mask_v, mig_s, picked, loaded, sems, row_sems,
+    tok_v, gain_v, ids_v, wts_v, mask_v, mig_s, loaded, sems, row_sems,
 ):
     groups = parcel.shape[0]
     rows = states.shape[0]
@@ -71,18 +71,15 @@
     row_copies = []
     for o in range(1, groups):
         base = ((group + o) % groups) * rows
-        spot = (CAP + 1) * o
-        for slot in range(CAP):
-            picked[spot + slot] = 0
-        count = jnp.int32(0)
+        ahead, behind = jnp.int32(0), jnp.int32(0)
         for i in range(rows):
-            old = mig_s[base + i]
-            picked[spot + jnp.minimum(count, CAP)] = old & (rows - 1)
-            count = count + ((old >> bits) == group).astype(jnp.int32)
-        for slot in range(CAP):
+            up, down = mig_s[base + i], mig_s[base + rows - 1 - i]
+            ahead = jnp.where((down >> bits) == group, down, ahead)
+            behind = jnp.where((up >> bits) == group, up, behind)
+        for slot, old in enumerate((ahead, behind)):
             k = (o - 1) * CAP + slot
             copy = pltpu.make_async_copy(
-                states.at[picked[spot + slot]], loaded.at[k], row_sems.at[k]
+                states.at[old & (rows - 1)], loaded.at[k], row_sems.at[k]
             )
             copy.start()
             row_copies.append(copy)
@@ -130,14 +127,14 @@
 
 
 def heads_kernel(
-    own_v, other_v, w_other_v, moved, log_rate, bias, w_own, w_vz, w_ab, head_gain, w_out, mig,
+    p0, p1, p2, p3, p4, p5, p6, p7, w_other_v, moved, log_rate, bias, w_own, w_vz, w_ab, head_gain, w_out, mig,
     states, tok, post_gain, *refs
 ):
-    part_own, part_other, k_out, w_rows, decay_out, comb_out = refs[:6]
+    part_own, part_other, k_out, w_rows, decay_out, comb_out, keep = refs[:7]
     (
         w_own_v, w_vz_v, w_ab_v, lr_v, bias_v, gain_v, w_out_v, mig_s, begin, tok_v, post_v,
         kq, ks, qs, q_all, v_all, z_all, d_all, b_all, m_all, h_all, dest, filled, sems,
-    ) = refs[6:]
+    ) = refs[7:]
     rows = states.shape[0]
     dim = states.shape[1]
     total = rows * STEPS
@@ -146,15 +143,19 @@
         sems, (w_own, w_own_v), (w_vz, w_vz_v),
         (w_ab, w_ab_v), (log_rate, lr_v), (bias, bias_v), (mig, mig_s), (states, begin),
         (head_gain, gain_v), (w_out, w_out_v), (tok, tok_v), (post_gain, post_v),
-    )
-    for copy in copies[:5]:
+        (moved, keep),
+    )
+    pieces = (p0, p1, p2, p3, p4, p5, p6, p7)
+    x = jnp.concatenate([piece[:, :width] for piece in pieces], axis=0)
+    extra = jnp.concatenate([piece[:, width:] for piece in pieces], axis=0).astype(F32)
+    live = extra[:, EXTRA - 1 :]
+    second = jnp.dot(x, w_other_v[...], preferred_element_type=F32)
+    copies[0].wait()
+    first = jnp.dot(x, w_own_v[...], preferred_element_type=F32)
+    copies[1].wait()
+    vz = jnp.dot(x, w_vz_v[...], preferred_element_type=F32)
+    for copy in copies[2:5]:
         copy.wait()
-    x = jnp.concatenate([own_v[:, :width], other_v[:, :width]], axis=0)
-    extra = jnp.concatenate([own_v[:, width:], other_v[:, width:]], axis=0).astype(F32)
-    live = extra[:, EXTRA - 1 :]
-    first = jnp.dot(x, w_own_v[...], preferred_element_type=F32)
-    second = jnp.dot(x, w_other_v[...], preferred_element_type=F32)
-    vz = jnp.dot(x, w_vz_v[...], preferred_element_type=F32)
     ab = lax.dot_general(
         x, w_ab_v[...], (((1,), (1,)), ((), ())), preferred_element_type=F32
     )
@@ -325,8 +326,7 @@
         scratch=[
             vm((STEPS, width), BF16), vm((1, width), F32), vm((STEPS, top), jnp.int32),
             vm((STEPS, top), BF16), vm((STEPS, rows), jnp.int32),
-            pltpu.SMEM((groups * rows,), jnp.int32), pltpu.SMEM((groups * (CAP + 1),), jnp.int32),
-            vm(((groups - 1) * CAP, dim, dim), F32), dma((6,)), dma(((groups - 1) * CAP,)),
+            pltpu.SMEM((groups * rows,), jnp.int32), vm(((groups - 1) * CAP, dim, dim), F32), dma((6,)), dma(((groups - 1) * CAP,)),
         ],
         limit=60,
     )(
@@ -335,39 +335,39 @@
     )
     recv = lax.all_to_all(parcel, "dp", split_axis=0, concat_axis=0, tiled=True)
     line = jnp.concatenate([payload] + [hop(payload, m) for m in (2, 4, 6)])
-    own_in = jnp.concatenate([line] + [hop(line, m) for m in (8, 16, 24)])
-    other_in = core_swap(own_in)
+    pieces = [line] + [hop(line, m) for m in (8, 16, 24)]
+    pieces = pieces + [core_swap(piece) for piece in pieces]
 
     tall = vm((total, dim), F32)
     plan = [pltpu.SMEM((groups * CAP,), jnp.int32), pltpu.SMEM((groups,), jnp.int32)]
-    part_own, part_other, k_rows, w_rows, decay, comb = call(
+    part_own, part_other, k_rows, w_rows, decay, comb, kept = call(
         heads_kernel,
         (
             sds((peers, STEPS, width), BF16), sds((peers, STEPS, width), BF16),
             sds((total, dim), F32), sds((total, dim), F32), sds((rows, dim), F32),
-            sds((peers, 2 * STEPS, EXTRA), F32),
+            sds((peers, 2 * STEPS, EXTRA), F32), sds((groups, CAP, dim, dim), BF16),
         ),
-        [VMEM] * 4 + [HBM] * 11,
-        (VMEM,) * 6,
+        [VMEM] * 10 + [HBM] * 11,
+        (VMEM,) * 6 + (HBM,),
         scratch=[
             vm((width, dim), BF16), vm((width, 2 * dim), BF16), vm((2, width), BF16),
             pltpu.SMEM((1,), F32), pltpu.SMEM((1,), F32),
             vm((1, dim), F32), vm((dim, width), BF16), pltpu.SMEM((groups * rows,), jnp.int32),
             vm((rows, dim, dim), F32), vm((STEPS, width), BF16), vm((1, width), F32),
             vm((2 * total, dim), F32),
-        ] + [tall] * 9 + plan + [dma((11,))],
+        ] + [tall] * 9 + plan + [dma((12,))],
         flops=2 * total * width * 700,
         moved=6 << 20,
-        limit=52,
+        limit=50,
     )(
-        own_in, other_in, w_other, recv, log_rate, step_bias, query_key, value_gate, gates_proj.T,
+        *pieces, w_other, recv, log_rate, step_bias, query_key, value_gate, gates_proj.T,
         head_gain.reshape(1, dim), out_proj, migration, states, tok, post_gain.reshape(1, width),
     )
     swapped = core_swap(part_other)
+    part = (part_own.astype(F32) + swapped.astype(F32)).astype(BF16)
     up_own = expert_up.reshape(width, -1)
     down_own = expert_down.reshape(-1, width)
     hidden = down_own.shape[0]
-    part = (part_own.astype(F32) + swapped.astype(F32)).astype(BF16)
     part, up_out, down_out = lax.optimization_barrier((part, up_own, down_own))
     up_other = core_swap(up_out)
     down_other = core_swap(down_out)
@@ -381,7 +381,7 @@
         scratch=[pltpu.SMEM((groups * rows,), jnp.int32)] + plan + [dma((2,))],
         flops=2 * total * dim * dim,
         moved=5 << 20,
-    )(k_rows, w_rows, decay, migration, states, recv)
+    )(k_rows, w_rows, decay, migration, states, kept)
 
     moe, mixed = call(
         mixed_kernel,

time: 83.9 us -> 80.3 us (0.957)
  local copies, waits for them, and re-layouts: 1.69 us -> 0.05 us
  waiting for transfers between devices: 17 us -> 15.6 us
  Pallas kernels: 15.1 us -> 14 us
    ppermute x6, waiting for transfers between devices: 9.98 us -> 8.91 us  [hop(): return lax.ppermute(value, 'expert', [(i, i ^ mask) for i in range(n)])]
    pallas_call x1, Pallas kernels: 4.64 us -> 3.58 us  [body(): call(heads_kernel, (sds((peers, STEPS, width), BF16), sds((peers, STEPS,...]
    concatenate x1 -> x0, local copies, waits for them, and re-layouts: 0.85 us -> none  [body(): own_in = jnp.concatenate([line] + [hop(line, m) for m in (8, 16, 24)])]
    ppermute x5 -> x8, starting transfers between devices: 1.05 us -> 1.71 us  [core_swap(): return lax.ppermute(value, 'expert', [(i, i ^ 1) for i in range(n)])]
  transfers between devices with their start and end apart: 13 -> 16, of which waited for: 7 -> 6; matrix products, arithmetic and copies ran while one was open for 2% -> 1% of each run, Pallas kernels for 4% -> 4%
where the time goes in v3:
time: 80.3 us; the launch traced here: 79.8 us
  blocking collectives  24.1 us (30%)
  starting transfers between devices  22.9 us (29%)
  waiting for transfers between devices  15.6 us (19%)
  Pallas kernels  14 us (17%)
  between operations  2.19 us (3%)
  other arithmetic  0.92 us (1%)
    all_to_all x2, blocking collectives, exchange(): lax.all_to_all(chunks, 'expert', split_axis=0, concat_axis=0, tiled=True,...  24.1 us
    ppermute x6, starting transfers between devices, hop(): return lax.ppermute(value, 'expert', [(i, i ^ mask) for i in range(n)])  8.97 us
    ppermute x6, waiting for transfers between devices, hop(): return lax.ppermute(value, 'expert', [(i, i ^ mask) for i in range(n)])  8.91 us
    all_to_all x1, starting transfers between devices, body(): recv = lax.all_to_all(parcel, 'dp', split_axis=0, concat_axis=0, tiled=True)  8.58 us
    all_to_all x1, waiting for transfers between devices, exchange(): lax.all_to_all(chunks, 'expert', split_axis=0, concat_axis=0, tiled=True,...  5.49 us
    all_to_all x1, starting transfers between devices, exchange(): lax.all_to_all(chunks, 'expert', split_axis=0, concat_axis=0, tiled=True,...  3.68 us
    pallas_call x1, Pallas kernels, body(): call(heads_kernel, (sds((peers, STEPS, width), BF16), sds((peers, STEPS,...  3.58 us
    pallas_call x1, Pallas kernels, body(): call(start_kernel, (sds((STEPS, width + EXTRA), BF16), sds((groups, CAP,...  3.52 us
  transfers between devices with their start and end apart: 16, of which 6 were waited for; matrix products, arithmetic and copies ran while one was open for 1% of the time, Pallas kernels for 4%

profile of v3, /device:TPU:32, one launch (start us, length us, event | category | flops | bytes accessed | tf_op | source)
XLA Modules:
  0.0 79.8 jit_solution(2013878826446369533)
XLA Ops:
  0.7 3.5 %shard_map.176 = (bf16[4,2176]{1,0:T(4,128)(2,1)}, bf16[8,2,128,128]{3,2,1,0:T(8,128)(2,1)}) custom-call(bf16[4,2048]{1,0:T(4,128)(2,1)} %bitcast.21, f32[1,2048]{1,0:T(1,128)} %bitcast.28, s32[4,10]{1,0:T(4,128)} %bitcast.29, bf16[4,10]{1,0:T(4,128)(2,1)} %bitcast.30, s32[4,32]{1,0:T(4,128)} %mask.1, s32[256]{0:T(256)} %mig.5, f32[32,128,128]{2,1,0:T(8,128)} %bitcast.14), custom_call_target="tpu_custom_call" | custom-call | tf_op jit(solution)/shard_map/pallas_call | solution.py:321
  4.2 8.6 %all-to-all-start = ((bf16[8,2,128,128]{3,2,1,0:T(8,128)(2,1)}), bf16[8,2,128,128]{3,2,1,0:T(8,128)(2,1)S(1)}, u32[]{:S(2)}, u32[]{:S(2)}) async-start(bf16[8,2,128,128]{3,2,1,0:T(8,128)(2,1)} %get-tuple-element.17), calls=%async_computation | async-start | bytes 1048576 | tf_op jit(solution)/shard_map/all_to_all | solution.py:336
  12.8 3.1 %collective-permute-start.2 = (bf16[4,2176]{1,0:T(4,128)(2,1)}, bf16[4,2176]{1,0:T(4,128)(2,1)S(1)}, u32[]{:S(2)}, u32[]{:S(2)}) collective-permute-start(bf16[4,2176]{1,0:T(4,128)(2,1)} %get-tuple-element.16), channel_id=1, source_target_pairs={{0,6},{1,7},{2,4},{3,5},{4,2},{5,3},{6,0},{7,1},{8,14},{9,15},{10,... | collective-permute-start | bytes 52232 | tf_op jit(solution)/shard_map/ppermute | solution.py:28
  15.9 0.6 collective-permute-start.1
  17.0 1.1 %collective-permute-done.2 = bf16[4,2176]{1,0:T(4,128)(2,1)S(1)} collective-permute-done((bf16[4,2176]{1,0:T(4,128)(2,1)}, bf16[4,2176]{1,0:T(4,128)(2,1)S(1)}, u32[]{:S(2)}, u32[]{:S(2)}) %collective-permute-start.2) | collective-permute-done | bytes 17440 | tf_op jit(solution)/shard_map/ppermute | solution.py:28
  18.1 3.3 %collective-permute-done.1 = bf16[4,2176]{1,0:T(4,128)(2,1)S(1)} collective-permute-done((bf16[4,2176]{1,0:T(4,128)(2,1)}, bf16[4,2176]{1,0:T(4,128)(2,1)S(1)}, u32[]{:S(2)}, u32[]{:S(2)}) %collective-permute-start.1) | collective-permute-done | bytes 17440 | tf_op jit(solution)/shard_map/ppermute | solution.py:28
  21.4 0.8 pad_maximum_fusion.p0
  22.2 1.6 %collective-permute-start.3 = (bf16[16,2176]{1,0:T(8,128)(2,1)S(1)}, bf16[16,2176]{1,0:T(8,128)(2,1)S(1)}, u32[]{:S(2)}, u32[]{:S(2)}) collective-permute-start(bf16[16,2176]{1,0:T(8,128)(2,1)S(1)} %pad_maximum_fusion.p0), channel_id=1, source_target_pairs={{0,8},{1,9},{2,10},{3,11},{4,12},{5,13},{6,14},{7,15},{8,0},{9,1},... | collective-permute-start | bytes 208904 | tf_op jit(solution)/shard_map/ppermute | solution.py:28
  23.7 2.7 %collective-permute-start.4 = (bf16[16,2176]{1,0:T(8,128)(2,1)S(1)}, bf16[16,2176]{1,0:T(8,128)(2,1)S(1)}, u32[]{:S(2)}, u32[]{:S(2)}) collective-permute-start(bf16[16,2176]{1,0:T(8,128)(2,1)S(1)} %pad_maximum_fusion.p0), channel_id=1, source_target_pairs={{0,16},{1,17},{2,18},{3,19},{4,20},{5,21},{6,22},{7,23},{8,24},{9,... | collective-permute-start | bytes 208904 | tf_op jit(solution)/shard_map/ppermute | solution.py:28
  26.5 0.5 collective-permute-start.5
  27.0 0.5 collective-permute-start.7
  27.5 2.1 %collective-permute-done.4.p2 = bf16[16,2176]{1,0:T(8,128)(2,1)S(1)} collective-permute-done((bf16[16,2176]{1,0:T(8,128)(2,1)S(1)}, bf16[16,2176]{1,0:T(8,128)(2,1)S(1)}, u32[]{:S(2)}, u32[]{:S(2)}) %collective-permute-start.4) | collective-permute-done | bytes 69664 | tf_op jit(solution)/shard_map/ppermute | solution.py:28
  29.6 2.4 %collective-permute-done.5.p3 = bf16[16,2176]{1,0:T(8,128)(2,1)S(1)} collective-permute-done((bf16[16,2176]{1,0:T(8,128)(2,1)S(1)}, bf16[16,2176]{1,0:T(8,128)(2,1)S(1)}, u32[]{:S(2)}, u32[]{:S(2)}) %collective-permute-start.5) | collective-permute-done | bytes 69664 | tf_op jit(solution)/shard_map/ppermute | solution.py:28
  33.4 3.6 %shard_map.177 = (bf16[16,4,2048]{2,1,0:T(4,128)(2,1)S(1)}, bf16[16,4,2048]{2,1,0:T(4,128)(2,1)S(1)}, f32[128,128]{1,0:T(8,128)S(1)}, f32[128,128]{1,0:T(8,128)S...) custom-call(bf16[16,2176]{1,0:T(8,128)(2,1)S(1)} %pad_maximum_fusion.p0, ...), custom_call_target="tpu_custom_call" | custom-call | flops 367001600 | bytes 6291456 | tf_op jit(solution)/shard_map/pallas_call | solution.py:343
  37.0 0.6 collective-permute-start.11
  37.6 1.2 %collective-permute-done.11 = bf16[16,4,2048]{2,1,0:T(4,128)(2,1)S(1)} collective-permute-done((bf16[16,4,2048]{2,1,0:T(4,128)(2,1)S(1)}, bf16[16,4,2048]{2,1,0:T(4,128)(2,1)S(1)}, u32[]{:S(2)}, u32[]{:S(2)}) %collective-permute-start.11) | collective-permute-done | bytes 262176 | tf_op jit(solution)/shard_map/ppermute | solution.py:23
  39.0 0.5 collective-permute-start.12
  39.6 12.2 %all_to_all.20.got = bf16[16,4,2048]{2,1,0:T(4,128)(2,1)S(1)} all-to-all(bf16[16,4,2048]{2,1,0:T(4,128)(2,1)S(1)} %add_convert_fusion), channel_id=1, replica_groups={{0,2,4,6,8,10,12,14,16,18,20,22,24,26,28,30},{1,3,5,7,9,11,13,15,17,19,..., dimensions={0} | all-to-all | bytes 524288 | tf_op jit(solution)/shard_map/all_to_all | solution.py:34
  52.0 11.9 %all_to_all.21.rows_in = bf16[16,4,2048]{2,1,0:T(4,128)(2,1)S(1)} all-to-all(bf16[16,4,2048]{2,1,0:T(4,128)(2,1)S(1)} %get-tuple-element.21), channel_id=1, replica_groups={{0,2,4,6,8,10,12,14,16,18,20,22,24,26,28,30},{1,3,5,7,9,11,13,15,17,19,..., dimensions={0} | all-to-all | bytes 524288 | tf_op jit(solution)/shard_map/all_to_all | solution.py:34
  63.9 3.0 %shard_map.179 = bf16[16,4,2048]{2,1,0:T(4,128)(2,1)} custom-call(bf16[16,4,2048]{2,1,0:T(4,128)(2,1)S(1)} %all_to_all.21.rows_in, f32[16,8,128]{2,1,0:T(8,128)S(1)} %get-tuple-element.22.packed, bf16[2048,512]{1,0:T(8,128)(2,1)S(1)} %bitcast.18, bf16[2048,512]{1,0:T(8,128)(2,1)S(1)} %collective-permute-done.12.up_other, bf16[256,2048]{1,0:T(8,128)(2,1)S(1)} %bitcast.20, ...), custom_call_target="tpu_custom_call" | custom-call | flops 536870912 | bytes 7340032 | tf_op jit(solution)/shard_map/pallas_call | solution.py:393
  66.9 3.7 %all-to-all-start.3 = ((bf16[16,4,2048]{2,1,0:T(4,128)(2,1)}), bf16[16,4,2048]{2,1,0:T(4,128)(2,1)S(1)}, u32[]{:S(2)}, u32[]{:S(2)}) async-start(bf16[16,4,2048]{2,1,0:T(4,128)(2,1)} %shard_map.179), calls=%async_computation.3 | async-start | bytes 524288 | tf_op jit(solution)/shard_map/all_to_all | solution.py:34
  70.6 3.0 %shard_map.181 = f32[32,128,128]{2,1,0:T(8,128)} custom-call(f32[128,128]{1,0:T(8,128)S(1)} %get-tuple-element.26.k_in, f32[128,128]{1,0:T(8,128)S(1)} %get-tuple-element.27.w_rows, f32[32,128]{1,0:T(8,128)S(1)} %get-tuple-element.28.decay, s32[256]{0:T(256)S(1)} %copy-done.6, f32[32,128,128]{2,1,0:T(8,128)S(1)} %bitcast.16, ...), custom_call_target="tpu_custom_call" | custom-call | flops 4194304 | bytes 5242880 | tf_op jit(solution)/shard_map/pallas_call | solution.py:376
  73.6 5.5 %all-to-all-done.3.got = bf16[16,4,2048]{2,1,0:T(4,128)(2,1)S(1)} async-done(((bf16[16,4,2048]{2,1,0:T(4,128)(2,1)}), bf16[16,4,2048]{2,1,0:T(4,128)(2,1)S(1)}, u32[]{:S(2)}, u32[]{:S(2)}) %all-to-all-start.3) | async-done | bytes 262176 | tf_op jit(solution)/shard_map/all_to_all | solution.py:34
  79.1 0.7 shard_map.180
  (38 shorter events, 1.1 us)
Async XLA Ops:
  0.6 32.7 %copy-start.5 = (bf16[4,1,2048]{2,0,1:T(4,128)(2,1)S(1)}, bf16[4,1,2048]{2,0,1:T(4,128)(2,1)}, u32[]{:S(2)}) copy-start(bf16[4,1,2048]{2,0,1:T(4,128)(2,1)} %param.17) | copy-start | bytes 49156
  0.6 32.7 %copy-start.6 = (s32[256]{0:T(256)S(1)}, s32[256]{0:T(256)}, u32[]{:S(2)}) copy-start(s32[256]{0:T(256)} %mig.5) | copy-start | bytes 3076
  0.7 12.2 %copy-start.3 = (bf16[2048,128]{1,0:T(8,128)(2,1)S(1)}, bf16[2048,128]{1,0:T(8,128)(2,1)}, u32[]{:S(2)}) copy-start(bf16[2048,128]{1,0:T(8,128)(2,1)} %w_own.1) | copy-start | bytes 1572868
  0.7 32.7 %copy-start.7 = (bf16[2048,2]{0,1:T(2,128)(2,1)S(1)}, bf16[2048,2]{0,1:T(2,128)(2,1)}, u32[]{:S(2)}) copy-start(bf16[2048,2]{0,1:T(2,128)(2,1)} %param.26) | copy-start | bytes 24580
  0.7 32.7 %copy-start.9 = (f32[128]{0:T(128)S(1)}, f32[128]{0:T(128)}, u32[]{:S(2)}) copy-start(f32[128]{0:T(128)} %param.29) | copy-start | bytes 1540
  0.7 32.7 %copy-start.4 = (bf16[128,2048]{1,0:T(8,128)(2,1)S(1)}, bf16[128,2048]{1,0:T(8,128)(2,1)}, u32[]{:S(2)}) copy-start(bf16[128,2048]{1,0:T(8,128)(2,1)} %w_out.1) | copy-start | bytes 1572868
  0.7 32.7 %copy-start.8 = (f32[2048]{0:T(1024)S(1)}, f32[2048]{0:T(1024)}, u32[]{:S(2)}) copy-start(f32[2048]{0:T(1024)} %param.31) | copy-start | bytes 24580
  4.2 29.1 %all-to-all-start = ((bf16[8,2,128,128]{3,2,1,0:T(8,128)(2,1)}), bf16[8,2,128,128]{3,2,1,0:T(8,128)(2,1)S(1)}, u32[]{:S(2)}, u32[]{:S(2)}) async-start(bf16[8,2,128,128]{3,2,1,0:T(8,128)(2,1)} %get-tuple-element.17), calls=%async_computation | async-start | bytes 1048576 | tf_op jit(solution)/shard_map/all_to_all | solution.py:336
  12.8 20.5 %collective-permute-start.10 = (bf16[2048,128]{1,0:T(8,128)(2,1)S(1)}, bf16[2048,128]{1,0:T(8,128)(2,1)S(1)}, u32[]{:S(2)}, u32[]{:S(2)}) collective-permute-start(bf16[2048,128]{1,0:T(8,128)(2,1)S(1)} %copy-done.3), channel_id=1, source_target_pairs={{0,1},{1,0},{2,3},{3,2},{4,5},{5,4},{6,7},{7,6},{8,9},{9,8},{10,11... | collective-permute-start | bytes 1572872 | tf_op jit(solution)/shard_map/ppermute | solution.py:23
  12.8 5.3 %collective-permute-start.2 = (bf16[4,2176]{1,0:T(4,128)(2,1)}, bf16[4,2176]{1,0:T(4,128)(2,1)S(1)}, u32[]{:S(2)}, u32[]{:S(2)}) collective-permute-start(bf16[4,2176]{1,0:T(4,128)(2,1)} %get-tuple-element.16), channel_id=1, source_target_pairs={{0,6},{1,7},{2,4},{3,5},{4,2},{5,3},{6,0},{7,1},{8,14},{9,15},{10,... | collective-permute-start | bytes 52232 | tf_op jit(solution)/shard_map/ppermute | solution.py:28
  15.9 5.5 %collective-permute-start.1 = (bf16[4,2176]{1,0:T(4,128)(2,1)}, bf16[4,2176]{1,0:T(4,128)(2,1)S(1)}, u32[]{:S(2)}, u32[]{:S(2)}) collective-permute-start(bf16[4,2176]{1,0:T(4,128)(2,1)} %get-tuple-element.16), channel_id=1, source_target_pairs={{0,4},{1,5},{2,6},{3,7},{4,0},{5,1},{6,2},{7,3},{8,12},{9,13},{10,... | collective-permute-start | bytes 52232 | tf_op jit(solution)/shard_map/ppermute | solution.py:28
  16.6 4.8 %collective-permute-start = (bf16[4,2176]{1,0:T(4,128)(2,1)}, bf16[4,2176]{1,0:T(4,128)(2,1)S(1)}, u32[]{:S(2)}, u32[]{:S(2)}) collective-permute-start(bf16[4,2176]{1,0:T(4,128)(2,1)} %get-tuple-element.16), channel_id=1, source_target_pairs={{0,2},{1,3},{2,0},{3,1},{4,6},{5,7},{6,4},{7,5},{8,10},{9,11},{10,... | collective-permute-start | bytes 52232 | tf_op jit(solution)/shard_map/ppermute | solution.py:28
  22.2 4.8 %collective-permute-start.3 = (bf16[16,2176]{1,0:T(8,128)(2,1)S(1)}, bf16[16,2176]{1,0:T(8,128)(2,1)S(1)}, u32[]{:S(2)}, u32[]{:S(2)}) collective-permute-start(bf16[16,2176]{1,0:T(8,128)(2,1)S(1)} %pad_maximum_fusion.p0), channel_id=1, source_target_pairs={{0,8},{1,9},{2,10},{3,11},{4,12},{5,13},{6,14},{7,15},{8,0},{9,1},... | collective-permute-start | bytes 208904 | tf_op jit(solution)/shard_map/ppermute | solution.py:28
  23.7 5.9 %collective-permute-start.4 = (bf16[16,2176]{1,0:T(8,128)(2,1)S(1)}, bf16[16,2176]{1,0:T(8,128)(2,1)S(1)}, u32[]{:S(2)}, u32[]{:S(2)}) collective-permute-start(bf16[16,2176]{1,0:T(8,128)(2,1)S(1)} %pad_maximum_fusion.p0), channel_id=1, source_target_pairs={{0,16},{1,17},{2,18},{3,19},{4,20},{5,21},{6,22},{7,23},{8,24},{9,... | collective-permute-start | bytes 208904 | tf_op jit(solution)/shard_map/ppermute | solution.py:28
  26.5 5.5 %collective-permute-start.5 = (bf16[16,2176]{1,0:T(8,128)(2,1)S(1)}, bf16[16,2176]{1,0:T(8,128)(2,1)S(1)}, u32[]{:S(2)}, u32[]{:S(2)}) collective-permute-start(bf16[16,2176]{1,0:T(8,128)(2,1)S(1)} %pad_maximum_fusion.p0), channel_id=1, source_target_pairs={{0,24},{1,25},{2,26},{3,27},{4,28},{5,29},{6,30},{7,31},{8,16},{9,... | collective-permute-start | bytes 208904 | tf_op jit(solution)/shard_map/ppermute | solution.py:28
  26.9 6.3 %collective-permute-start.6 = (bf16[16,2176]{1,0:T(8,128)(2,1)S(1)}, bf16[16,2176]{1,0:T(8,128)(2,1)S(1)}, u32[]{:S(2)}, u32[]{:S(2)}) collective-permute-start(bf16[16,2176]{1,0:T(8,128)(2,1)S(1)} %pad_maximum_fusion.p0), channel_id=1, source_target_pairs={{0,1},{1,0},{2,3},{3,2},{4,5},{5,4},{6,7},{7,6},{8,9},{9,8},{10,11... | collective-permute-start | bytes 208904 | tf_op jit(solution)/shard_map/ppermute | solution.py:23
  27.0 6.4 %collective-permute-start.7 = (bf16[16,2176]{1,0:T(8,128)(2,1)S(1)}, bf16[16,2176]{1,0:T(8,128)(2,1)S(1)}, u32[]{:S(2)}, u32[]{:S(2)}) collective-permute-start(bf16[16,2176]{1,0:T(8,128)(2,1)S(1)} %collective-permute-done.3.p1), channel_id=1, source_target_pairs={{0,1},{1,0},{2,3},{3,2},{4,5},{5,4},{6,7},{7,6},{8,9},{9,8},{10,11... | collective-permute-start | bytes 208904 | tf_op jit(solution)/shard_map/ppermute | solution.py:23
  29.6 3.7 %collective-permute-start.8 = (bf16[16,2176]{1,0:T(8,128)(2,1)S(1)}, bf16[16,2176]{1,0:T(8,128)(2,1)S(1)}, u32[]{:S(2)}, u32[]{:S(2)}) collective-permute-start(bf16[16,2176]{1,0:T(8,128)(2,1)S(1)} %collective-permute-done.4.p2), channel_id=1, source_target_pairs={{0,1},{1,0},{2,3},{3,2},{4,5},{5,4},{6,7},{7,6},{8,9},{9,8},{10,11... | collective-permute-start | bytes 208904 | tf_op jit(solution)/shard_map/ppermute | solution.py:23
  32.0 1.3 %collective-permute-start.9 = (bf16[16,2176]{1,0:T(8,128)(2,1)S(1)}, bf16[16,2176]{1,0:T(8,128)(2,1)S(1)}, u32[]{:S(2)}, u32[]{:S(2)}) collective-permute-start(bf16[16,2176]{1,0:T(8,128)(2,1)S(1)} %collective-permute-done.5.p3), channel_id=1, source_target_pairs={{0,1},{1,0},{2,3},{3,2},{4,5},{5,4},{6,7},{7,6},{8,9},{9,8},{10,11... | collective-permute-start | bytes 208904 | tf_op jit(solution)/shard_map/ppermute | solution.py:23
  37.0 1.8 %collective-permute-start.11 = (bf16[16,4,2048]{2,1,0:T(4,128)(2,1)S(1)}, bf16[16,4,2048]{2,1,0:T(4,128)(2,1)S(1)}, u32[]{:S(2)}, u32[]{:S(2)}) collective-permute-start(bf16[16,4,2048]{2,1,0:T(4,128)(2,1)S(1)} %get-tuple-element.19), channel_id=1, source_target_pairs={{0,1},{1,0},{2,3},{3,2},{4,5},{5,4},{6,7},{7,6},{8,9},{9,8},{10,11... | collective-permute-start | bytes 786440 | tf_op jit(solution)/shard_map/ppermute | solution.py:23
  39.0 25.0 %collective-permute-start.12 = (bf16[2048,512]{1,0:T(8,128)(2,1)S(1)}, bf16[2048,512]{1,0:T(8,128)(2,1)S(1)}, u32[]{:S(2)}, u32[]{:S(2)}) collective-permute-start(bf16[2048,512]{1,0:T(8,128)(2,1)S(1)} %bitcast.17), channel_id=1, source_target_pairs={{0,1},{1,0},{2,3},{3,2},{4,5},{5,4},{6,7},{7,6},{8,9},{9,8},{10,11... | collective-permute-start | bytes 6291464 | tf_op jit(solution)/shard_map/ppermute | solution.py:23
  39.4 24.5 %collective-permute-start.13 = (bf16[256,2048]{1,0:T(8,128)(2,1)S(1)}, bf16[256,2048]{1,0:T(8,128)(2,1)S(1)}, u32[]{:S(2)}, u32[]{:S(2)}) collective-permute-start(bf16[256,2048]{1,0:T(8,128)(2,1)S(1)} %bitcast.19), channel_id=1, source_target_pairs={{0,1},{1,0},{2,3},{3,2},{4,5},{5,4},{6,7},{7,6},{8,9},{9,8},{10,11... | collective-permute-start | bytes 3145736 | tf_op jit(solution)/shard_map/ppermute | solution.py:23
  63.9 6.7 %copy-start = (f32[32,1,128,128]{3,2,1,0:T(8,128)S(1)}, f32[32,1,128,128]{3,2,1,0:T(8,128)}, u32[]{:S(2)}) copy-start(f32[32,1,128,128]{3,2,1,0:T(8,128)} %param.22) | copy-start | bytes 6291460
  66.9 12.2 %all-to-all-start.3 = ((bf16[16,4,2048]{2,1,0:T(4,128)(2,1)}), bf16[16,4,2048]{2,1,0:T(4,128)(2,1)S(1)}, u32[]{:S(2)}, u32[]{:S(2)}) async-start(bf16[16,4,2048]{2,1,0:T(4,128)(2,1)} %shard_map.179), calls=%async_computation.3 | async-start | bytes 524288 | tf_op jit(solution)/shard_map/all_to_all | solution.py:34
  (2 other events, 11.5 us)

commit v4 on v3

--- a/solution.py
+++ b/solution.py
@@ -57,7 +57,7 @@
 
 def start_kernel(
     tok, gain, ids, wts, mask, mig, states, out, parcel,
-    tok_v, gain_v, ids_v, wts_v, mask_v, mig_s, loaded, sems, row_sems,
+    tok_v, gain_v, ids_v, wts_v, mask_v, mig_v, loaded, sems, row_sems,
 ):
     groups = parcel.shape[0]
     rows = states.shape[0]
@@ -65,21 +65,23 @@
     group = lax.axis_index("dp")
     me = lax.axis_index("expert")
     copies = fetch(
-        sems, (mig, mig_s), (tok, tok_v), (gain, gain_v), (ids, ids_v), (wts, wts_v), (mask, mask_v)
+        sems, (mig, mig_v), (tok, tok_v), (gain, gain_v), (ids, ids_v), (wts, wts_v), (mask, mask_v)
     )
     copies[0].wait()
+    old = mig_v[...]
+    lane = lax.broadcasted_iota(jnp.int32, old.shape, 0) * old.shape[1]
+    lane = lane + lax.broadcasted_iota(jnp.int32, old.shape, 1)
+    ours = (old >> bits) == group
+    key = ((lane & (rows - 1)) * rows + (old & (rows - 1))).astype(F32)
     row_copies = []
-    for o in range(1, groups):
-        base = ((group + o) % groups) * rows
-        ahead, behind = jnp.int32(0), jnp.int32(0)
-        for i in range(rows):
-            up, down = mig_s[base + i], mig_s[base + rows - 1 - i]
-            ahead = jnp.where((down >> bits) == group, down, ahead)
-            behind = jnp.where((up >> bits) == group, up, behind)
-        for slot, old in enumerate((ahead, behind)):
-            k = (o - 1) * CAP + slot
+    for g in range(groups):
+        mask = ours & ((lane >> bits) == g)
+        ahead = jnp.min(jnp.where(mask, key, float(rows * rows - 1)))
+        behind = jnp.max(jnp.where(mask, key, 0.0))
+        for slot, found in enumerate((ahead, behind)):
+            k = g * CAP + slot
             copy = pltpu.make_async_copy(
-                states.at[old & (rows - 1)], loaded.at[k], row_sems.at[k]
+                states.at[found.astype(jnp.int32) & (rows - 1)], loaded.at[k], row_sems.at[k]
             )
             copy.start()
             row_copies.append(copy)
@@ -101,10 +103,9 @@
     width = x.shape[1]
     out[:, :width] = normed
     out[:, width:] = comb
-    parcel[group] = jnp.zeros(parcel.shape[1:], BF16)
     for k, copy in enumerate(row_copies):
         copy.wait()
-        parcel[(group + k // CAP + 1) % groups, k % CAP] = loaded[k].astype(BF16)
+        parcel[k // CAP, k % CAP] = loaded[k].astype(BF16)
 
 
 def place_moved(mig_s, filled, dest, begin, moved):
@@ -127,12 +128,12 @@
 
 
 def heads_kernel(
-    p0, p1, p2, p3, p4, p5, p6, p7, w_other_v, moved, log_rate, bias, w_own, w_vz, w_ab, head_gain, w_out, mig,
+    p0, p1, p2, p3, p4, p5, p6, p7, w_other_v, moved, rates, w_own, w_vz, w_ab, head_gain, w_out, mig,
     states, tok, post_gain, *refs
 ):
     part_own, part_other, k_out, w_rows, decay_out, comb_out, keep = refs[:7]
     (
-        w_own_v, w_vz_v, w_ab_v, lr_v, bias_v, gain_v, w_out_v, mig_s, begin, tok_v, post_v,
+        w_own_v, w_vz_v, w_ab_v, rates_v, gain_v, w_out_v, mig_s, begin, tok_v, post_v,
         kq, ks, qs, q_all, v_all, z_all, d_all, b_all, m_all, h_all, dest, filled, sems,
     ) = refs[7:]
     rows = states.shape[0]
@@ -141,7 +142,7 @@
     width = w_own.shape[0]
     copies = fetch(
         sems, (w_own, w_own_v), (w_vz, w_vz_v),
-        (w_ab, w_ab_v), (log_rate, lr_v), (bias, bias_v), (mig, mig_s), (states, begin),
+        (w_ab, w_ab_v), (rates, rates_v), (mig, mig_s), (states, begin),
         (head_gain, gain_v), (w_out, w_out_v), (tok, tok_v), (post_gain, post_v),
         (moved, keep),
     )
@@ -154,7 +155,7 @@
     first = jnp.dot(x, w_own_v[...], preferred_element_type=F32)
     copies[1].wait()
     vz = jnp.dot(x, w_vz_v[...], preferred_element_type=F32)
-    for copy in copies[2:5]:
+    for copy in copies[2:4]:
         copy.wait()
     ab = lax.dot_general(
         x, w_ab_v[...], (((1,), (1,)), ((), ())), preferred_element_type=F32
@@ -166,8 +167,8 @@
     q = q * (lax.rsqrt(jnp.sum(q * q, axis=-1, keepdims=True) + EPS) * dim**-0.5)
     k = k * lax.rsqrt(jnp.sum(k * k, axis=-1, keepdims=True) + EPS)
     beta = jax.nn.sigmoid(ab[:, 1:2])
-    rate = jnp.exp(jnp.full((total, 1), lr_v[0], F32))
-    drive = ab[:, 0:1] + bias_v[0]
+    rate = jnp.exp(rates_v[0:1, 0:1])
+    drive = ab[:, 0:1] + rates_v[1:2, 0:1]
     soft = jnp.maximum(drive, 0.0) + jnp.log1p(jnp.exp(-jnp.abs(drive)))
     decay = jnp.exp(-rate * soft)
     wide = (total, dim)
@@ -181,7 +182,7 @@
     for s in range(rows):
         kq[8 * s : 8 * s + 4] = k[4 * s : 4 * s + 4]
         kq[8 * s + 4 : 8 * s + 8] = q[4 * s : 4 * s + 4]
-    for copy in copies[5:]:
+    for copy in copies[4:]:
         copy.wait()
     place_moved(mig_s, filled, dest, begin, moved)
     for s in range(rows):
@@ -258,34 +259,23 @@
 
 
 def expert_kernel(
-    rows_in, packed, up_own, up_other, down_own, down_other, out,
-    extra_v, up_own_v, up_other_v, down_own_v, down_other_v, sems,
+    rows_in, extra_v, up_own_v, up_other_v, down_own_v, down_other_v, out
 ):
     half = rows_in.shape[0] * STEPS
-    copies = fetch(
-        sems, (up_own, up_own_v), (down_own, down_own_v), (up_other, up_other_v),
-        (down_other, down_other_v), (packed, extra_v),
-    )
     me = lax.axis_index("expert")
     partner = me + 1 - 2 * (me % 2)
-    copies[4].wait()
     extra = extra_v[...]
     gain = jnp.concatenate([extra[j, STEPS : STEPS + 1] for j in range(extra.shape[0])], axis=1)
     x = (rows_in[...].astype(F32).reshape(half, -1) * gain).astype(BF16)
     comb = extra[:, :STEPS].reshape(half, EXTRA)
     lane = lax.broadcasted_iota(jnp.int32, comb.shape, 1)
     total = None
-    for index, up, down, up_copy, down_copy in (
-        (me, up_own_v, down_own_v, copies[0], copies[1]),
-        (partner, up_other_v, down_other_v, copies[2], copies[3]),
-    ):
+    for index, up, down in ((me, up_own_v, down_own_v), (partner, up_other_v, down_other_v)):
         hidden = down.shape[0]
-        up_copy.wait()
         proj = jnp.dot(x, up[...], preferred_element_type=F32)
         g, u = proj[:, :hidden], proj[:, hidden:]
         act = (g * jax.nn.sigmoid(g) * u).astype(BF16)
         weight = jnp.sum(jnp.where(lane == index, comb, 0.0), axis=-1, keepdims=True)
-        down_copy.wait()
         result = weight * jnp.dot(act, down[...], preferred_element_type=F32)
         total = result if total is None else total + result
     total = total.astype(BF16)
@@ -326,15 +316,18 @@
         scratch=[
             vm((STEPS, width), BF16), vm((1, width), F32), vm((STEPS, top), jnp.int32),
             vm((STEPS, top), BF16), vm((STEPS, rows), jnp.int32),
-            pltpu.SMEM((groups * rows,), jnp.int32), vm(((groups - 1) * CAP, dim, dim), F32), dma((6,)), dma(((groups - 1) * CAP,)),
+            vm((groups * rows // 128, 128), jnp.int32), vm((groups * CAP, dim, dim), F32),
+            dma((6,)), dma((groups * CAP,)),
         ],
         limit=60,
     )(
         tok, in_gain.reshape(1, width), route_ids.reshape(STEPS, top),
-        route_weights.reshape(STEPS, top), active_mask, migration, states,
+        route_weights.reshape(STEPS, top), active_mask, migration.reshape(-1, 128), states,
     )
     recv = lax.all_to_all(parcel, "dp", split_axis=0, concat_axis=0, tiled=True)
     line = jnp.concatenate([payload] + [hop(payload, m) for m in (2, 4, 6)])
+    rates = jnp.broadcast_to(jnp.concatenate([log_rate, step_bias])[:, None], (2, dim))
+    line, rates = lax.optimization_barrier((line, rates))
     pieces = [line] + [hop(line, m) for m in (8, 16, 24)]
     pieces = pieces + [core_swap(piece) for piece in pieces]
 
@@ -347,20 +340,20 @@
             sds((total, dim), F32), sds((total, dim), F32), sds((rows, dim), F32),
             sds((peers, 2 * STEPS, EXTRA), F32), sds((groups, CAP, dim, dim), BF16),
         ),
-        [VMEM] * 10 + [HBM] * 11,
+        [VMEM] * 10 + [ANY] + [HBM] * 9,
         (VMEM,) * 6 + (HBM,),
         scratch=[
             vm((width, dim), BF16), vm((width, 2 * dim), BF16), vm((2, width), BF16),
-            pltpu.SMEM((1,), F32), pltpu.SMEM((1,), F32),
+            vm((2, dim), F32),
             vm((1, dim), F32), vm((dim, width), BF16), pltpu.SMEM((groups * rows,), jnp.int32),
             vm((rows, dim, dim), F32), vm((STEPS, width), BF16), vm((1, width), F32),
             vm((2 * total, dim), F32),
-        ] + [tall] * 9 + plan + [dma((12,))],
+        ] + [tall] * 9 + plan + [dma((11,))],
         flops=2 * total * width * 700,
         moved=6 << 20,
         limit=50,
     )(
-        *pieces, w_other, recv, log_rate, step_bias, query_key, value_gate, gates_proj.T,
+        *pieces, w_other, recv, rates, query_key, value_gate, gates_proj.T,
         head_gain.reshape(1, dim), out_proj, migration, states, tok, post_gain.reshape(1, width),
     )
     swapped = core_swap(part_other)
@@ -393,14 +386,11 @@
     served = call(
         expert_kernel,
         sds((peers, STEPS, width), BF16),
-        [VMEM, ANY] + [HBM] * 4,
+        [VMEM] * 6,
         VMEM,
-        scratch=[
-            vm((peers, 2 * STEPS, EXTRA), F32), vm((width, 2 * hidden), BF16), vm((width, 2 * hidden), BF16),
-            vm((hidden, width), BF16), vm((hidden, width), BF16), dma((5,)),
-        ],
         flops=1 << 29,
         moved=7 << 20,
+        limit=10,
     )(moe_rows, comb, up_own, up_other, down_own, down_other)
     back = exchange(served)
     out = call(sum_kernel, sds((STEPS, width), BF16), [VMEM] * 2, VMEM)(back, mixed)

time: 80.3 us -> 78.5 us (0.978)
  Pallas kernels: 14 us -> 12.7 us
    ppermute x8, waiting for transfers between devices: 1.18 us -> 2.63 us  [core_swap(): return lax.ppermute(value, 'expert', [(i, i ^ 1) for i in range(n)])]
    ppermute x6, waiting for transfers between devices: 8.91 us -> 7.53 us  [hop(): return lax.ppermute(value, 'expert', [(i, i ^ mask) for i in range(n)])]
    pallas_call x1, Pallas kernels: 2.96 us -> 2.09 us  [body(): call(expert_kernel, sds((peers, STEPS, width), BF16), [VMEM] * 6, VMEM, f...]
where the time goes in v4:
time: 78.5 us; the launch traced here: 78.1 us
  blocking collectives  24.1 us (31%)
  starting transfers between devices  22.4 us (29%)
  waiting for transfers between devices  15.7 us (20%)
  Pallas kernels  12.7 us (16%)
  between operations  2.14 us (3%)
  other arithmetic  0.99 us (1%)
    all_to_all x2, blocking collectives, exchange(): lax.all_to_all(chunks, 'expert', split_axis=0, concat_axis=0, tiled=True,...  24.1 us
    ppermute x6, starting transfers between devices, hop(): return lax.ppermute(value, 'expert', [(i, i ^ mask) for i in range(n)])  8.82 us
    all_to_all x1, starting transfers between devices, body(): recv = lax.all_to_all(parcel, 'dp', split_axis=0, concat_axis=0, tiled=True)  8.57 us
    ppermute x6, waiting for transfers between devices, hop(): return lax.ppermute(value, 'expert', [(i, i ^ mask) for i in range(n)])  7.53 us
    all_to_all x1, waiting for transfers between devices, exchange(): lax.all_to_all(chunks, 'expert', split_axis=0, concat_axis=0, tiled=True,...  5.49 us
    all_to_all x1, starting transfers between devices, exchange(): lax.all_to_all(chunks, 'expert', split_axis=0, concat_axis=0, tiled=True,...  3.63 us
    pallas_call x1, Pallas kernels, body(): call(heads_kernel, (sds((peers, STEPS, width), BF16), sds((peers, STEPS,...  3.56 us
    pallas_call x1, Pallas kernels, body(): call(start_kernel, (sds((STEPS, width + EXTRA), BF16), sds((groups, CAP,...  3.12 us
  transfers between devices with their start and end apart: 16, of which 6 were waited for; matrix products, arithmetic and copies ran while one was open for 1% of the time, Pallas kernels for 4%

profile of v4, /device:TPU:32, one launch (start us, length us, event | category | flops | bytes accessed | tf_op | source)
XLA Modules:
  0.0 78.1 jit_solution(16973168388980949957)
XLA Ops:
  0.7 3.1 %shard_map.176 = (bf16[4,2176]{1,0:T(4,128)(2,1)}, bf16[8,2,128,128]{3,2,1,0:T(8,128)(2,1)}) custom-call(bf16[4,2048]{1,0:T(4,128)(2,1)} %bitcast.22, f32[1,2048]{1,0:T(1,128)} %bitcast.30, s32[4,10]{1,0:T(4,128)} %bitcast.31, bf16[4,10]{1,0:T(4,128)(2,1)} %bitcast.32, s32[4,32]{1,0:T(4,128)} %mask.1, s32[2,128]{1,0:T(2,128)} %bitcast.24, ...), custom_call_target="tpu_custom_call" | custom-call | tf_op jit(solution)/shard_map/pallas_call | solution.py:311
  3.8 8.6 %all-to-all-start = ((bf16[8,2,128,128]{3,2,1,0:T(8,128)(2,1)}), bf16[8,2,128,128]{3,2,1,0:T(8,128)(2,1)S(1)}, u32[]{:S(2)}, u32[]{:S(2)}) async-start(bf16[8,2,128,128]{3,2,1,0:T(8,128)(2,1)} %get-tuple-element.20), calls=%async_computation | async-start | bytes 1048576 | tf_op jit(solution)/shard_map/all_to_all | solution.py:327
  12.4 3.0 %collective-permute-start.2 = (bf16[4,2176]{1,0:T(4,128)(2,1)}, bf16[4,2176]{1,0:T(4,128)(2,1)S(1)}, u32[]{:S(2)}, u32[]{:S(2)}) collective-permute-start(bf16[4,2176]{1,0:T(4,128)(2,1)} %get-tuple-element.18), channel_id=1, source_target_pairs={{0,6},{1,7},{2,4},{3,5},{4,2},{5,3},{6,0},{7,1},{8,14},{9,15},{10,... | collective-permute-start | bytes 52232 | tf_op jit(solution)/shard_map/ppermute | solution.py:28
  15.4 0.6 collective-permute-start.1
  16.1 0.5 collective-permute-start
  17.9 3.0 %collective-permute-done.1 = bf16[4,2176]{1,0:T(4,128)(2,1)S(1)} collective-permute-done((bf16[4,2176]{1,0:T(4,128)(2,1)}, bf16[4,2176]{1,0:T(4,128)(2,1)S(1)}, u32[]{:S(2)}, u32[]{:S(2)}) %collective-permute-start.1) | collective-permute-done | bytes 17440 | tf_op jit(solution)/shard_map/ppermute | solution.py:28
  20.9 0.8 pad_maximum_fusion.p0
  21.7 1.5 %collective-permute-start.3 = (bf16[16,2176]{1,0:T(8,128)(2,1)S(1)}, bf16[16,2176]{1,0:T(8,128)(2,1)S(1)}, u32[]{:S(2)}, u32[]{:S(2)}) collective-permute-start(bf16[16,2176]{1,0:T(8,128)(2,1)S(1)} %pad_maximum_fusion.p0), channel_id=1, source_target_pairs={{0,8},{1,9},{2,10},{3,11},{4,12},{5,13},{6,14},{7,15},{8,0},{9,1},... | collective-permute-start | bytes 208904 | tf_op jit(solution)/shard_map/ppermute | solution.py:28
  23.3 2.7 %collective-permute-start.4 = (bf16[16,2176]{1,0:T(8,128)(2,1)S(1)}, bf16[16,2176]{1,0:T(8,128)(2,1)S(1)}, u32[]{:S(2)}, u32[]{:S(2)}) collective-permute-start(bf16[16,2176]{1,0:T(8,128)(2,1)S(1)} %pad_maximum_fusion.p0), channel_id=1, source_target_pairs={{0,16},{1,17},{2,18},{3,19},{4,20},{5,21},{6,22},{7,23},{8,24},{9,... | collective-permute-start | bytes 208904 | tf_op jit(solution)/shard_map/ppermute | solution.py:28
  26.0 0.5 collective-permute-start.5
  26.5 0.5 collective-permute-start.7
  27.0 2.1 %collective-permute-done.4.p2 = bf16[16,2176]{1,0:T(8,128)(2,1)S(1)} collective-permute-done((bf16[16,2176]{1,0:T(8,128)(2,1)S(1)}, bf16[16,2176]{1,0:T(8,128)(2,1)S(1)}, u32[]{:S(2)}, u32[]{:S(2)}) %collective-permute-start.4) | collective-permute-done | bytes 69664 | tf_op jit(solution)/shard_map/ppermute | solution.py:28
  29.1 2.4 %collective-permute-done.5.p3 = bf16[16,2176]{1,0:T(8,128)(2,1)S(1)} collective-permute-done((bf16[16,2176]{1,0:T(8,128)(2,1)S(1)}, bf16[16,2176]{1,0:T(8,128)(2,1)S(1)}, u32[]{:S(2)}, u32[]{:S(2)}) %collective-permute-start.5) | collective-permute-done | bytes 69664 | tf_op jit(solution)/shard_map/ppermute | solution.py:28
  31.5 1.2 %collective-permute-done.9.p7 = bf16[16,2176]{1,0:T(8,128)(2,1)S(1)} collective-permute-done((bf16[16,2176]{1,0:T(8,128)(2,1)S(1)}, bf16[16,2176]{1,0:T(8,128)(2,1)S(1)}, u32[]{:S(2)}, u32[]{:S(2)}) %collective-permute-start.9) | collective-permute-done | bytes 69664 | tf_op jit(solution)/shard_map/ppermute | solution.py:23
  32.9 3.6 %shard_map.177 = (bf16[16,4,2048]{2,1,0:T(4,128)(2,1)S(1)}, bf16[16,4,2048]{2,1,0:T(4,128)(2,1)S(1)}, f32[128,128]{1,0:T(8,128)S(1)}, f32[128,128]{1,0:T(8,128)S...) custom-call(bf16[16,2176]{1,0:T(8,128)(2,1)S(1)} %pad_maximum_fusion.p0, ...), custom_call_target="tpu_custom_call" | custom-call | flops 367001600 | bytes 6291456 | tf_op jit(solution)/shard_map/pallas_call | solution.py:336
  36.7 1.4 %collective-permute-done.11 = bf16[16,4,2048]{2,1,0:T(4,128)(2,1)S(1)} collective-permute-done((bf16[16,4,2048]{2,1,0:T(4,128)(2,1)S(1)}, bf16[16,4,2048]{2,1,0:T(4,128)(2,1)S(1)}, u32[]{:S(2)}, u32[]{:S(2)}) %collective-permute-start.11) | collective-permute-done | bytes 262176 | tf_op jit(solution)/shard_map/ppermute | solution.py:23
  38.4 0.4 collective-permute-start.13
  38.8 12.2 %all_to_all.20.got = bf16[16,4,2048]{2,1,0:T(4,128)(2,1)S(1)} all-to-all(bf16[16,4,2048]{2,1,0:T(4,128)(2,1)S(1)} %add_convert_fusion), channel_id=1, replica_groups={{0,2,4,6,8,10,12,14,16,18,20,22,24,26,28,30},{1,3,5,7,9,11,13,15,17,19,..., dimensions={0} | all-to-all | bytes 524288 | tf_op jit(solution)/shard_map/all_to_all | solution.py:34
  51.2 11.9 %all_to_all.21.rows_in = bf16[16,4,2048]{2,1,0:T(4,128)(2,1)S(1)} all-to-all(bf16[16,4,2048]{2,1,0:T(4,128)(2,1)S(1)} %get-tuple-element.25), channel_id=1, replica_groups={{0,2,4,6,8,10,12,14,16,18,20,22,24,26,28,30},{1,3,5,7,9,11,13,15,17,19,..., dimensions={0} | all-to-all | bytes 524288 | tf_op jit(solution)/shard_map/all_to_all | solution.py:34
  63.2 2.1 %shard_map.179 = bf16[16,4,2048]{2,1,0:T(4,128)(2,1)} custom-call(bf16[16,4,2048]{2,1,0:T(4,128)(2,1)S(1)} %all_to_all.21.rows_in, f32[16,8,128]{2,1,0:T(8,128)S(1)} %get-tuple-element.26.extra_v, bf16[2048,512]{1,0:T(8,128)(2,1)S(1)} %bitcast.19, bf16[2048,512]{1,0:T(8,128)(2,1)S(1)} %collective-permute-done.12.up_other_v, bf16[256,2048]{1,0:T(8,128)(2,1)S(1)} %bitcast.21, ...), custom_call_target="tpu_custom_call" | custom-call | flops 536870912 | bytes 7340032 | tf_op jit(solution)/shard_map/pallas_call | solution.py:386
  65.2 3.6 %all-to-all-start.3 = ((bf16[16,4,2048]{2,1,0:T(4,128)(2,1)}), bf16[16,4,2048]{2,1,0:T(4,128)(2,1)S(1)}, u32[]{:S(2)}, u32[]{:S(2)}) async-start(bf16[16,4,2048]{2,1,0:T(4,128)(2,1)} %shard_map.179), calls=%async_computation.3 | async-start | bytes 524288 | tf_op jit(solution)/shard_map/all_to_all | solution.py:34
  68.9 3.0 %shard_map.181 = f32[32,128,128]{2,1,0:T(8,128)} custom-call(f32[128,128]{1,0:T(8,128)S(1)} %get-tuple-element.30.k_in, f32[128,128]{1,0:T(8,128)S(1)} %get-tuple-element.31.w_rows, f32[32,128]{1,0:T(8,128)S(1)} %get-tuple-element.32.decay, s32[256]{0:T(256)S(1)} %copy-done.6, f32[32,128,128]{2,1,0:T(8,128)S(1)} %bitcast.17, ...), custom_call_target="tpu_custom_call" | custom-call | flops 4194304 | bytes 5242880 | tf_op jit(solution)/shard_map/pallas_call | solution.py:369
  71.9 5.5 %all-to-all-done.3.got = bf16[16,4,2048]{2,1,0:T(4,128)(2,1)S(1)} async-done(((bf16[16,4,2048]{2,1,0:T(4,128)(2,1)}), bf16[16,4,2048]{2,1,0:T(4,128)(2,1)S(1)}, u32[]{:S(2)}, u32[]{:S(2)}) %all-to-all-start.3) | async-done | bytes 262176 | tf_op jit(solution)/shard_map/all_to_all | solution.py:34
  77.4 0.7 shard_map.180
  (40 shorter events, 1.1 us)
Async XLA Ops:
  0.6 32.1 %copy-start.5 = (bf16[4,1,2048]{2,0,1:T(4,128)(2,1)S(1)}, bf16[4,1,2048]{2,0,1:T(4,128)(2,1)}, u32[]{:S(2)}) copy-start(bf16[4,1,2048]{2,0,1:T(4,128)(2,1)} %param.17) | copy-start | bytes 49156
  0.6 32.1 %copy-start.6 = (s32[256]{0:T(256)S(1)}, s32[256]{0:T(256)}, u32[]{:S(2)}) copy-start(s32[256]{0:T(256)} %mig.3) | copy-start | bytes 3076
  0.7 15.9 %copy-start.3 = (bf16[2048,128]{1,0:T(8,128)(2,1)S(1)}, bf16[2048,128]{1,0:T(8,128)(2,1)}, u32[]{:S(2)}) copy-start(bf16[2048,128]{1,0:T(8,128)(2,1)} %w_own.1) | copy-start | bytes 1572868
  0.7 32.1 %copy-start.7 = (bf16[2048,2]{0,1:T(2,128)(2,1)S(1)}, bf16[2048,2]{0,1:T(2,128)(2,1)}, u32[]{:S(2)}) copy-start(bf16[2048,2]{0,1:T(2,128)(2,1)} %param.26) | copy-start | bytes 24580
  0.7 32.1 %copy-start.9 = (f32[128]{0:T(128)S(1)}, f32[128]{0:T(128)}, u32[]{:S(2)}) copy-start(f32[128]{0:T(128)} %param.29) | copy-start | bytes 1540
  0.7 32.1 %copy-start.4 = (bf16[128,2048]{1,0:T(8,128)(2,1)S(1)}, bf16[128,2048]{1,0:T(8,128)(2,1)}, u32[]{:S(2)}) copy-start(bf16[128,2048]{1,0:T(8,128)(2,1)} %w_out.1) | copy-start | bytes 1572868
  0.7 32.1 %copy-start.8 = (f32[2048]{0:T(1024)S(1)}, f32[2048]{0:T(1024)}, u32[]{:S(2)}) copy-start(f32[2048]{0:T(1024)} %param.31) | copy-start | bytes 24580
  3.8 28.9 %all-to-all-start = ((bf16[8,2,128,128]{3,2,1,0:T(8,128)(2,1)}), bf16[8,2,128,128]{3,2,1,0:T(8,128)(2,1)S(1)}, u32[]{:S(2)}, u32[]{:S(2)}) async-start(bf16[8,2,128,128]{3,2,1,0:T(8,128)(2,1)} %get-tuple-element.20), calls=%async_computation | async-start | bytes 1048576 | tf_op jit(solution)/shard_map/all_to_all | solution.py:327
  12.4 5.5 %collective-permute-start.2 = (bf16[4,2176]{1,0:T(4,128)(2,1)}, bf16[4,2176]{1,0:T(4,128)(2,1)S(1)}, u32[]{:S(2)}, u32[]{:S(2)}) collective-permute-start(bf16[4,2176]{1,0:T(4,128)(2,1)} %get-tuple-element.18), channel_id=1, source_target_pairs={{0,6},{1,7},{2,4},{3,5},{4,2},{5,3},{6,0},{7,1},{8,14},{9,15},{10,... | collective-permute-start | bytes 52232 | tf_op jit(solution)/shard_map/ppermute | solution.py:28
  15.4 5.5 %collective-permute-start.1 = (bf16[4,2176]{1,0:T(4,128)(2,1)}, bf16[4,2176]{1,0:T(4,128)(2,1)S(1)}, u32[]{:S(2)}, u32[]{:S(2)}) collective-permute-start(bf16[4,2176]{1,0:T(4,128)(2,1)} %get-tuple-element.18), channel_id=1, source_target_pairs={{0,4},{1,5},{2,6},{3,7},{4,0},{5,1},{6,2},{7,3},{8,12},{9,13},{10,... | collective-permute-start | bytes 52232 | tf_op jit(solution)/shard_map/ppermute | solution.py:28
  16.1 4.8 %collective-permute-start = (bf16[4,2176]{1,0:T(4,128)(2,1)}, bf16[4,2176]{1,0:T(4,128)(2,1)S(1)}, u32[]{:S(2)}, u32[]{:S(2)}) collective-permute-start(bf16[4,2176]{1,0:T(4,128)(2,1)} %get-tuple-element.18), channel_id=1, source_target_pairs={{0,2},{1,3},{2,0},{3,1},{4,6},{5,7},{6,4},{7,5},{8,10},{9,11},{10,... | collective-permute-start | bytes 52232 | tf_op jit(solution)/shard_map/ppermute | solution.py:28
  16.5 16.3 %collective-permute-start.10 = (bf16[2048,128]{1,0:T(8,128)(2,1)S(1)}, bf16[2048,128]{1,0:T(8,128)(2,1)S(1)}, u32[]{:S(2)}, u32[]{:S(2)}) collective-permute-start(bf16[2048,128]{1,0:T(8,128)(2,1)S(1)} %copy-done.3), channel_id=1, source_target_pairs={{0,1},{1,0},{2,3},{3,2},{4,5},{5,4},{6,7},{7,6},{8,9},{9,8},{10,11... | collective-permute-start | bytes 1572872 | tf_op jit(solution)/shard_map/ppermute | solution.py:23
  21.7 4.7 %collective-permute-start.3 = (bf16[16,2176]{1,0:T(8,128)(2,1)S(1)}, bf16[16,2176]{1,0:T(8,128)(2,1)S(1)}, u32[]{:S(2)}, u32[]{:S(2)}) collective-permute-start(bf16[16,2176]{1,0:T(8,128)(2,1)S(1)} %pad_maximum_fusion.p0), channel_id=1, source_target_pairs={{0,8},{1,9},{2,10},{3,11},{4,12},{5,13},{6,14},{7,15},{8,0},{9,1},... | collective-permute-start | bytes 208904 | tf_op jit(solution)/shard_map/ppermute | solution.py:28
  23.3 5.8 %collective-permute-start.4 = (bf16[16,2176]{1,0:T(8,128)(2,1)S(1)}, bf16[16,2176]{1,0:T(8,128)(2,1)S(1)}, u32[]{:S(2)}, u32[]{:S(2)}) collective-permute-start(bf16[16,2176]{1,0:T(8,128)(2,1)S(1)} %pad_maximum_fusion.p0), channel_id=1, source_target_pairs={{0,16},{1,17},{2,18},{3,19},{4,20},{5,21},{6,22},{7,23},{8,24},{9,... | collective-permute-start | bytes 208904 | tf_op jit(solution)/shard_map/ppermute | solution.py:28
  26.0 5.5 %collective-permute-start.5 = (bf16[16,2176]{1,0:T(8,128)(2,1)S(1)}, bf16[16,2176]{1,0:T(8,128)(2,1)S(1)}, u32[]{:S(2)}, u32[]{:S(2)}) collective-permute-start(bf16[16,2176]{1,0:T(8,128)(2,1)S(1)} %pad_maximum_fusion.p0), channel_id=1, source_target_pairs={{0,24},{1,25},{2,26},{3,27},{4,28},{5,29},{6,30},{7,31},{8,16},{9,... | collective-permute-start | bytes 208904 | tf_op jit(solution)/shard_map/ppermute | solution.py:28
  26.5 5.0 %collective-permute-start.6 = (bf16[16,2176]{1,0:T(8,128)(2,1)S(1)}, bf16[16,2176]{1,0:T(8,128)(2,1)S(1)}, u32[]{:S(2)}, u32[]{:S(2)}) collective-permute-start(bf16[16,2176]{1,0:T(8,128)(2,1)S(1)} %pad_maximum_fusion.p0), channel_id=1, source_target_pairs={{0,1},{1,0},{2,3},{3,2},{4,5},{5,4},{6,7},{7,6},{8,9},{9,8},{10,11... | collective-permute-start | bytes 208904 | tf_op jit(solution)/shard_map/ppermute | solution.py:23
  26.5 5.0 %collective-permute-start.7 = (bf16[16,2176]{1,0:T(8,128)(2,1)S(1)}, bf16[16,2176]{1,0:T(8,128)(2,1)S(1)}, u32[]{:S(2)}, u32[]{:S(2)}) collective-permute-start(bf16[16,2176]{1,0:T(8,128)(2,1)S(1)} %collective-permute-done.3.p1), channel_id=1, source_target_pairs={{0,1},{1,0},{2,3},{3,2},{4,5},{5,4},{6,7},{7,6},{8,9},{9,8},{10,11... | collective-permute-start | bytes 208904 | tf_op jit(solution)/shard_map/ppermute | solution.py:23
  29.1 2.5 %collective-permute-start.8 = (bf16[16,2176]{1,0:T(8,128)(2,1)S(1)}, bf16[16,2176]{1,0:T(8,128)(2,1)S(1)}, u32[]{:S(2)}, u32[]{:S(2)}) collective-permute-start(bf16[16,2176]{1,0:T(8,128)(2,1)S(1)} %collective-permute-done.4.p2), channel_id=1, source_target_pairs={{0,1},{1,0},{2,3},{3,2},{4,5},{5,4},{6,7},{7,6},{8,9},{9,8},{10,11... | collective-permute-start | bytes 208904 | tf_op jit(solution)/shard_map/ppermute | solution.py:23
  31.5 1.3 %collective-permute-start.9 = (bf16[16,2176]{1,0:T(8,128)(2,1)S(1)}, bf16[16,2176]{1,0:T(8,128)(2,1)S(1)}, u32[]{:S(2)}, u32[]{:S(2)}) collective-permute-start(bf16[16,2176]{1,0:T(8,128)(2,1)S(1)} %collective-permute-done.5.p3), channel_id=1, source_target_pairs={{0,1},{1,0},{2,3},{3,2},{4,5},{5,4},{6,7},{7,6},{8,9},{9,8},{10,11... | collective-permute-start | bytes 208904 | tf_op jit(solution)/shard_map/ppermute | solution.py:23
  36.4 1.6 %collective-permute-start.11 = (bf16[16,4,2048]{2,1,0:T(4,128)(2,1)S(1)}, bf16[16,4,2048]{2,1,0:T(4,128)(2,1)S(1)}, u32[]{:S(2)}, u32[]{:S(2)}) collective-permute-start(bf16[16,4,2048]{2,1,0:T(4,128)(2,1)S(1)} %get-tuple-element.23), channel_id=1, source_target_pairs={{0,1},{1,0},{2,3},{3,2},{4,5},{5,4},{6,7},{7,6},{8,9},{9,8},{10,11... | collective-permute-start | bytes 786440 | tf_op jit(solution)/shard_map/ppermute | solution.py:23
  38.2 25.0 %collective-permute-start.12 = (bf16[2048,512]{1,0:T(8,128)(2,1)S(1)}, bf16[2048,512]{1,0:T(8,128)(2,1)S(1)}, u32[]{:S(2)}, u32[]{:S(2)}) collective-permute-start(bf16[2048,512]{1,0:T(8,128)(2,1)S(1)} %bitcast.18), channel_id=1, source_target_pairs={{0,1},{1,0},{2,3},{3,2},{4,5},{5,4},{6,7},{7,6},{8,9},{9,8},{10,11... | collective-permute-start | bytes 6291464 | tf_op jit(solution)/shard_map/ppermute | solution.py:23
  38.4 24.7 %collective-permute-start.13 = (bf16[256,2048]{1,0:T(8,128)(2,1)S(1)}, bf16[256,2048]{1,0:T(8,128)(2,1)S(1)}, u32[]{:S(2)}, u32[]{:S(2)}) collective-permute-start(bf16[256,2048]{1,0:T(8,128)(2,1)S(1)} %bitcast.20), channel_id=1, source_target_pairs={{0,1},{1,0},{2,3},{3,2},{4,5},{5,4},{6,7},{7,6},{8,9},{9,8},{10,11... | collective-permute-start | bytes 3145736 | tf_op jit(solution)/shard_map/ppermute | solution.py:23
  63.2 5.7 %copy-start = (f32[32,1,128,128]{3,2,1,0:T(8,128)S(1)}, f32[32,1,128,128]{3,2,1,0:T(8,128)}, u32[]{:S(2)}) copy-start(f32[32,1,128,128]{3,2,1,0:T(8,128)} %param.22) | copy-start | bytes 6291460
  65.2 12.1 %all-to-all-start.3 = ((bf16[16,4,2048]{2,1,0:T(4,128)(2,1)}), bf16[16,4,2048]{2,1,0:T(4,128)(2,1)S(1)}, u32[]{:S(2)}, u32[]{:S(2)}) async-start(bf16[16,4,2048]{2,1,0:T(4,128)(2,1)} %shard_map.179), calls=%async_computation.3 | async-start | bytes 524288 | tf_op jit(solution)/shard_map/all_to_all | solution.py:34
  (2 other events, 11.0 us)

commit v5 on v4

--- a/solution.py
+++ b/solution.py
@@ -73,18 +73,17 @@
     lane = lane + lax.broadcasted_iota(jnp.int32, old.shape, 1)
     ours = (old >> bits) == group
     key = ((lane & (rows - 1)) * rows + (old & (rows - 1))).astype(F32)
-    row_copies = []
+    found = []
     for g in range(groups):
         mask = ours & ((lane >> bits) == g)
-        ahead = jnp.min(jnp.where(mask, key, float(rows * rows - 1)))
-        behind = jnp.max(jnp.where(mask, key, 0.0))
-        for slot, found in enumerate((ahead, behind)):
-            k = g * CAP + slot
-            copy = pltpu.make_async_copy(
-                states.at[found.astype(jnp.int32) & (rows - 1)], loaded.at[k], row_sems.at[k]
-            )
-            copy.start()
-            row_copies.append(copy)
+        found.append(jnp.min(jnp.where(mask, key, float(rows * rows - 1))))
+        found.append(jnp.max(jnp.where(mask, key, 0.0)))
+    picked = [value.astype(jnp.int32) & (rows - 1) for value in found]
+    row_copies = []
+    for k, row in enumerate(picked):
+        copy = pltpu.make_async_copy(states.at[row], loaded.at[k], row_sems.at[k])
+        copy.start()
+        row_copies.append(copy)
     for copy in copies[1:]:
         copy.wait()
     x = tok_v[...].astype(F32)
@@ -128,20 +127,20 @@
 
 
 def heads_kernel(
-    p0, p1, p2, p3, p4, p5, p6, p7, w_other_v, moved, rates, w_own, w_vz, w_ab, head_gain, w_out, mig,
+    p0, p1, p2, p3, p4, p5, p6, p7, w_other_v, moved, w_own_v, rates, w_vz, w_ab, head_gain, w_out, mig,
     states, tok, post_gain, *refs
 ):
     part_own, part_other, k_out, w_rows, decay_out, comb_out, keep = refs[:7]
     (
-        w_own_v, w_vz_v, w_ab_v, rates_v, gain_v, w_out_v, mig_s, begin, tok_v, post_v,
+        w_vz_v, w_ab_v, rates_v, gain_v, w_out_v, mig_s, begin, tok_v, post_v,
         kq, ks, qs, q_all, v_all, z_all, d_all, b_all, m_all, h_all, dest, filled, sems,
     ) = refs[7:]
     rows = states.shape[0]
     dim = states.shape[1]
     total = rows * STEPS
-    width = w_own.shape[0]
+    width = w_own_v.shape[0]
     copies = fetch(
-        sems, (w_own, w_own_v), (w_vz, w_vz_v),
+        sems, (w_vz, w_vz_v),
         (w_ab, w_ab_v), (rates, rates_v), (mig, mig_s), (states, begin),
         (head_gain, gain_v), (w_out, w_out_v), (tok, tok_v), (post_gain, post_v),
         (moved, keep),
@@ -151,11 +150,10 @@
     extra = jnp.concatenate([piece[:, width:] for piece in pieces], axis=0).astype(F32)
     live = extra[:, EXTRA - 1 :]
     second = jnp.dot(x, w_other_v[...], preferred_element_type=F32)
+    first = jnp.dot(x, w_own_v[...], preferred_element_type=F32)
     copies[0].wait()
-    first = jnp.dot(x, w_own_v[...], preferred_element_type=F32)
-    copies[1].wait()
     vz = jnp.dot(x, w_vz_v[...], preferred_element_type=F32)
-    for copy in copies[2:4]:
+    for copy in copies[1:3]:
         copy.wait()
     ab = lax.dot_general(
         x, w_ab_v[...], (((1,), (1,)), ((), ())), preferred_element_type=F32
@@ -182,7 +180,7 @@
     for s in range(rows):
         kq[8 * s : 8 * s + 4] = k[4 * s : 4 * s + 4]
         kq[8 * s + 4 : 8 * s + 8] = q[4 * s : 4 * s + 4]
-    for copy in copies[4:]:
+    for copy in copies[3:]:
         copy.wait()
     place_moved(mig_s, filled, dest, begin, moved)
     for s in range(rows):
@@ -310,7 +308,7 @@
     w_other = core_swap(query_key)
     payload, parcel = call(
         start_kernel,
-        (sds((STEPS, width + EXTRA), BF16), sds((groups, CAP, dim, dim), BF16)),
+        (vm((STEPS, width + EXTRA), BF16), vm((groups, CAP, dim, dim), BF16)),
         [HBM] * 7,
         (VMEM, VMEM),
         scratch=[
@@ -327,8 +325,8 @@
     recv = lax.all_to_all(parcel, "dp", split_axis=0, concat_axis=0, tiled=True)
     line = jnp.concatenate([payload] + [hop(payload, m) for m in (2, 4, 6)])
     rates = jnp.broadcast_to(jnp.concatenate([log_rate, step_bias])[:, None], (2, dim))
-    line, rates = lax.optimization_barrier((line, rates))
     pieces = [line] + [hop(line, m) for m in (8, 16, 24)]
+    pieces[1], rates = lax.optimization_barrier((pieces[1], rates))
     pieces = pieces + [core_swap(piece) for piece in pieces]
 
     tall = vm((total, dim), F32)
@@ -340,20 +338,20 @@
             sds((total, dim), F32), sds((total, dim), F32), sds((rows, dim), F32),
             sds((peers, 2 * STEPS, EXTRA), F32), sds((groups, CAP, dim, dim), BF16),
         ),
-        [VMEM] * 10 + [ANY] + [HBM] * 9,
+        [VMEM] * 11 + [ANY] + [HBM] * 8,
         (VMEM,) * 6 + (HBM,),
         scratch=[
-            vm((width, dim), BF16), vm((width, 2 * dim), BF16), vm((2, width), BF16),
+            vm((width, 2 * dim), BF16), vm((2, width), BF16),
             vm((2, dim), F32),
             vm((1, dim), F32), vm((dim, width), BF16), pltpu.SMEM((groups * rows,), jnp.int32),
             vm((rows, dim, dim), F32), vm((STEPS, width), BF16), vm((1, width), F32),
             vm((2 * total, dim), F32),
-        ] + [tall] * 9 + plan + [dma((11,))],
+        ] + [tall] * 9 + plan + [dma((10,))],
         flops=2 * total * width * 700,
         moved=6 << 20,
         limit=50,
     )(
-        *pieces, w_other, recv, rates, query_key, value_gate, gates_proj.T,
+        *pieces, w_other, recv, query_key, rates, value_gate, gates_proj.T,
         head_gain.reshape(1, dim), out_proj, migration, states, tok, post_gain.reshape(1, width),
     )
     swapped = core_swap(part_other)
@@ -385,7 +383,7 @@
     moe_rows = exchange(moe)
     served = call(
         expert_kernel,
-        sds((peers, STEPS, width), BF16),
+        vm((peers, STEPS, width), BF16),
         [VMEM] * 6,
         VMEM,
         flops=1 << 29,

time: 78.5 us -> 77.8 us (level)
  transfers between devices with their start and end apart: 16 -> 16, of which waited for: 6 -> 6; matrix products, arithmetic and copies ran while one was open for 1% -> 0% of each run, Pallas kernels for 4% -> 4%
where the time goes in v5:
time: 77.8 us; the launch traced here: 77.2 us
  blocking collectives  24.1 us (31%)
  starting transfers between devices  22.5 us (29%)
  waiting for transfers between devices  15.3 us (20%)
  Pallas kernels  12.7 us (16%)
  between operations  2.17 us (3%)
    all_to_all x2, blocking collectives, exchange(): lax.all_to_all(chunks, 'expert', split_axis=0, concat_axis=0, tiled=True,...  24.1 us
    ppermute x6, starting transfers between devices, hop(): return lax.ppermute(value, 'expert', [(i, i ^ mask) for i in range(n)])  8.88 us
    all_to_all x1, starting transfers between devices, body(): recv = lax.all_to_all(parcel, 'dp', split_axis=0, concat_axis=0, tiled=True)  8.58 us
    ppermute x6, waiting for transfers between devices, hop(): return lax.ppermute(value, 'expert', [(i, i ^ mask) for i in range(n)])  7.23 us
    all_to_all x1, waiting for transfers between devices, exchange(): lax.all_to_all(chunks, 'expert', split_axis=0, concat_axis=0, tiled=True,...  5.48 us
    all_to_all x1, starting transfers between devices, exchange(): lax.all_to_all(chunks, 'expert', split_axis=0, concat_axis=0, tiled=True,...  3.67 us
    pallas_call x1, Pallas kernels, body(): call(heads_kernel, (sds((peers, STEPS, width), BF16), sds((peers, STEPS,...  3.52 us
    pallas_call x1, Pallas kernels, body(): call(start_kernel, (vm((STEPS, width + EXTRA), BF16), vm((groups, CAP, di...  3.12 us
  transfers between devices with their start and end apart: 16, of which 6 were waited for; matrix products, arithmetic and copies ran while one was open for 0% of the time, Pallas kernels for 4%

profile of v5, /device:TPU:32, one launch (start us, length us, event | category | flops | bytes accessed | tf_op | source)
XLA Modules:
  0.0 77.2 jit_solution(11784360083837160960)
XLA Ops:
  0.7 3.1 %shard_map.176 = (bf16[4,2176]{1,0:T(4,128)(2,1)S(1)}, bf16[8,2,128,128]{3,2,1,0:T(8,128)(2,1)}) custom-call(bf16[4,2048]{1,0:T(4,128)(2,1)} %bitcast.22, f32[1,2048]{1,0:T(1,128)} %bitcast.30, s32[4,10]{1,0:T(4,128)} %bitcast.31, bf16[4,10]{1,0:T(4,128)(2,1)} %bitcast.32, s32[4,32]{1,0:T(4,128)} %mask.1, s32[2,128]{1,0:T(2,128)} %bitcast.24, ...), custom_call_target="tpu_custom_call" | custom-call | tf_op jit(solution)/shard_map/pallas_call | solution.py:309
  3.8 8.6 %all-to-all-start = ((bf16[8,2,128,128]{3,2,1,0:T(8,128)(2,1)}), bf16[8,2,128,128]{3,2,1,0:T(8,128)(2,1)S(1)}, u32[]{:S(2)}, u32[]{:S(2)}) async-start(bf16[8,2,128,128]{3,2,1,0:T(8,128)(2,1)} %get-tuple-element.20), calls=%async_computation | async-start | bytes 1048576 | tf_op jit(solution)/shard_map/all_to_all | solution.py:325
  12.4 3.0 %collective-permute-start.2 = (bf16[4,2176]{1,0:T(4,128)(2,1)S(1)}, bf16[4,2176]{1,0:T(4,128)(2,1)S(1)}, u32[]{:S(2)}, u32[]{:S(2)}) collective-permute-start(bf16[4,2176]{1,0:T(4,128)(2,1)S(1)} %get-tuple-element.18), channel_id=1, source_target_pairs={{0,6},{1,7},{2,4},{3,5},{4,2},{5,3},{6,0},{7,1},{8,14},{9,15},{10,... | collective-permute-start | bytes 52232 | tf_op jit(solution)/shard_map/ppermute | solution.py:28
  15.4 0.6 collective-permute-start.1
  16.1 0.5 collective-permute-start
  17.8 2.9 %collective-permute-done.1 = bf16[4,2176]{1,0:T(4,128)(2,1)S(1)} collective-permute-done((bf16[4,2176]{1,0:T(4,128)(2,1)S(1)}, bf16[4,2176]{1,0:T(4,128)(2,1)S(1)}, u32[]{:S(2)}, u32[]{:S(2)}) %collective-permute-start.1) | collective-permute-done | bytes 17440 | tf_op jit(solution)/shard_map/ppermute | solution.py:28
  20.7 1.6 %collective-permute-start.3 = (bf16[16,2176]{1,0:T(8,128)(2,1)S(1)}, bf16[16,2176]{1,0:T(8,128)(2,1)S(1)}, u32[]{:S(2)}, u32[]{:S(2)}) collective-permute-start(bf16[16,2176]{1,0:T(8,128)(2,1)S(1)} %pad_maximum_fusion.p0), channel_id=1, source_target_pairs={{0,8},{1,9},{2,10},{3,11},{4,12},{5,13},{6,14},{7,15},{8,0},{9,1},... | collective-permute-start | bytes 208904 | tf_op jit(solution)/shard_map/ppermute | solution.py:28
  22.3 2.7 %collective-permute-start.4 = (bf16[16,2176]{1,0:T(8,128)(2,1)S(1)}, bf16[16,2176]{1,0:T(8,128)(2,1)S(1)}, u32[]{:S(2)}, u32[]{:S(2)}) collective-permute-start(bf16[16,2176]{1,0:T(8,128)(2,1)S(1)} %pad_maximum_fusion.p0), channel_id=1, source_target_pairs={{0,16},{1,17},{2,18},{3,19},{4,20},{5,21},{6,22},{7,23},{8,24},{9,... | collective-permute-start | bytes 208904 | tf_op jit(solution)/shard_map/ppermute | solution.py:28
  25.0 0.5 collective-permute-start.5
  25.7 0.5 collective-permute-start.7
  26.2 1.9 %collective-permute-done.4.p2 = bf16[16,2176]{1,0:T(8,128)(2,1)S(1)} collective-permute-done((bf16[16,2176]{1,0:T(8,128)(2,1)S(1)}, bf16[16,2176]{1,0:T(8,128)(2,1)S(1)}, u32[]{:S(2)}, u32[]{:S(2)}) %collective-permute-start.4) | collective-permute-done | bytes 69664 | tf_op jit(solution)/shard_map/ppermute | solution.py:28
  28.1 2.4 %collective-permute-done.5.p3 = bf16[16,2176]{1,0:T(8,128)(2,1)S(1)} collective-permute-done((bf16[16,2176]{1,0:T(8,128)(2,1)S(1)}, bf16[16,2176]{1,0:T(8,128)(2,1)S(1)}, u32[]{:S(2)}, u32[]{:S(2)}) %collective-permute-start.5) | collective-permute-done | bytes 69664 | tf_op jit(solution)/shard_map/ppermute | solution.py:28
  30.6 1.2 %collective-permute-done.9.p7 = bf16[16,2176]{1,0:T(8,128)(2,1)S(1)} collective-permute-done((bf16[16,2176]{1,0:T(8,128)(2,1)S(1)}, bf16[16,2176]{1,0:T(8,128)(2,1)S(1)}, u32[]{:S(2)}, u32[]{:S(2)}) %collective-permute-start.9) | collective-permute-done | bytes 69664 | tf_op jit(solution)/shard_map/ppermute | solution.py:23
  31.9 3.5 %shard_map.177 = (bf16[16,4,2048]{2,1,0:T(4,128)(2,1)S(1)}, bf16[16,4,2048]{2,1,0:T(4,128)(2,1)S(1)}, f32[128,128]{1,0:T(8,128)S(1)}, f32[128,128]{1,0:T(8,128)S...) custom-call(bf16[16,2176]{1,0:T(8,128)(2,1)S(1)} %pad_maximum_fusion.p0, ...), custom_call_target="tpu_custom_call" | custom-call | flops 367001600 | bytes 6291456 | tf_op jit(solution)/shard_map/pallas_call | solution.py:334
  35.7 1.4 %collective-permute-done.11 = bf16[16,4,2048]{2,1,0:T(4,128)(2,1)S(1)} collective-permute-done((bf16[16,4,2048]{2,1,0:T(4,128)(2,1)S(1)}, bf16[16,4,2048]{2,1,0:T(4,128)(2,1)S(1)}, u32[]{:S(2)}, u32[]{:S(2)}) %collective-permute-start.11) | collective-permute-done | bytes 262176 | tf_op jit(solution)/shard_map/ppermute | solution.py:23
  37.2 0.2 collective-permute-start.12
  37.5 0.4 collective-permute-start.13
  37.8 12.2 %all_to_all.20.got = bf16[16,4,2048]{2,1,0:T(4,128)(2,1)S(1)} all-to-all(bf16[16,4,2048]{2,1,0:T(4,128)(2,1)S(1)} %add_convert_fusion), channel_id=1, replica_groups={{0,2,4,6,8,10,12,14,16,18,20,22,24,26,28,30},{1,3,5,7,9,11,13,15,17,19,..., dimensions={0} | all-to-all | bytes 524288 | tf_op jit(solution)/shard_map/all_to_all | solution.py:34
  50.3 11.9 %all_to_all.21.rows_in = bf16[16,4,2048]{2,1,0:T(4,128)(2,1)S(1)} all-to-all(bf16[16,4,2048]{2,1,0:T(4,128)(2,1)S(1)} %get-tuple-element.25), channel_id=1, replica_groups={{0,2,4,6,8,10,12,14,16,18,20,22,24,26,28,30},{1,3,5,7,9,11,13,15,17,19,..., dimensions={0} | all-to-all | bytes 524288 | tf_op jit(solution)/shard_map/all_to_all | solution.py:34
  62.2 2.1 %shard_map.179 = bf16[16,4,2048]{2,1,0:T(4,128)(2,1)} custom-call(bf16[16,4,2048]{2,1,0:T(4,128)(2,1)S(1)} %all_to_all.21.rows_in, f32[16,8,128]{2,1,0:T(8,128)S(1)} %get-tuple-element.26.extra_v, bf16[2048,512]{1,0:T(8,128)(2,1)S(1)} %bitcast.19, bf16[2048,512]{1,0:T(8,128)(2,1)S(1)} %collective-permute-done.12.up_other_v, bf16[256,2048]{1,0:T(8,128)(2,1)S(1)} %bitcast.21, ...), custom_call_target="tpu_custom_call" | custom-call | flops 536870912 | bytes 7340032 | tf_op jit(solution)/shard_map/pallas_call | solution.py:384
  64.3 3.7 %all-to-all-start.3 = ((bf16[16,4,2048]{2,1,0:T(4,128)(2,1)}), bf16[16,4,2048]{2,1,0:T(4,128)(2,1)S(1)}, u32[]{:S(2)}, u32[]{:S(2)}) async-start(bf16[16,4,2048]{2,1,0:T(4,128)(2,1)} %shard_map.179), calls=%async_computation.3 | async-start | bytes 524288 | tf_op jit(solution)/shard_map/all_to_all | solution.py:34
  68.0 3.0 %shard_map.181 = f32[32,128,128]{2,1,0:T(8,128)} custom-call(f32[128,128]{1,0:T(8,128)S(1)} %get-tuple-element.30.k_in, f32[128,128]{1,0:T(8,128)S(1)} %get-tuple-element.31.w_rows, f32[32,128]{1,0:T(8,128)S(1)} %get-tuple-element.32.decay, s32[256]{0:T(256)S(1)} %copy-done.6, f32[32,128,128]{2,1,0:T(8,128)S(1)} %bitcast.17, ...), custom_call_target="tpu_custom_call" | custom-call | flops 4194304 | bytes 5242880 | tf_op jit(solution)/shard_map/pallas_call | solution.py:367
  71.0 5.5 %all-to-all-done.3.got = bf16[16,4,2048]{2,1,0:T(4,128)(2,1)S(1)} async-done(((bf16[16,4,2048]{2,1,0:T(4,128)(2,1)}), bf16[16,4,2048]{2,1,0:T(4,128)(2,1)S(1)}, u32[]{:S(2)}, u32[]{:S(2)}) %all-to-all-start.3) | async-done | bytes 262176 | tf_op jit(solution)/shard_map/all_to_all | solution.py:34
  76.5 0.7 shard_map.180
  (40 shorter events, 0.9 us)
Async XLA Ops:
  0.6 31.2 %copy-start.5 = (bf16[4,1,2048]{2,0,1:T(4,128)(2,1)S(1)}, bf16[4,1,2048]{2,0,1:T(4,128)(2,1)}, u32[]{:S(2)}) copy-start(bf16[4,1,2048]{2,0,1:T(4,128)(2,1)} %param.17) | copy-start | bytes 49156
  0.6 31.2 %copy-start.6 = (s32[256]{0:T(256)S(1)}, s32[256]{0:T(256)}, u32[]{:S(2)}) copy-start(s32[256]{0:T(256)} %mig.3) | copy-start | bytes 3076
  0.7 15.9 %copy-start.3 = (bf16[2048,128]{1,0:T(8,128)(2,1)S(1)}, bf16[2048,128]{1,0:T(8,128)(2,1)}, u32[]{:S(2)}) copy-start(bf16[2048,128]{1,0:T(8,128)(2,1)} %w_own_v.1) | copy-start | bytes 1572868
  0.7 31.2 %copy-start.7 = (bf16[2048,2]{0,1:T(2,128)(2,1)S(1)}, bf16[2048,2]{0,1:T(2,128)(2,1)}, u32[]{:S(2)}) copy-start(bf16[2048,2]{0,1:T(2,128)(2,1)} %param.26) | copy-start | bytes 24580
  0.7 31.2 %copy-start.9 = (f32[128]{0:T(128)S(1)}, f32[128]{0:T(128)}, u32[]{:S(2)}) copy-start(f32[128]{0:T(128)} %param.29) | copy-start | bytes 1540
  0.7 31.2 %copy-start.4 = (bf16[128,2048]{1,0:T(8,128)(2,1)S(1)}, bf16[128,2048]{1,0:T(8,128)(2,1)}, u32[]{:S(2)}) copy-start(bf16[128,2048]{1,0:T(8,128)(2,1)} %w_out.1) | copy-start | bytes 1572868
  0.7 31.2 %copy-start.8 = (f32[2048]{0:T(1024)S(1)}, f32[2048]{0:T(1024)}, u32[]{:S(2)}) copy-start(f32[2048]{0:T(1024)} %param.31) | copy-start | bytes 24580
  3.8 28.0 %all-to-all-start = ((bf16[8,2,128,128]{3,2,1,0:T(8,128)(2,1)}), bf16[8,2,128,128]{3,2,1,0:T(8,128)(2,1)S(1)}, u32[]{:S(2)}, u32[]{:S(2)}) async-start(bf16[8,2,128,128]{3,2,1,0:T(8,128)(2,1)} %get-tuple-element.20), calls=%async_computation | async-start | bytes 1048576 | tf_op jit(solution)/shard_map/all_to_all | solution.py:325
  12.4 5.4 %collective-permute-start.2 = (bf16[4,2176]{1,0:T(4,128)(2,1)S(1)}, bf16[4,2176]{1,0:T(4,128)(2,1)S(1)}, u32[]{:S(2)}, u32[]{:S(2)}) collective-permute-start(bf16[4,2176]{1,0:T(4,128)(2,1)S(1)} %get-tuple-element.18), channel_id=1, source_target_pairs={{0,6},{1,7},{2,4},{3,5},{4,2},{5,3},{6,0},{7,1},{8,14},{9,15},{10,... | collective-permute-start | bytes 52232 | tf_op jit(solution)/shard_map/ppermute | solution.py:28
  15.4 5.3 %collective-permute-start.1 = (bf16[4,2176]{1,0:T(4,128)(2,1)S(1)}, bf16[4,2176]{1,0:T(4,128)(2,1)S(1)}, u32[]{:S(2)}, u32[]{:S(2)}) collective-permute-start(bf16[4,2176]{1,0:T(4,128)(2,1)S(1)} %get-tuple-element.18), channel_id=1, source_target_pairs={{0,4},{1,5},{2,6},{3,7},{4,0},{5,1},{6,2},{7,3},{8,12},{9,13},{10,... | collective-permute-start | bytes 52232 | tf_op jit(solution)/shard_map/ppermute | solution.py:28
  16.1 4.6 %collective-permute-start = (bf16[4,2176]{1,0:T(4,128)(2,1)S(1)}, bf16[4,2176]{1,0:T(4,128)(2,1)S(1)}, u32[]{:S(2)}, u32[]{:S(2)}) collective-permute-start(bf16[4,2176]{1,0:T(4,128)(2,1)S(1)} %get-tuple-element.18), channel_id=1, source_target_pairs={{0,2},{1,3},{2,0},{3,1},{4,6},{5,7},{6,4},{7,5},{8,10},{9,11},{10,... | collective-permute-start | bytes 52232 | tf_op jit(solution)/shard_map/ppermute | solution.py:28
  16.5 15.3 %collective-permute-start.10 = (bf16[2048,128]{1,0:T(8,128)(2,1)S(1)}, bf16[2048,128]{1,0:T(8,128)(2,1)S(1)}, u32[]{:S(2)}, u32[]{:S(2)}) collective-permute-start(bf16[2048,128]{1,0:T(8,128)(2,1)S(1)} %copy-done.3), channel_id=1, source_target_pairs={{0,1},{1,0},{2,3},{3,2},{4,5},{5,4},{6,7},{7,6},{8,9},{9,8},{10,11... | collective-permute-start | bytes 1572872 | tf_op jit(solution)/shard_map/ppermute | solution.py:23
  20.7 4.9 %collective-permute-start.3 = (bf16[16,2176]{1,0:T(8,128)(2,1)S(1)}, bf16[16,2176]{1,0:T(8,128)(2,1)S(1)}, u32[]{:S(2)}, u32[]{:S(2)}) collective-permute-start(bf16[16,2176]{1,0:T(8,128)(2,1)S(1)} %pad_maximum_fusion.p0), channel_id=1, source_target_pairs={{0,8},{1,9},{2,10},{3,11},{4,12},{5,13},{6,14},{7,15},{8,0},{9,1},... | collective-permute-start | bytes 208904 | tf_op jit(solution)/shard_map/ppermute | solution.py:28
  22.3 5.8 %collective-permute-start.4 = (bf16[16,2176]{1,0:T(8,128)(2,1)S(1)}, bf16[16,2176]{1,0:T(8,128)(2,1)S(1)}, u32[]{:S(2)}, u32[]{:S(2)}) collective-permute-start(bf16[16,2176]{1,0:T(8,128)(2,1)S(1)} %pad_maximum_fusion.p0), channel_id=1, source_target_pairs={{0,16},{1,17},{2,18},{3,19},{4,20},{5,21},{6,22},{7,23},{8,24},{9,... | collective-permute-start | bytes 208904 | tf_op jit(solution)/shard_map/ppermute | solution.py:28
  25.0 5.5 %collective-permute-start.5 = (bf16[16,2176]{1,0:T(8,128)(2,1)S(1)}, bf16[16,2176]{1,0:T(8,128)(2,1)S(1)}, u32[]{:S(2)}, u32[]{:S(2)}) collective-permute-start(bf16[16,2176]{1,0:T(8,128)(2,1)S(1)} %pad_maximum_fusion.p0), channel_id=1, source_target_pairs={{0,24},{1,25},{2,26},{3,27},{4,28},{5,29},{6,30},{7,31},{8,16},{9,... | collective-permute-start | bytes 208904 | tf_op jit(solution)/shard_map/ppermute | solution.py:28
  25.6 5.0 %collective-permute-start.6 = (bf16[16,2176]{1,0:T(8,128)(2,1)S(1)}, bf16[16,2176]{1,0:T(8,128)(2,1)S(1)}, u32[]{:S(2)}, u32[]{:S(2)}) collective-permute-start(bf16[16,2176]{1,0:T(8,128)(2,1)S(1)} %pad_maximum_fusion.p0), channel_id=1, source_target_pairs={{0,1},{1,0},{2,3},{3,2},{4,5},{5,4},{6,7},{7,6},{8,9},{9,8},{10,11... | collective-permute-start | bytes 208904 | tf_op jit(solution)/shard_map/ppermute | solution.py:23
  25.7 4.9 %collective-permute-start.7 = (bf16[16,2176]{1,0:T(8,128)(2,1)S(1)}, bf16[16,2176]{1,0:T(8,128)(2,1)S(1)}, u32[]{:S(2)}, u32[]{:S(2)}) collective-permute-start(bf16[16,2176]{1,0:T(8,128)(2,1)S(1)} %collective-permute-done.3.p1), channel_id=1, source_target_pairs={{0,1},{1,0},{2,3},{3,2},{4,5},{5,4},{6,7},{7,6},{8,9},{9,8},{10,11... | collective-permute-start | bytes 208904 | tf_op jit(solution)/shard_map/ppermute | solution.py:23
  28.1 2.5 %collective-permute-start.8 = (bf16[16,2176]{1,0:T(8,128)(2,1)S(1)}, bf16[16,2176]{1,0:T(8,128)(2,1)S(1)}, u32[]{:S(2)}, u32[]{:S(2)}) collective-permute-start(bf16[16,2176]{1,0:T(8,128)(2,1)S(1)} %collective-permute-done.4.p2), channel_id=1, source_target_pairs={{0,1},{1,0},{2,3},{3,2},{4,5},{5,4},{6,7},{7,6},{8,9},{9,8},{10,11... | collective-permute-start | bytes 208904 | tf_op jit(solution)/shard_map/ppermute | solution.py:23
  30.6 1.3 %collective-permute-start.9 = (bf16[16,2176]{1,0:T(8,128)(2,1)S(1)}, bf16[16,2176]{1,0:T(8,128)(2,1)S(1)}, u32[]{:S(2)}, u32[]{:S(2)}) collective-permute-start(bf16[16,2176]{1,0:T(8,128)(2,1)S(1)} %collective-permute-done.5.p3), channel_id=1, source_target_pairs={{0,1},{1,0},{2,3},{3,2},{4,5},{5,4},{6,7},{7,6},{8,9},{9,8},{10,11... | collective-permute-start | bytes 208904 | tf_op jit(solution)/shard_map/ppermute | solution.py:23
  35.4 1.6 %collective-permute-start.11 = (bf16[16,4,2048]{2,1,0:T(4,128)(2,1)S(1)}, bf16[16,4,2048]{2,1,0:T(4,128)(2,1)S(1)}, u32[]{:S(2)}, u32[]{:S(2)}) collective-permute-start(bf16[16,4,2048]{2,1,0:T(4,128)(2,1)S(1)} %get-tuple-element.23), channel_id=1, source_target_pairs={{0,1},{1,0},{2,3},{3,2},{4,5},{5,4},{6,7},{7,6},{8,9},{9,8},{10,11... | collective-permute-start | bytes 786440 | tf_op jit(solution)/shard_map/ppermute | solution.py:23
  37.2 25.0 %collective-permute-start.12 = (bf16[2048,512]{1,0:T(8,128)(2,1)S(1)}, bf16[2048,512]{1,0:T(8,128)(2,1)S(1)}, u32[]{:S(2)}, u32[]{:S(2)}) collective-permute-start(bf16[2048,512]{1,0:T(8,128)(2,1)S(1)} %bitcast.18), channel_id=1, source_target_pairs={{0,1},{1,0},{2,3},{3,2},{4,5},{5,4},{6,7},{7,6},{8,9},{9,8},{10,11... | collective-permute-start | bytes 6291464 | tf_op jit(solution)/shard_map/ppermute | solution.py:23
  37.5 24.7 %collective-permute-start.13 = (bf16[256,2048]{1,0:T(8,128)(2,1)S(1)}, bf16[256,2048]{1,0:T(8,128)(2,1)S(1)}, u32[]{:S(2)}, u32[]{:S(2)}) collective-permute-start(bf16[256,2048]{1,0:T(8,128)(2,1)S(1)} %bitcast.20), channel_id=1, source_target_pairs={{0,1},{1,0},{2,3},{3,2},{4,5},{5,4},{6,7},{7,6},{8,9},{9,8},{10,11... | collective-permute-start | bytes 3145736 | tf_op jit(solution)/shard_map/ppermute | solution.py:23
  62.2 5.8 %copy-start = (f32[32,1,128,128]{3,2,1,0:T(8,128)S(1)}, f32[32,1,128,128]{3,2,1,0:T(8,128)}, u32[]{:S(2)}) copy-start(f32[32,1,128,128]{3,2,1,0:T(8,128)} %param.22) | copy-start | bytes 6291460
  64.3 12.1 %all-to-all-start.3 = ((bf16[16,4,2048]{2,1,0:T(4,128)(2,1)}), bf16[16,4,2048]{2,1,0:T(4,128)(2,1)S(1)}, u32[]{:S(2)}, u32[]{:S(2)}) async-start(bf16[16,4,2048]{2,1,0:T(4,128)(2,1)} %shard_map.179), calls=%async_computation.3 | async-start | bytes 524288 | tf_op jit(solution)/shard_map/all_to_all | solution.py:34
  (2 other events, 10.9 us)

commit v6 on v5

--- a/solution.py
+++ b/solution.py
@@ -107,9 +107,7 @@
         parcel[k // CAP, k % CAP] = loaded[k].astype(BF16)
 
 
-def place_moved(mig_s, filled, dest, begin, moved):
-    rows = begin.shape[0]
-    groups = moved.shape[0]
+def plan_moved(mig_s, filled, dest, rows, groups):
     group = lax.axis_index("dp")
     for g in range(groups):
         filled[g] = 0
@@ -118,6 +116,10 @@
         slot = filled[g]
         dest[CAP * g + jnp.minimum(slot, CAP - 1)] = r
         filled[g] = slot + 1
+
+def place_moved(filled, dest, begin, moved):
+    group = lax.axis_index("dp")
+    groups = moved.shape[0]
     for g in range(groups):
         for slot in range(CAP):
 
@@ -151,6 +153,8 @@
     live = extra[:, EXTRA - 1 :]
     second = jnp.dot(x, w_other_v[...], preferred_element_type=F32)
     first = jnp.dot(x, w_own_v[...], preferred_element_type=F32)
+    copies[3].wait()
+    plan_moved(mig_s, filled, dest, rows, moved.shape[0])
     copies[0].wait()
     vz = jnp.dot(x, w_vz_v[...], preferred_element_type=F32)
     for copy in copies[1:3]:
@@ -180,9 +184,9 @@
     for s in range(rows):
         kq[8 * s : 8 * s + 4] = k[4 * s : 4 * s + 4]
         kq[8 * s + 4 : 8 * s + 8] = q[4 * s : 4 * s + 4]
-    for copy in copies[3:]:
+    for copy in copies[4:]:
         copy.wait()
-    place_moved(mig_s, filled, dest, begin, moved)
+    place_moved(filled, dest, begin, moved)
     for s in range(rows):
         r = me ^ (2 * (s % (rows // 2)) + s // (rows // 2))
         both = jnp.dot(
@@ -236,7 +240,8 @@
     )
     for copy in copies:
         copy.wait()
-    place_moved(mig_s, filled, dest, out, moved)
+    plan_moved(mig_s, filled, dest, rows, moved.shape[0])
+    place_moved(filled, dest, out, moved)
     me = lax.axis_index("expert")
     for s in range(rows):
         r = me ^ (2 * (s % (rows // 2)) + s // (rows // 2))

time: 77.8 us -> 77.7 us (level)
  no operation moved by 1% of the time
where the time goes in v6:
time: 77.7 us; the launch traced here: 77 us
  blocking collectives  24.1 us (31%)
  starting transfers between devices  22.5 us (29%)
  waiting for transfers between devices  15.4 us (20%)
  Pallas kernels  12.5 us (16%)
  between operations  2.17 us (3%)
    all_to_all x2, blocking collectives, exchange(): lax.all_to_all(chunks, 'expert', split_axis=0, concat_axis=0, tiled=True,...  24.1 us
    ppermute x6, starting transfers between devices, hop(): return lax.ppermute(value, 'expert', [(i, i ^ mask) for i in range(n)])  8.88 us
    all_to_all x1, starting transfers between devices, body(): recv = lax.all_to_all(parcel, 'dp', split_axis=0, concat_axis=0, tiled=True)  8.58 us
    ppermute x6, waiting for transfers between devices, hop(): return lax.ppermute(value, 'expert', [(i, i ^ mask) for i in range(n)])  7.23 us
    all_to_all x1, waiting for transfers between devices, exchange(): lax.all_to_all(chunks, 'expert', split_axis=0, concat_axis=0, tiled=True,...  5.49 us
    all_to_all x1, starting transfers between devices, exchange(): lax.all_to_all(chunks, 'expert', split_axis=0, concat_axis=0, tiled=True,...  3.67 us
    pallas_call x1, Pallas kernels, body(): call(heads_kernel, (sds((peers, STEPS, width), BF16), sds((peers, STEPS,...  3.35 us
    pallas_call x1, Pallas kernels, body(): call(start_kernel, (vm((STEPS, width + EXTRA), BF16), vm((groups, CAP, di...  3.12 us
  transfers between devices with their start and end apart: 16, of which 6 were waited for; matrix products, arithmetic and copies ran while one was open for 0% of the time, Pallas kernels for 4%

profile of v6, /device:TPU:32, one launch (start us, length us, event | category | flops | bytes accessed | tf_op | source)
XLA Modules:
  0.0 77.0 jit_solution(9759014366034559879)
XLA Ops:
  0.7 3.1 %shard_map.176 = (bf16[4,2176]{1,0:T(4,128)(2,1)S(1)}, bf16[8,2,128,128]{3,2,1,0:T(8,128)(2,1)}) custom-call(bf16[4,2048]{1,0:T(4,128)(2,1)} %bitcast.22, f32[1,2048]{1,0:T(1,128)} %bitcast.30, s32[4,10]{1,0:T(4,128)} %bitcast.31, bf16[4,10]{1,0:T(4,128)(2,1)} %bitcast.32, s32[4,32]{1,0:T(4,128)} %mask.1, s32[2,128]{1,0:T(2,128)} %bitcast.24, ...), custom_call_target="tpu_custom_call" | custom-call | tf_op jit(solution)/shard_map/pallas_call | solution.py:314
  3.8 8.6 %all-to-all-start = ((bf16[8,2,128,128]{3,2,1,0:T(8,128)(2,1)}), bf16[8,2,128,128]{3,2,1,0:T(8,128)(2,1)S(1)}, u32[]{:S(2)}, u32[]{:S(2)}) async-start(bf16[8,2,128,128]{3,2,1,0:T(8,128)(2,1)} %get-tuple-element.20), calls=%async_computation | async-start | bytes 1048576 | tf_op jit(solution)/shard_map/all_to_all | solution.py:330
  12.4 3.0 %collective-permute-start.2 = (bf16[4,2176]{1,0:T(4,128)(2,1)S(1)}, bf16[4,2176]{1,0:T(4,128)(2,1)S(1)}, u32[]{:S(2)}, u32[]{:S(2)}) collective-permute-start(bf16[4,2176]{1,0:T(4,128)(2,1)S(1)} %get-tuple-element.18), channel_id=1, source_target_pairs={{0,6},{1,7},{2,4},{3,5},{4,2},{5,3},{6,0},{7,1},{8,14},{9,15},{10,... | collective-permute-start | bytes 52232 | tf_op jit(solution)/shard_map/ppermute | solution.py:28
  15.4 0.6 collective-permute-start.1
  16.1 0.5 collective-permute-start
  17.8 2.9 %collective-permute-done.1 = bf16[4,2176]{1,0:T(4,128)(2,1)S(1)} collective-permute-done((bf16[4,2176]{1,0:T(4,128)(2,1)S(1)}, bf16[4,2176]{1,0:T(4,128)(2,1)S(1)}, u32[]{:S(2)}, u32[]{:S(2)}) %collective-permute-start.1) | collective-permute-done | bytes 17440 | tf_op jit(solution)/shard_map/ppermute | solution.py:28
  20.7 1.6 %collective-permute-start.3 = (bf16[16,2176]{1,0:T(8,128)(2,1)S(1)}, bf16[16,2176]{1,0:T(8,128)(2,1)S(1)}, u32[]{:S(2)}, u32[]{:S(2)}) collective-permute-start(bf16[16,2176]{1,0:T(8,128)(2,1)S(1)} %pad_maximum_fusion.p0), channel_id=1, source_target_pairs={{0,8},{1,9},{2,10},{3,11},{4,12},{5,13},{6,14},{7,15},{8,0},{9,1},... | collective-permute-start | bytes 208904 | tf_op jit(solution)/shard_map/ppermute | solution.py:28
  22.3 2.7 %collective-permute-start.4 = (bf16[16,2176]{1,0:T(8,128)(2,1)S(1)}, bf16[16,2176]{1,0:T(8,128)(2,1)S(1)}, u32[]{:S(2)}, u32[]{:S(2)}) collective-permute-start(bf16[16,2176]{1,0:T(8,128)(2,1)S(1)} %pad_maximum_fusion.p0), channel_id=1, source_target_pairs={{0,16},{1,17},{2,18},{3,19},{4,20},{5,21},{6,22},{7,23},{8,24},{9,... | collective-permute-start | bytes 208904 | tf_op jit(solution)/shard_map/ppermute | solution.py:28
  25.0 0.5 collective-permute-start.5
  25.7 0.5 collective-permute-start.7
  26.2 1.9 %collective-permute-done.4.p2 = bf16[16,2176]{1,0:T(8,128)(2,1)S(1)} collective-permute-done((bf16[16,2176]{1,0:T(8,128)(2,1)S(1)}, bf16[16,2176]{1,0:T(8,128)(2,1)S(1)}, u32[]{:S(2)}, u32[]{:S(2)}) %collective-permute-start.4) | collective-permute-done | bytes 69664 | tf_op jit(solution)/shard_map/ppermute | solution.py:28
  28.1 2.4 %collective-permute-done.5.p3 = bf16[16,2176]{1,0:T(8,128)(2,1)S(1)} collective-permute-done((bf16[16,2176]{1,0:T(8,128)(2,1)S(1)}, bf16[16,2176]{1,0:T(8,128)(2,1)S(1)}, u32[]{:S(2)}, u32[]{:S(2)}) %collective-permute-start.5) | collective-permute-done | bytes 69664 | tf_op jit(solution)/shard_map/ppermute | solution.py:28
  30.6 1.2 %collective-permute-done.9.p7 = bf16[16,2176]{1,0:T(8,128)(2,1)S(1)} collective-permute-done((bf16[16,2176]{1,0:T(8,128)(2,1)S(1)}, bf16[16,2176]{1,0:T(8,128)(2,1)S(1)}, u32[]{:S(2)}, u32[]{:S(2)}) %collective-permute-start.9) | collective-permute-done | bytes 69664 | tf_op jit(solution)/shard_map/ppermute | solution.py:23
  31.9 3.3 %shard_map.177 = (bf16[16,4,2048]{2,1,0:T(4,128)(2,1)S(1)}, bf16[16,4,2048]{2,1,0:T(4,128)(2,1)S(1)}, f32[128,128]{1,0:T(8,128)S(1)}, f32[128,128]{1,0:T(8,128)S...) custom-call(bf16[16,2176]{1,0:T(8,128)(2,1)S(1)} %pad_maximum_fusion.p0, ...), custom_call_target="tpu_custom_call" | custom-call | flops 367001600 | bytes 6291456 | tf_op jit(solution)/shard_map/pallas_call | solution.py:339
  35.3 0.2 collective-permute-start.11
  35.5 1.4 %collective-permute-done.11 = bf16[16,4,2048]{2,1,0:T(4,128)(2,1)S(1)} collective-permute-done((bf16[16,4,2048]{2,1,0:T(4,128)(2,1)S(1)}, bf16[16,4,2048]{2,1,0:T(4,128)(2,1)S(1)}, u32[]{:S(2)}, u32[]{:S(2)}) %collective-permute-start.11) | collective-permute-done | bytes 262176 | tf_op jit(solution)/shard_map/ppermute | solution.py:23
  37.3 0.4 collective-permute-start.13
  37.7 12.2 %all_to_all.20.got = bf16[16,4,2048]{2,1,0:T(4,128)(2,1)S(1)} all-to-all(bf16[16,4,2048]{2,1,0:T(4,128)(2,1)S(1)} %add_convert_fusion), channel_id=1, replica_groups={{0,2,4,6,8,10,12,14,16,18,20,22,24,26,28,30},{1,3,5,7,9,11,13,15,17,19,..., dimensions={0} | all-to-all | bytes 524288 | tf_op jit(solution)/shard_map/all_to_all | solution.py:34
  50.1 11.9 %all_to_all.21.rows_in = bf16[16,4,2048]{2,1,0:T(4,128)(2,1)S(1)} all-to-all(bf16[16,4,2048]{2,1,0:T(4,128)(2,1)S(1)} %get-tuple-element.25), channel_id=1, replica_groups={{0,2,4,6,8,10,12,14,16,18,20,22,24,26,28,30},{1,3,5,7,9,11,13,15,17,19,..., dimensions={0} | all-to-all | bytes 524288 | tf_op jit(solution)/shard_map/all_to_all | solution.py:34
  62.0 2.1 %shard_map.179 = bf16[16,4,2048]{2,1,0:T(4,128)(2,1)} custom-call(bf16[16,4,2048]{2,1,0:T(4,128)(2,1)S(1)} %all_to_all.21.rows_in, f32[16,8,128]{2,1,0:T(8,128)S(1)} %get-tuple-element.26.extra_v, bf16[2048,512]{1,0:T(8,128)(2,1)S(1)} %bitcast.19, bf16[2048,512]{1,0:T(8,128)(2,1)S(1)} %collective-permute-done.12.up_other_v, bf16[256,2048]{1,0:T(8,128)(2,1)S(1)} %bitcast.21, ...), custom_call_target="tpu_custom_call" | custom-call | flops 536870912 | bytes 7340032 | tf_op jit(solution)/shard_map/pallas_call | solution.py:389
  64.1 3.7 %all-to-all-start.3 = ((bf16[16,4,2048]{2,1,0:T(4,128)(2,1)}), bf16[16,4,2048]{2,1,0:T(4,128)(2,1)S(1)}, u32[]{:S(2)}, u32[]{:S(2)}) async-start(bf16[16,4,2048]{2,1,0:T(4,128)(2,1)} %shard_map.179), calls=%async_computation.3 | async-start | bytes 524288 | tf_op jit(solution)/shard_map/all_to_all | solution.py:34
  67.8 3.0 %shard_map.181 = f32[32,128,128]{2,1,0:T(8,128)} custom-call(f32[128,128]{1,0:T(8,128)S(1)} %get-tuple-element.30.k_in, f32[128,128]{1,0:T(8,128)S(1)} %get-tuple-element.31.w_rows, f32[32,128]{1,0:T(8,128)S(1)} %get-tuple-element.32.decay, s32[256]{0:T(256)S(1)} %copy-done.6, f32[32,128,128]{2,1,0:T(8,128)S(1)} %bitcast.17, ...), custom_call_target="tpu_custom_call" | custom-call | flops 4194304 | bytes 5242880 | tf_op jit(solution)/shard_map/pallas_call | solution.py:372
  70.8 5.5 %all-to-all-done.3.got = bf16[16,4,2048]{2,1,0:T(4,128)(2,1)S(1)} async-done(((bf16[16,4,2048]{2,1,0:T(4,128)(2,1)}), bf16[16,4,2048]{2,1,0:T(4,128)(2,1)S(1)}, u32[]{:S(2)}, u32[]{:S(2)}) %all-to-all-start.3) | async-done | bytes 262176 | tf_op jit(solution)/shard_map/all_to_all | solution.py:34
  76.3 0.7 shard_map.180
  (40 shorter events, 0.9 us)
Async XLA Ops:
  0.6 31.2 %copy-start.5 = (bf16[4,1,2048]{2,0,1:T(4,128)(2,1)S(1)}, bf16[4,1,2048]{2,0,1:T(4,128)(2,1)}, u32[]{:S(2)}) copy-start(bf16[4,1,2048]{2,0,1:T(4,128)(2,1)} %param.17) | copy-start | bytes 49156
  0.6 31.2 %copy-start.6 = (s32[256]{0:T(256)S(1)}, s32[256]{0:T(256)}, u32[]{:S(2)}) copy-start(s32[256]{0:T(256)} %mig.3) | copy-start | bytes 3076
  0.7 15.9 %copy-start.3 = (bf16[2048,128]{1,0:T(8,128)(2,1)S(1)}, bf16[2048,128]{1,0:T(8,128)(2,1)}, u32[]{:S(2)}) copy-start(bf16[2048,128]{1,0:T(8,128)(2,1)} %w_own_v.1) | copy-start | bytes 1572868
  0.7 31.2 %copy-start.7 = (bf16[2048,2]{0,1:T(2,128)(2,1)S(1)}, bf16[2048,2]{0,1:T(2,128)(2,1)}, u32[]{:S(2)}) copy-start(bf16[2048,2]{0,1:T(2,128)(2,1)} %param.26) | copy-start | bytes 24580
  0.7 31.2 %copy-start.9 = (f32[128]{0:T(128)S(1)}, f32[128]{0:T(128)}, u32[]{:S(2)}) copy-start(f32[128]{0:T(128)} %param.29) | copy-start | bytes 1540
  0.7 31.2 %copy-start.4 = (bf16[128,2048]{1,0:T(8,128)(2,1)S(1)}, bf16[128,2048]{1,0:T(8,128)(2,1)}, u32[]{:S(2)}) copy-start(bf16[128,2048]{1,0:T(8,128)(2,1)} %w_out.1) | copy-start | bytes 1572868
  0.7 31.2 %copy-start.8 = (f32[2048]{0:T(1024)S(1)}, f32[2048]{0:T(1024)}, u32[]{:S(2)}) copy-start(f32[2048]{0:T(1024)} %param.31) | copy-start | bytes 24580
  3.8 28.0 %all-to-all-start = ((bf16[8,2,128,128]{3,2,1,0:T(8,128)(2,1)}), bf16[8,2,128,128]{3,2,1,0:T(8,128)(2,1)S(1)}, u32[]{:S(2)}, u32[]{:S(2)}) async-start(bf16[8,2,128,128]{3,2,1,0:T(8,128)(2,1)} %get-tuple-element.20), calls=%async_computation | async-start | bytes 1048576 | tf_op jit(solution)/shard_map/all_to_all | solution.py:330
  12.4 5.4 %collective-permute-start.2 = (bf16[4,2176]{1,0:T(4,128)(2,1)S(1)}, bf16[4,2176]{1,0:T(4,128)(2,1)S(1)}, u32[]{:S(2)}, u32[]{:S(2)}) collective-permute-start(bf16[4,2176]{1,0:T(4,128)(2,1)S(1)} %get-tuple-element.18), channel_id=1, source_target_pairs={{0,6},{1,7},{2,4},{3,5},{4,2},{5,3},{6,0},{7,1},{8,14},{9,15},{10,... | collective-permute-start | bytes 52232 | tf_op jit(solution)/shard_map/ppermute | solution.py:28
  15.4 5.3 %collective-permute-start.1 = (bf16[4,2176]{1,0:T(4,128)(2,1)S(1)}, bf16[4,2176]{1,0:T(4,128)(2,1)S(1)}, u32[]{:S(2)}, u32[]{:S(2)}) collective-permute-start(bf16[4,2176]{1,0:T(4,128)(2,1)S(1)} %get-tuple-element.18), channel_id=1, source_target_pairs={{0,4},{1,5},{2,6},{3,7},{4,0},{5,1},{6,2},{7,3},{8,12},{9,13},{10,... | collective-permute-start | bytes 52232 | tf_op jit(solution)/shard_map/ppermute | solution.py:28
  16.1 4.6 %collective-permute-start = (bf16[4,2176]{1,0:T(4,128)(2,1)S(1)}, bf16[4,2176]{1,0:T(4,128)(2,1)S(1)}, u32[]{:S(2)}, u32[]{:S(2)}) collective-permute-start(bf16[4,2176]{1,0:T(4,128)(2,1)S(1)} %get-tuple-element.18), channel_id=1, source_target_pairs={{0,2},{1,3},{2,0},{3,1},{4,6},{5,7},{6,4},{7,5},{8,10},{9,11},{10,... | collective-permute-start | bytes 52232 | tf_op jit(solution)/shard_map/ppermute | solution.py:28
  16.5 15.3 %collective-permute-start.10 = (bf16[2048,128]{1,0:T(8,128)(2,1)S(1)}, bf16[2048,128]{1,0:T(8,128)(2,1)S(1)}, u32[]{:S(2)}, u32[]{:S(2)}) collective-permute-start(bf16[2048,128]{1,0:T(8,128)(2,1)S(1)} %copy-done.3), channel_id=1, source_target_pairs={{0,1},{1,0},{2,3},{3,2},{4,5},{5,4},{6,7},{7,6},{8,9},{9,8},{10,11... | collective-permute-start | bytes 1572872 | tf_op jit(solution)/shard_map/ppermute | solution.py:23
  20.7 4.9 %collective-permute-start.3 = (bf16[16,2176]{1,0:T(8,128)(2,1)S(1)}, bf16[16,2176]{1,0:T(8,128)(2,1)S(1)}, u32[]{:S(2)}, u32[]{:S(2)}) collective-permute-start(bf16[16,2176]{1,0:T(8,128)(2,1)S(1)} %pad_maximum_fusion.p0), channel_id=1, source_target_pairs={{0,8},{1,9},{2,10},{3,11},{4,12},{5,13},{6,14},{7,15},{8,0},{9,1},... | collective-permute-start | bytes 208904 | tf_op jit(solution)/shard_map/ppermute | solution.py:28
  22.3 5.8 %collective-permute-start.4 = (bf16[16,2176]{1,0:T(8,128)(2,1)S(1)}, bf16[16,2176]{1,0:T(8,128)(2,1)S(1)}, u32[]{:S(2)}, u32[]{:S(2)}) collective-permute-start(bf16[16,2176]{1,0:T(8,128)(2,1)S(1)} %pad_maximum_fusion.p0), channel_id=1, source_target_pairs={{0,16},{1,17},{2,18},{3,19},{4,20},{5,21},{6,22},{7,23},{8,24},{9,... | collective-permute-start | bytes 208904 | tf_op jit(solution)/shard_map/ppermute | solution.py:28
  25.0 5.5 %collective-permute-start.5 = (bf16[16,2176]{1,0:T(8,128)(2,1)S(1)}, bf16[16,2176]{1,0:T(8,128)(2,1)S(1)}, u32[]{:S(2)}, u32[]{:S(2)}) collective-permute-start(bf16[16,2176]{1,0:T(8,128)(2,1)S(1)} %pad_maximum_fusion.p0), channel_id=1, source_target_pairs={{0,24},{1,25},{2,26},{3,27},{4,28},{5,29},{6,30},{7,31},{8,16},{9,... | collective-permute-start | bytes 208904 | tf_op jit(solution)/shard_map/ppermute | solution.py:28
  25.6 5.0 %collective-permute-start.6 = (bf16[16,2176]{1,0:T(8,128)(2,1)S(1)}, bf16[16,2176]{1,0:T(8,128)(2,1)S(1)}, u32[]{:S(2)}, u32[]{:S(2)}) collective-permute-start(bf16[16,2176]{1,0:T(8,128)(2,1)S(1)} %pad_maximum_fusion.p0), channel_id=1, source_target_pairs={{0,1},{1,0},{2,3},{3,2},{4,5},{5,4},{6,7},{7,6},{8,9},{9,8},{10,11... | collective-permute-start | bytes 208904 | tf_op jit(solution)/shard_map/ppermute | solution.py:23
  25.7 4.9 %collective-permute-start.7 = (bf16[16,2176]{1,0:T(8,128)(2,1)S(1)}, bf16[16,2176]{1,0:T(8,128)(2,1)S(1)}, u32[]{:S(2)}, u32[]{:S(2)}) collective-permute-start(bf16[16,2176]{1,0:T(8,128)(2,1)S(1)} %collective-permute-done.3.p1), channel_id=1, source_target_pairs={{0,1},{1,0},{2,3},{3,2},{4,5},{5,4},{6,7},{7,6},{8,9},{9,8},{10,11... | collective-permute-start | bytes 208904 | tf_op jit(solution)/shard_map/ppermute | solution.py:23
  28.1 2.5 %collective-permute-start.8 = (bf16[16,2176]{1,0:T(8,128)(2,1)S(1)}, bf16[16,2176]{1,0:T(8,128)(2,1)S(1)}, u32[]{:S(2)}, u32[]{:S(2)}) collective-permute-start(bf16[16,2176]{1,0:T(8,128)(2,1)S(1)} %collective-permute-done.4.p2), channel_id=1, source_target_pairs={{0,1},{1,0},{2,3},{3,2},{4,5},{5,4},{6,7},{7,6},{8,9},{9,8},{10,11... | collective-permute-start | bytes 208904 | tf_op jit(solution)/shard_map/ppermute | solution.py:23
  30.6 1.3 %collective-permute-start.9 = (bf16[16,2176]{1,0:T(8,128)(2,1)S(1)}, bf16[16,2176]{1,0:T(8,128)(2,1)S(1)}, u32[]{:S(2)}, u32[]{:S(2)}) collective-permute-start(bf16[16,2176]{1,0:T(8,128)(2,1)S(1)} %collective-permute-done.5.p3), channel_id=1, source_target_pairs={{0,1},{1,0},{2,3},{3,2},{4,5},{5,4},{6,7},{7,6},{8,9},{9,8},{10,11... | collective-permute-start | bytes 208904 | tf_op jit(solution)/shard_map/ppermute | solution.py:23
  35.3 1.6 %collective-permute-start.11 = (bf16[16,4,2048]{2,1,0:T(4,128)(2,1)S(1)}, bf16[16,4,2048]{2,1,0:T(4,128)(2,1)S(1)}, u32[]{:S(2)}, u32[]{:S(2)}) collective-permute-start(bf16[16,4,2048]{2,1,0:T(4,128)(2,1)S(1)} %get-tuple-element.23), channel_id=1, source_target_pairs={{0,1},{1,0},{2,3},{3,2},{4,5},{5,4},{6,7},{7,6},{8,9},{9,8},{10,11... | collective-permute-start | bytes 786440 | tf_op jit(solution)/shard_map/ppermute | solution.py:23
  37.1 25.0 %collective-permute-start.12 = (bf16[2048,512]{1,0:T(8,128)(2,1)S(1)}, bf16[2048,512]{1,0:T(8,128)(2,1)S(1)}, u32[]{:S(2)}, u32[]{:S(2)}) collective-permute-start(bf16[2048,512]{1,0:T(8,128)(2,1)S(1)} %bitcast.18), channel_id=1, source_target_pairs={{0,1},{1,0},{2,3},{3,2},{4,5},{5,4},{6,7},{7,6},{8,9},{9,8},{10,11... | collective-permute-start | bytes 6291464 | tf_op jit(solution)/shard_map/ppermute | solution.py:23
  37.3 24.7 %collective-permute-start.13 = (bf16[256,2048]{1,0:T(8,128)(2,1)S(1)}, bf16[256,2048]{1,0:T(8,128)(2,1)S(1)}, u32[]{:S(2)}, u32[]{:S(2)}) collective-permute-start(bf16[256,2048]{1,0:T(8,128)(2,1)S(1)} %bitcast.20), channel_id=1, source_target_pairs={{0,1},{1,0},{2,3},{3,2},{4,5},{5,4},{6,7},{7,6},{8,9},{9,8},{10,11... | collective-permute-start | bytes 3145736 | tf_op jit(solution)/shard_map/ppermute | solution.py:23
  62.0 5.8 %copy-start = (f32[32,1,128,128]{3,2,1,0:T(8,128)S(1)}, f32[32,1,128,128]{3,2,1,0:T(8,128)}, u32[]{:S(2)}) copy-start(f32[32,1,128,128]{3,2,1,0:T(8,128)} %param.22) | copy-start | bytes 6291460
  64.1 12.1 %all-to-all-start.3 = ((bf16[16,4,2048]{2,1,0:T(4,128)(2,1)}), bf16[16,4,2048]{2,1,0:T(4,128)(2,1)S(1)}, u32[]{:S(2)}, u32[]{:S(2)}) async-start(bf16[16,4,2048]{2,1,0:T(4,128)(2,1)} %shard_map.179), calls=%async_computation.3 | async-start | bytes 524288 | tf_op jit(solution)/shard_map/all_to_all | solution.py:34
  (2 other events, 10.6 us)
